TPU v7x, 32 devices: a whole 2x2x4 slice. The times are simulated.
32 devices in a mesh: section: 8 (over y, x, core), uly: 4 (over z).
Axes of the slice: x: 2, y: 2, z: 4, core: 2. Of those that a mesh axis runs over, the one named last changes fastest.
Arguments:
- state: bfloat16 [8, 128, 3072], P('section', 'uly'), may hold values from -6 to 6
- patch_slot: int32 [8], replicated, may hold values from 0 to 3
- section_active: int32 [8], P('section'), may hold values from 1 to 2
- qkv_weight: bfloat16 [8, 3072, 3, 1536], P('section', None, None, 'uly'), may hold values from -0.109375 to 0.109375
- out_weight: bfloat16 [8, 1536, 3072], P('section', 'uly'), may hold values from -0.15625 to 0.15625
- norm_gain: bfloat16 [8, 3072], P('section'), may hold values from 0.099609375 to 1.8984375
- stale_keys: bfloat16 [8, 512, 1536], P('section', None, 'uly'), may hold values from -6 to 6
- stale_values: bfloat16 [8, 512, 1536], P('section', None, 'uly'), may hold values from -6 to 6
Outputs:
- final_state: bfloat16 [8, 128, 3072], P('section', 'uly')
All inputs are finite; a program needn't handle non-finite values.
Results may differ from a plain program's by a relative error of at most 0.019.
Values may be sent and summed in bfloat16 or wider, within the bound.
No kernel may reach another device: no remote copies, remote signals or barrier semaphores. Data moves between devices by JAX's collectives and lax.ppermute only.
A program may use at most 64 MiB of HBM per device.

v0:
```python
import jax
import jax.numpy as jnp
from jax import lax
from jax.sharding import PartitionSpec as P

HD = 128
TICKS = 3


def passed_along(block, axis, distance):
    devices = range(lax.axis_size(axis))
    route = [((i - distance) % len(devices), i) for i in devices]
    return lax.ppermute(block, axis, route)


def normalize(current, gain_row):
    widened = current.astype(jnp.float32)
    mean_square = jnp.mean(widened * widened, axis=-1, keepdims=True)
    return (widened * lax.rsqrt(mean_square + 1e-06) * gain_row).astype(jnp.bfloat16)


def attend(projected, key_cache, value_cache, patch_index):
    row_count = projected.shape[0]
    width = projected.shape[2]
    head_count = width // HD
    seq_rows = key_cache.shape[0]
    row_start = patch_index * row_count
    zero_index = jnp.zeros((), jnp.int32)
    key_cache = lax.dynamic_update_slice(key_cache, projected[:, 1], (row_start, zero_index))
    value_cache = lax.dynamic_update_slice(value_cache, projected[:, 2], (row_start, zero_index))
    query_heads = projected[:, 0].reshape(row_count, head_count, HD)
    key_heads = key_cache.reshape(seq_rows, head_count, HD)
    value_heads = value_cache.reshape(seq_rows, head_count, HD)
    scores = jnp.einsum(
        "thd,shd->hts", query_heads, key_heads, preferred_element_type=jnp.float32
    ) * HD ** (-0.5)
    probs = jax.nn.softmax(scores, axis=-1).astype(jnp.bfloat16)
    attended = jnp.einsum("hts,shd->thd", probs, value_heads, preferred_element_type=jnp.float32)
    return (attended.astype(jnp.bfloat16).reshape(row_count, width), key_cache, value_cache)


def shards(
    state, patch_slot, section_active, qkv_weight, out_weight, norm_gain, stale_keys, stale_values
):
    section_count = lax.axis_size("section")
    section_index = lax.axis_index("section")
    uly_index = lax.axis_index("uly")
    width = qkv_weight.shape[3]
    model_width = qkv_weight.shape[1]
    w_qkv = qkv_weight[0].reshape(model_width, 3 * width)
    w_out = out_weight[0]
    gain_row = norm_gain[0].astype(jnp.float32)
    block_count = section_active[0]
    key_cache = stale_keys[0]
    value_cache = stale_values[0]
    local_rows = state.shape[1]
    current = lax.all_gather(state[0], "uly", axis=0, tiled=True)
    for tick_index in range(TICKS):
        patch_index = patch_slot[(section_index - tick_index) % section_count]
        for pass_index in range(2):
            normed = normalize(current, gain_row)
            projected = jnp.dot(normed, w_qkv, preferred_element_type=jnp.float32).astype(
                jnp.bfloat16
            )
            projected = projected.reshape(current.shape[0], 3, width)
            attended, new_keys, new_values = attend(projected, key_cache, value_cache, patch_index)
            head_term = jnp.dot(attended, w_out, preferred_element_type=jnp.float32)
            head_total = lax.psum(head_term.astype(jnp.bfloat16), "uly").astype(jnp.float32)
            updated = (current.astype(jnp.float32) + head_total).astype(jnp.bfloat16)
            applies = block_count > pass_index
            current = jnp.where(applies, updated, current)
            key_cache = jnp.where(applies, new_keys, key_cache)
            value_cache = jnp.where(applies, new_values, value_cache)
        current = passed_along(current, "section", 1)
    return lax.dynamic_slice_in_dim(current, uly_index * local_rows, local_rows, 0)[None]


def solution(mesh):
    return jax.shard_map(
        shards,
        mesh=mesh,
        in_specs=(
            P("section", "uly", None),
            P(),
            P("section"),
            P("section", None, None, "uly"),
            P("section", "uly", None),
            P("section", None),
            P("section", None, "uly"),
            P("section", None, "uly"),
        ),
        out_specs=P("section", "uly", None),
        check_vma=False,
    )
```

profile of v0, /device:TPU:14, one launch (start us, length us, event | category | flops | bytes accessed | tf_op | source)
XLA Modules:
  0.0 469.0 jit_solution(768797472624579355)
XLA Ops:
  13.5 18.1 %all-gather = bf16[1,128,3072]{2,1,0:T(8,128)(2,1)S(1)} all-gather(bf16[1,32,3072]{2,1,0:T(8,128)(2,1)} %param.8), channel_id=2, replica_groups=mesh['section'=8,'uly'=4] {'uly'}, dimensions={1}, use_global_device_ids=true | all-gather | bytes 983040 | tf_op jit(solution)/shard_map/all_gather | solution.py:57
  31.8 10.3 %copy.34 = bf16[1,3072,3,384]{1,3,2,0:T(8,128)(2,1)} copy(bf16[1,3072,3,384]{3,1,2,0:T(8,128)(2,1)} %param.11) | data formatting | bytes 14155776 | tf_op args[3]
  42.1 6.1 %convolution_convert_fusion.11 = bf16[128,1152]{1,0:T(8,128)(2,1)} fusion(bf16[3072,1152]{0,1:T(8,128)(2,1)} %bitcast.172, bf16[1,128,3072]{2,1,0:T(8,128)(2,1)S(1)} %all-gather, f32[3072]{0:T(1024)S(1)} %bitcast.209, f32[128]{0:T(128)S(1)} %add_rsqrt_fusion.5), kind=kOutput, calls=%fused_computation.17 | convolution fusion | flops 907689984 | bytes 8172032 | tf_op jit(solution)/shard_map/dot_general | solution.py:62
  54.8 2.2 convolution_multiply_fusion.5
  57.0 3.0 convolution_convert_fusion.17
  60.0 2.4 convolution_convert_fusion.5
  66.2 41.0 %all-reduce.7.cloned.1.call-done = bf16[128,3072]{1,0:T(8,128)(2,1)} async-done(((bf16[128,3072]{1,0:T(8,128)(2,1)}), bf16[128,3072]{1,0:T(8,128)(2,1)}) %all-reduce.7.cloned.1.call-update) | async-done | bytes 786448 | tf_op jit(solution)/shard_map/psum | solution.py:68
  109.6 5.4 %convolution_convert_fusion.10 = bf16[128,1152]{1,0:T(8,128)(2,1)S(1)} fusion(bf16[3072,1152]{0,1:T(8,128)(2,1)} %bitcast.173, bf16[128,3072]{1,0:T(8,128)(2,1)S(1)} %get-tuple-element.10, f32[128]{0:T(128)S(1)} %add_rsqrt_fusion.4, f32[3072]{0:T(1024)S(1)} %bitcast.210), kind=kOutput, calls=%fused_computation.16 | convolution fusion | flops 907689984 | bytes 8172032 | tf_op jit(solution)/shard_map/dot_general | solution.py:62
  119.6 3.0 convolution_convert_fusion.16
  122.6 2.6 convolution_convert_fusion.4
  125.3 43.1 %all-reduce.9.cloned.1.call-done = bf16[128,3072]{1,0:T(8,128)(2,1)} async-done(((bf16[128,3072]{1,0:T(8,128)(2,1)}), bf16[128,3072]{1,0:T(8,128)(2,1)}) %all-reduce.9.cloned.1.call-update) | async-done | bytes 786448 | tf_op jit(solution)/shard_map/psum | solution.py:68
  168.4 2.2 fusion.52
  174.0 8.2 %collective-permute-done = bf16[128,3072]{1,0:T(8,128)(2,1)S(1)} collective-permute-done((bf16[128,3072]{1,0:T(8,128)(2,1)}, bf16[128,3072]{1,0:T(8,128)(2,1)S(1)}, u32[]{:S(2)}, u32[]{:S(2)}) %collective-permute-start) | collective-permute-done | bytes 786464 | tf_op jit(solution)/shard_map/ppermute | solution.py:13
  182.5 6.2 %convolution_convert_fusion.9 = bf16[128,1152]{1,0:T(8,128)(2,1)} fusion(bf16[3072,1152]{0,1:T(8,128)(2,1)} %bitcast.174, bf16[128,3072]{1,0:T(8,128)(2,1)S(1)} %collective-permute-done, f32[128]{0:T(128)S(1)} %add_rsqrt_fusion.3, f32[3072]{0:T(1024)S(1)} %bitcast.211), kind=kOutput, calls=%fused_computation.15 | convolution fusion | flops 907689984 | bytes 8172032 | tf_op jit(solution)/shard_map/dot_general | solution.py:62
  197.6 2.5 convolution_convert_fusion.3
  203.0 40.3 %all-reduce.11.cloned.1.call-done = bf16[128,3072]{1,0:T(8,128)(2,1)} async-done(((bf16[128,3072]{1,0:T(8,128)(2,1)}), bf16[128,3072]{1,0:T(8,128)(2,1)}) %all-reduce.11.cloned.1.call-update) | async-done | bytes 786448 | tf_op jit(solution)/shard_map/psum | solution.py:68
  243.3 2.1 fusion.24
  245.5 6.1 %convolution_convert_fusion.8 = bf16[128,1152]{1,0:T(8,128)(2,1)} fusion(bf16[3072,1152]{0,1:T(8,128)(2,1)} %bitcast.175, bf16[128,3072]{1,0:T(8,128)(2,1)S(1)} %get-tuple-element.8, f32[128]{0:T(128)S(1)} %add_rsqrt_fusion.2, f32[3072]{0:T(1024)S(1)} %bitcast.212), kind=kOutput, calls=%fused_computation.14 | convolution fusion | flops 907689984 | bytes 8172032 | tf_op jit(solution)/shard_map/dot_general | solution.py:62
  258.3 2.2 convolution_multiply_fusion.2
  260.5 2.9 convolution_convert_fusion.14
  263.4 2.4 convolution_convert_fusion.2
  265.9 43.1 %all-reduce.13.cloned.1.call-done = bf16[128,3072]{1,0:T(8,128)(2,1)} async-done(((bf16[128,3072]{1,0:T(8,128)(2,1)}), bf16[128,3072]{1,0:T(8,128)(2,1)}) %all-reduce.13.cloned.1.call-update) | async-done | bytes 786448 | tf_op jit(solution)/shard_map/psum | solution.py:68
  308.9 2.2 fusion.50
  314.7 8.1 %collective-permute-done.1 = bf16[128,3072]{1,0:T(8,128)(2,1)S(1)} collective-permute-done((bf16[128,3072]{1,0:T(8,128)(2,1)}, bf16[128,3072]{1,0:T(8,128)(2,1)S(1)}, u32[]{:S(2)}, u32[]{:S(2)}) %collective-permute-start.1) | collective-permute-done | bytes 786464 | tf_op jit(solution)/shard_map/ppermute | solution.py:13
  323.1 6.2 %convolution_convert_fusion.7 = bf16[128,1152]{1,0:T(8,128)(2,1)} fusion(bf16[3072,1152]{0,1:T(8,128)(2,1)} %bitcast.176, bf16[128,3072]{1,0:T(8,128)(2,1)S(1)} %collective-permute-done.1, f32[128]{0:T(128)S(1)} %add_rsqrt_fusion.1, f32[3072]{0:T(1024)S(1)} %bitcast.213), kind=kOutput, calls=%fused_computation.13 | convolution fusion | flops 907689984 | bytes 8172032 | tf_op jit(solution)/shard_map/dot_general | solution.py:62
  338.1 2.5 convolution_convert_fusion.1
  343.3 40.5 %all-reduce.15.cloned.1.call-done = bf16[128,3072]{1,0:T(8,128)(2,1)} async-done(((bf16[128,3072]{1,0:T(8,128)(2,1)}), bf16[128,3072]{1,0:T(8,128)(2,1)}) %all-reduce.15.cloned.1.call-update) | async-done | bytes 786448 | tf_op jit(solution)/shard_map/psum | solution.py:68
  385.9 6.2 %convolution_convert_fusion.6 = bf16[128,1152]{1,0:T(8,128)(2,1)} fusion(bf16[3072,1152]{0,1:T(8,128)(2,1)} %bitcast.177, bf16[128,3072]{1,0:T(8,128)(2,1)S(1)} %get-tuple-element.6, f32[128]{0:T(128)S(1)} %add_rsqrt_fusion, f32[3072]{0:T(1024)S(1)} %bitcast.214), kind=kOutput, calls=%fused_computation.12 | convolution fusion | flops 907689984 | bytes 8172032 | tf_op jit(solution)/shard_map/dot_general | solution.py:62
  400.5 2.4 convolution_convert_fusion.12
  404.4 43.1 %all-reduce.17.cloned.1.call-done = bf16[128,3072]{1,0:T(8,128)(2,1)} async-done(((bf16[128,3072]{1,0:T(8,128)(2,1)}), bf16[128,3072]{1,0:T(8,128)(2,1)}) %all-reduce.17.cloned.1.call-update) | async-done | bytes 786448 | tf_op jit(solution)/shard_map/psum | solution.py:68
  447.6 2.3 fusion.48
  449.8 11.6 %collective-permute-done.2 = bf16[128,3072]{1,0:T(8,128)(2,1)S(1)} collective-permute-done((bf16[128,3072]{1,0:T(8,128)(2,1)}, bf16[128,3072]{1,0:T(8,128)(2,1)S(1)}, u32[]{:S(2)}, u32[]{:S(2)}) %collective-permute-start.2) | collective-permute-done | bytes 786464 | tf_op jit(solution)/shard_map/ppermute | solution.py:13
  (146 shorter events, 71.9 us)
Async XLA Ops:
  6.5 53.5 %copy-start = (bf16[1,384,3072]{2,1,0:T(8,128)(2,1)S(1)}, bf16[1,384,3072]{2,1,0:T(8,128)(2,1)}, u32[]{:S(2)}) copy-start(bf16[1,384,3072]{2,1,0:T(8,128)(2,1)} %param.12) | copy-start | bytes 7077892
  6.5 100.6 %all-reduce.7.cloned.1.call-start = ((), (), s32[]{:S(2)}) async-start(), calls=%async_computation | async-start | bytes 1572864 | tf_op jit(solution)/shard_map/psum | solution.py:68
  62.5 105.9 %all-reduce.9.cloned.1.call-start = ((), (), s32[]{:S(2)}) async-start(), calls=%async_computation.1 | async-start | bytes 1572864 | tf_op jit(solution)/shard_map/psum | solution.py:68
  109.6 7.3 %copy-start.29 = (bf16[512,384]{0,1:T(8,128)(2,1)S(1)}, bf16[512,384]{0,1:T(8,128)(2,1)}, u32[]{:S(2)}) copy-start(bf16[512,384]{0,1:T(8,128)(2,1)} %copy.70) | copy-start | bytes 1179652
  117.8 4.8 %copy-start.26 = (bf16[512,384]{0,1:T(8,128)(2,1)}, bf16[512,384]{0,1:T(8,128)(2,1)S(1)}, u32[]{:S(2)}) copy-start(bf16[512,384]{0,1:T(8,128)(2,1)S(1)} %get-tuple-element.19) | copy-start | bytes 1179652
  117.8 4.8 %copy-start.30 = (bf16[512,384]{0,1:T(8,128)(2,1)}, bf16[512,384]{0,1:T(8,128)(2,1)S(1)}, u32[]{:S(2)}) copy-start(bf16[512,384]{0,1:T(8,128)(2,1)S(1)} %get-tuple-element.20) | copy-start | bytes 1179652
  122.6 45.7 %copy-start.2 = (bf16[128,3072]{1,0:T(8,128)(2,1)S(1)}, bf16[128,3072]{1,0:T(8,128)(2,1)}, u32[]{:S(2)}) copy-start(bf16[128,3072]{1,0:T(8,128)(2,1)} %copy-done.1) | copy-start | bytes 2359300
  125.2 118.1 %all-reduce.11.cloned.1.call-start = ((), (), s32[]{:S(2)}) async-start(), calls=%async_computation.2 | async-start | bytes 1572864 | tf_op jit(solution)/shard_map/psum | solution.py:68
  170.6 1.8 copy-start.7
  170.6 11.6 %collective-permute-start = (bf16[128,3072]{1,0:T(8,128)(2,1)}, bf16[128,3072]{1,0:T(8,128)(2,1)S(1)}, u32[]{:S(2)}, u32[]{:S(2)}) collective-permute-start(bf16[128,3072]{1,0:T(8,128)(2,1)} %fusion.52), channel_id=1, source_target_pairs={{28,0},{0,4},{4,8},{8,12},{12,16},{16,20},{20,24},{24,28},{29,1},{... | collective-permute-start | bytes 2359304 | tf_op jit(solution)/shard_map/ppermute | solution.py:13
  182.2 6.4 %copy-start.4 = (bf16[128,3072]{1,0:T(8,128)(2,1)}, bf16[128,3072]{1,0:T(8,128)(2,1)S(1)}, u32[]{:S(2)}) copy-start(bf16[128,3072]{1,0:T(8,128)(2,1)S(1)} %collective-permute-done) | copy-start | bytes 2359300
  182.5 8.9 %copy-start.22 = (bf16[512,384]{0,1:T(8,128)(2,1)S(1)}, bf16[512,384]{0,1:T(8,128)(2,1)}, u32[]{:S(2)}) copy-start(bf16[512,384]{0,1:T(8,128)(2,1)} %copy-done.18) | copy-start | bytes 1179652
  191.4 1.7 copy-start.32
  193.1 4.5 copy-start.20
  197.6 2.6 copy-start.19
  197.6 2.6 copy-start.21
  200.2 108.8 %all-reduce.13.cloned.1.call-start = ((), (), s32[]{:S(2)}) async-start(), calls=%async_computation.3 | async-start | bytes 1572864 | tf_op jit(solution)/shard_map/psum | solution.py:68
  200.3 45.1 %copy-start.9 = (bf16[512,384]{0,1:T(8,128)(2,1)}, bf16[512,384]{0,1:T(8,128)(2,1)S(1)}, u32[]{:S(2)}) copy-start(bf16[512,384]{0,1:T(8,128)(2,1)S(1)} %broadcast_select_fusion.7) | copy-start | bytes 1179652
  245.4 9.5 %copy-start.12 = (bf16[512,384]{0,1:T(8,128)(2,1)S(1)}, bf16[512,384]{0,1:T(8,128)(2,1)}, u32[]{:S(2)}) copy-start(bf16[512,384]{0,1:T(8,128)(2,1)} %copy-done.9) | copy-start | bytes 1179652
  256.6 6.8 %copy-start.11 = (bf16[512,384]{0,1:T(8,128)(2,1)}, bf16[512,384]{0,1:T(8,128)(2,1)S(1)}, u32[]{:S(2)}) copy-start(bf16[512,384]{0,1:T(8,128)(2,1)S(1)} %get-tuple-element.16) | copy-start | bytes 1179652
  265.8 46.1 %copy-start.10 = (bf16[512,384]{0,1:T(8,128)(2,1)S(1)}, bf16[512,384]{0,1:T(8,128)(2,1)}, u32[]{:S(2)}) copy-start(bf16[512,384]{0,1:T(8,128)(2,1)} %copy-done.9) | copy-start | bytes 1179652
  265.8 117.9 %all-reduce.15.cloned.1.call-start = ((), (), s32[]{:S(2)}) async-start(), calls=%async_computation.4 | async-start | bytes 1572864 | tf_op jit(solution)/shard_map/psum | solution.py:68
  311.2 11.6 %collective-permute-start.1 = (bf16[128,3072]{1,0:T(8,128)(2,1)}, bf16[128,3072]{1,0:T(8,128)(2,1)S(1)}, u32[]{:S(2)}, u32[]{:S(2)}) collective-permute-start(bf16[128,3072]{1,0:T(8,128)(2,1)} %fusion.50), channel_id=1, source_target_pairs={{28,0},{0,4},{4,8},{8,12},{12,16},{16,20},{20,24},{24,28},{29,1},{... | collective-permute-start | bytes 2359304 | tf_op jit(solution)/shard_map/ppermute | solution.py:13
  311.9 1.2 copy-start.28
  322.8 6.4 %copy-start.3 = (bf16[128,3072]{1,0:T(8,128)(2,1)}, bf16[128,3072]{1,0:T(8,128)(2,1)S(1)}, u32[]{:S(2)}) copy-start(bf16[128,3072]{1,0:T(8,128)(2,1)S(1)} %collective-permute-done.1) | copy-start | bytes 2359300
  323.1 8.9 %copy-start.17 = (bf16[512,384]{0,1:T(8,128)(2,1)S(1)}, bf16[512,384]{0,1:T(8,128)(2,1)}, u32[]{:S(2)}) copy-start(bf16[512,384]{0,1:T(8,128)(2,1)} %copy-done.15) | copy-start | bytes 1179652
  332.0 1.7 copy-start.33
  338.1 2.6 copy-start.25
  340.6 1.9 copy-start.16
  340.6 106.9 %all-reduce.17.cloned.1.call-start = ((), (), s32[]{:S(2)}) async-start(), calls=%async_computation.5 | async-start | bytes 1572864 | tf_op jit(solution)/shard_map/psum | solution.py:68
  385.9 9.5 %copy-start.31 = (bf16[512,384]{0,1:T(8,128)(2,1)S(1)}, bf16[512,384]{0,1:T(8,128)(2,1)}, u32[]{:S(2)}) copy-start(bf16[512,384]{0,1:T(8,128)(2,1)} %broadcast_select_fusion.4) | copy-start | bytes 1179652
  449.8 11.6 %collective-permute-start.2 = (bf16[128,3072]{1,0:T(8,128)(2,1)}, bf16[128,3072]{1,0:T(8,128)(2,1)S(1)}, u32[]{:S(2)}, u32[]{:S(2)}) collective-permute-start(bf16[128,3072]{1,0:T(8,128)(2,1)} %fusion.48), channel_id=1, source_target_pairs={{28,0},{0,4},{4,8},{8,12},{12,16},{16,20},{20,24},{24,28},{29,1},{... | collective-permute-start | bytes 2359304 | tf_op jit(solution)/shard_map/ppermute | solution.py:13
  (11 other events, 9.8 us)
Sparse Core Ops, SparseCore 0:
  62.6 44.4 all-reduce.6
  125.3 42.9 all-reduce.8
  200.3 42.9 all-reduce.10
  265.9 42.9 all-reduce.12
  340.7 42.9 all-reduce.14
  404.5 42.9 all-reduce.16
where the time goes:
time: 474 us; the launch traced here: 469 us
  waiting for transfers between devices  279 us (59%)
  matrix products  83.2 us (18%)
  local copies, waits for them, and re-layouts  50.4 us (11%)
  other arithmetic  21.4 us (5%)
  blocking collectives  18.1 us (4%)
  between operations  16.5 us (3%)
    psum x6, waiting for transfers between devices, shards(): lax.psum(head_term.astype(jnp.bfloat16), 'uly').astype(jnp.float32)  251 us
    dot_general x6, matrix products, shards(): jnp.dot(normed, w_qkv, preferred_element_type=jnp.float32)  36.2 us
    ppermute x3, waiting for transfers between devices, passed_along(): return lax.ppermute(block, axis, route)  27.9 us
    unnamed x78, local copies, waits for them, and re-layouts  21.5 us
    all_gather x1, blocking collectives, shards(): current = lax.all_gather(state[0], 'uly', axis=0, tiled=True)  18.1 us
    dot_general x6, matrix products, attend(): jnp.einsum('hts,shd->thd', probs, value_heads, preferred_element_type=jnp...  14.3 us
    dot_general x6, matrix products, shards(): head_term = jnp.dot(attended, w_out, preferred_element_type=jnp.float32)  14 us
    dot_general x6, matrix products, attend(): jnp.einsum('thd,shd->hts', query_heads, key_heads, preferred_element_type...  10.5 us
  transfers between devices with their start and end apart: 9, of which 9 were waited for; matrix products, arithmetic and copies ran while one was open for 2% of the time, Pallas kernels for 0%

commit v1 on v0

v1 whole, which is shorter than its diff:
```python
import functools

import jax
import jax.numpy as jnp
from jax import lax
from jax.experimental import pallas as pl
from jax.experimental.pallas import tpu as pltpu
from jax.sharding import PartitionSpec as P

HD = 128
TICKS = 3
PASSES = 2
SPLITS = 4


def block_kernel(chunks, info, *refs):
    mids = refs[:chunks]
    ends = refs[chunks:2 * chunks]
    gain, w_hbm, wo_hbm, kc_in, vc_in = refs[2 * chunks:2 * chunks + 5]
    outs = refs[2 * chunks + 5:]
    terms = outs[:chunks]
    kc, vc = outs[chunks:chunks + 2]
    w, wo, normed, attended, w_sems, wo_sem = outs[chunks + 2:]
    depth = w.shape[1]
    piece = depth // SPLITS
    rows = mids[0].shape[0]
    total_rows = rows * chunks
    heads = kc.shape[1] // HD
    applies = info[2] > 0

    @pl.when(applies)
    def _():
        copies = []
        for part in range(3):
            for i in range(SPLITS):
                span = pl.ds(i * piece, piece)
                copy = pltpu.make_async_copy(
                    w_hbm.at[part, span], w.at[part, span], w_sems.at[part, i]
                )
                copy.start()
                copies.append(copy)
        wo_copy = pltpu.make_async_copy(wo_hbm, wo, wo_sem)
        wo_copy.start()

        is_end = info[1] > 0
        gain_row = gain[...].astype(jnp.float32)
        for c in range(chunks):
            span = pl.ds(c * rows, rows)

            def put(ref, span=span):
                wide = ref[...].astype(jnp.float32)
                mean_square = jnp.mean(wide * wide, axis=-1, keepdims=True)
                normed[span, :] = (
                    wide * lax.rsqrt(mean_square + 1e-06) * gain_row
                ).astype(jnp.bfloat16)

            @pl.when(is_end)
            def _(put=put, c=c):
                put(ends[c])

            @pl.when(jnp.logical_not(is_end))
            def _(put=put, c=c):
                put(mids[c])

        parts = []
        for part in range(3):
            total = None
            for i in range(SPLITS):
                copies[part * SPLITS + i].wait()
                span = pl.ds(i * piece, piece)
                product = jnp.dot(
                    normed[:, span], w[part, span, :], preferred_element_type=jnp.float32
                )
                total = product if total is None else total + product
            parts.append(total.astype(jnp.bfloat16))
        query, key, value = parts
        start = pl.multiple_of(info[0], total_rows)
        kc[...] = kc_in[...]
        vc[...] = vc_in[...]
        kc[pl.ds(start, total_rows), :] = key
        vc[pl.ds(start, total_rows), :] = value
        for h in range(heads):
            cols = pl.ds(h * HD, HD)
            scores = lax.dot_general(
                query[:, h * HD:(h + 1) * HD],
                kc[:, cols],
                (((1,), (1,)), ((), ())),
                preferred_element_type=jnp.float32,
            ) * HD ** (-0.5)
            top = jnp.max(scores, axis=-1, keepdims=True)
            weights = jnp.exp(scores - top)
            probs = (weights / jnp.sum(weights, axis=-1, keepdims=True)).astype(jnp.bfloat16)
            attended[:, cols] = jnp.dot(
                probs, vc[:, cols], preferred_element_type=jnp.float32
            ).astype(jnp.bfloat16)
        wo_copy.wait()
        for c in range(chunks):
            terms[c][...] = jnp.dot(
                attended[pl.ds(c * rows, rows), :], wo[...], preferred_element_type=jnp.float32
            ).astype(jnp.bfloat16)

    @pl.when(jnp.logical_not(applies))
    def _():
        kc[...] = kc_in[...]
        vc[...] = vc_in[...]
        for c in range(chunks):
            terms[c][...] = jnp.zeros_like(terms[c])


def block_terms(info, mids, ends, gain, w, wo, kc, vc):
    chunks = len(mids)
    rows, width = mids[0].shape
    vmem = pl.BlockSpec(memory_space=pltpu.VMEM)
    hbm = pl.BlockSpec(memory_space=pl.ANY)
    row_count = rows * chunks
    flops = 2 * row_count * (w.size + wo.size + 2 * kc.size)
    out = pl.pallas_call(
        functools.partial(block_kernel, chunks),
        out_shape=[jax.ShapeDtypeStruct((rows, width), jnp.bfloat16)] * chunks
        + [jax.ShapeDtypeStruct(kc.shape, kc.dtype)] * 2,
        in_specs=[pl.BlockSpec(memory_space=pltpu.SMEM)]
        + [vmem] * (2 * chunks)
        + [vmem, hbm, hbm, vmem, vmem],
        out_specs=[vmem] * (chunks + 2),
        scratch_shapes=[
            pltpu.VMEM(w.shape, w.dtype),
            pltpu.VMEM(wo.shape, wo.dtype),
            pltpu.VMEM((row_count, width), jnp.bfloat16),
            pltpu.VMEM((row_count, kc.shape[1]), jnp.bfloat16),
            pltpu.SemaphoreType.DMA((3, SPLITS)),
            pltpu.SemaphoreType.DMA,
        ],
        compiler_params=pltpu.CompilerParams(vmem_limit_bytes=28 * 2**20),
        cost_estimate=pl.CostEstimate(
            flops=flops, bytes_accessed=2 * (w.size + wo.size), transcendentals=0
        ),
    )(info, *mids, *ends, gain, w, wo, kc, vc)
    return out[:chunks], out[chunks], out[chunks + 1]


def send(block, pairs, hop):
    sections = lax.axis_size("section")
    n = lax.axis_size("uly")
    route = [
        (s * n + a, (s + hop) % sections * n + b) for s in range(sections) for a, b in pairs
    ]
    return lax.ppermute(block, ("section", "uly"), route)


def added(*blocks):
    total = blocks[0].astype(jnp.float32)
    for block in blocks[1:]:
        total = total + block.astype(jnp.float32)
    return total.astype(jnp.bfloat16)


INWARD = ((0, 1), (3, 2))
ACROSS = ((1, 2), (2, 1))
OUTWARD = ((1, 0), (2, 3))
STAY = ((1, 1), (2, 2))


def gathered(own, place):
    n = lax.axis_size("uly")
    right, left = own, own
    from_left, from_right = [own], [own]
    for step in range(1, n):
        right = send(right, [(i, i + 1) for i in range(step - 1, n - 1)], 0)
        left = send(left, [(i, i - 1) for i in range(1, n - step + 1)], 0)
        from_left.append(right)
        from_right.append(left)
    shards_in_order = []
    for j in range(n):
        block = own
        for z in range(n):
            if z != j:
                other = from_left[z - j] if z > j else from_right[j - z]
                block = jnp.where(place == z, other, block)
        shards_in_order.append(block)
    return shards_in_order


def shards(
    state, patch_slot, section_active, qkv_weight, out_weight, norm_gain, stale_keys, stale_values
):
    section_count = lax.axis_size("section")
    section_index = lax.axis_index("section")
    place = lax.axis_index("uly")
    w = jnp.transpose(qkv_weight[0], (1, 0, 2))
    wo = out_weight[0]
    block_count = section_active[0]
    kc = stale_keys[0]
    vc = stale_values[0]
    patch_rows = state.shape[1] * lax.axis_size("uly")
    is_end = ((place == 0) | (place == 3)).astype(jnp.int32)
    lower = place <= 1
    mids = gathered(state[0], place)
    ends = mids
    for tick in range(TICKS):
        slot = patch_slot[(section_index - tick) % section_count]
        for index in range(PASSES):
            applies = block_count > index
            info = jnp.stack([slot * patch_rows, is_end, applies.astype(jnp.int32)])
            terms, kc, vc = block_terms(info, mids, ends, norm_gain, w, wo, kc, vc)
            last = index == PASSES - 1
            if last and tick == TICKS - 1:
                sums = [None] * 4
                for c in (0, 3, 1, 2):
                    sums[c] = added(terms[c], send(terms[c], INWARD, 0))
                results = []
                for near, far in ((0, 3), (1, 2)):
                    arrived = send(jnp.where(lower, sums[far], sums[near]), ACROSS, 0)
                    own = jnp.where(lower, sums[near], sums[far])
                    before = jnp.where(lower, mids[near], mids[far])
                    after = jnp.where(applies, added(before, own, arrived), before)
                    results.append(send(after, OUTWARD if near == 0 else STAY, 1))
                return jnp.where(is_end > 0, results[0], results[1])[None]
            next_mids, next_ends = [], []
            for c in range(len(terms)):
                inner = added(terms[c], send(terms[c], INWARD, 0))
                arrived = send(inner, ACROSS, 0)
                after = jnp.where(applies, added(mids[c], inner, arrived), mids[c])
                next_ends.append(send(after, OUTWARD, 1 if last else 0))
                next_mids.append(send(after, STAY, 1) if last else after)
            mids, ends = next_mids, next_ends


def solution(mesh):
    return jax.shard_map(
        shards,
        mesh=mesh,
        in_specs=(
            P("section", "uly", None),
            P(),
            P("section"),
            P("section", None, None, "uly"),
            P("section", "uly", None),
            P("section", None),
            P("section", None, "uly"),
            P("section", None, "uly"),
        ),
        out_specs=P("section", "uly", None),
        check_vma=False,
    )
```

time: 474 us -> 332 us (0.70)
  waiting for transfers between devices: 279 us -> 90.1 us
  starting transfers between devices: 0.22 us -> 163 us
  matrix products: 83.2 us -> 0 us
  Pallas kernels: 0 us -> 56.3 us
  local copies, waits for them, and re-layouts: 50.4 us -> 8.81 us
  blocking collectives: 18.1 us -> 0 us
  other arithmetic: 21.4 us -> 5.57 us
  between operations: 16.5 us -> 4.11 us
    psum x6 -> x0, waiting for transfers between devices: 251 us -> none  [shards(): lax.psum(head_term.astype(jnp.bfloat16), 'uly').astype(jnp.float32)]
    ppermute x3 -> x82, starting transfers between devices: 0.01 us -> 163 us  [send(): return lax.ppermute(block, ('section', 'uly'), route)]
    dot_general x24 -> x0, matrix products: 74.9 us -> none  [the longest x6 36.2 us: shards(): jnp.dot(normed, w_qkv, preferred_element_type=jnp.float32)]
    ppermute x3 -> x82, waiting for transfers between devices: 27.9 us -> 90.1 us  [send(): return lax.ppermute(block, ('section', 'uly'), route)]
    pallas_call x0 -> x6, Pallas kernels: none -> 56.3 us  [block_terms(): pl.pallas_call(functools.partial(block_kernel, chunks), out_shape=[jax.Sh...]
    all_gather x1 -> x0, blocking collectives: 18.1 us -> none  [shards(): current = lax.all_gather(state[0], 'uly', axis=0, tiled=True)]
    unnamed x78 -> x16, local copies, waits for them, and re-layouts: 21.5 us -> 7.38 us
    select_n x12 -> x25, other arithmetic: 14.2 us -> 3.41 us  [the longest x20 1.8 us: shards(): after = jnp.where(applies, added(mids[c], inner, arrived), mids[c])]
  transfers between devices with their start and end apart: 9 -> 82, of which waited for: 9 -> 36; matrix products, arithmetic and copies ran while one was open for 2% -> 2% of each run, Pallas kernels for 0% -> 0%
where the time goes in v1:
time: 332 us; the launch traced here: 328 us
  starting transfers between devices  163 us (49%)
  waiting for transfers between devices  90.1 us (27%)
  Pallas kernels  56.3 us (17%)
  local copies, waits for them, and re-layouts  8.81 us (3%)
  other arithmetic  5.57 us (2%)
  between operations  4.11 us (1%)
    ppermute x82, starting transfers between devices, send(): return lax.ppermute(block, ('section', 'uly'), route)  163 us
    ppermute x82, waiting for transfers between devices, send(): return lax.ppermute(block, ('section', 'uly'), route)  90.1 us
    pallas_call x6, Pallas kernels, block_terms(): pl.pallas_call(functools.partial(block_kernel, chunks), out_shape=[jax.Sh...  56.3 us
    unnamed x16, local copies, waits for them, and re-layouts  7.38 us
  transfers between devices with their start and end apart: 82, of which 36 were waited for; matrix products, arithmetic and copies ran while one was open for 2% of the time, Pallas kernels for 0%

profile of v1, /device:TPU:14, one launch (start us, length us, event | category | flops | bytes accessed | tf_op | source)
XLA Modules:
  0.0 327.7 jit_solution(7383879585460580732)
XLA Ops:
  2.4 3.5 %collective-permute-start = (bf16[32,3072]{1,0:T(8,128)(2,1)}, bf16[32,3072]{1,0:T(8,128)(2,1)S(1)}, u32[]{:S(2)}, u32[]{:S(2)}) collective-permute-start(bf16[32,3072]{1,0:T(8,128)(2,1)} %bitcast.31), channel_id=1, source_target_pairs={{0,1},{1,2},{2,3},{4,5},{5,6},{6,7},{8,9},{9,10},{10,11},{12,13},{... | collective-permute-start | bytes 589832 | tf_op jit(solution)/shard_map/ppermute | solution.py:147
  11.1 3.5 %collective-permute-start.1 = (bf16[32,3072]{1,0:T(8,128)(2,1)S(1)}, bf16[32,3072]{1,0:T(8,128)(2,1)S(1)}, u32[]{:S(2)}, u32[]{:S(2)}) collective-permute-start(bf16[32,3072]{1,0:T(8,128)(2,1)S(1)} %collective-permute-done), channel_id=1, source_target_pairs={{1,2},{2,3},{5,6},{6,7},{9,10},{10,11},{13,14},{14,15},{17,18},{18... | collective-permute-start | bytes 589832 | tf_op jit(solution)/shard_map/ppermute | solution.py:147
  23.4 3.0 copy-done
  30.7 8.4 %shard_map.82 = (bf16[32,3072]{1,0:T(8,128)(2,1)S(1)}, bf16[32,3072]{1,0:T(8,128)(2,1)S(1)}, bf16[32,3072]{1,0:T(8,128)(2,1)S(1)}, bf16[32,3072]{1,0:T(8,128)(2,...) custom-call(s32[3]{0:T(128)S(1)} %pad_add_fusion.5.info, ...), custom_call_target="tpu_custom_call" | custom-call | flops 1308622848 | bytes 9437184 | tf_op jit(solution)/shard_map/pallas_call | solution.py:117
  44.4 4.5 %collective-permute-done.6 = bf16[32,3072]{1,0:T(8,128)(2,1)S(1)} collective-permute-done((bf16[32,3072]{1,0:T(8,128)(2,1)S(1)}, bf16[32,3072]{1,0:T(8,128)(2,1)S(1)}, u32[]{:S(2)}, u32[]{:S(2)}) %collective-permute-start.6) | collective-permute-done | bytes 196640 | tf_op jit(solution)/shard_map/ppermute | solution.py:147
  49.0 6.2 %collective-permute-start.7 = (bf16[32,3072]{1,0:T(8,128)(2,1)S(1)}, bf16[32,3072]{1,0:T(8,128)(2,1)S(1)}, u32[]{:S(2)}, u32[]{:S(2)}) collective-permute-start(bf16[32,3072]{1,0:T(8,128)(2,1)S(1)} %add_convert_fusion.45), channel_id=1, source_target_pairs={{1,2},{2,1},{5,6},{6,5},{9,10},{10,9},{13,14},{14,13},{17,18},{18,... | collective-permute-start | bytes 589832 | tf_op jit(solution)/shard_map/ppermute | solution.py:147
  55.2 4.1 %collective-permute-start.9 = (bf16[32,3072]{1,0:T(8,128)(2,1)S(1)}, bf16[32,3072]{1,0:T(8,128)(2,1)S(1)}, u32[]{:S(2)}, u32[]{:S(2)}) collective-permute-start(bf16[32,3072]{1,0:T(8,128)(2,1)S(1)} %add_convert_fusion.43), channel_id=1, source_target_pairs={{1,2},{2,1},{5,6},{6,5},{9,10},{10,9},{13,14},{14,13},{17,18},{18,... | collective-permute-start | bytes 589832 | tf_op jit(solution)/shard_map/ppermute | solution.py:147
  61.7 3.7 %collective-permute-start.13 = (bf16[32,3072]{1,0:T(8,128)(2,1)S(1)}, bf16[32,3072]{1,0:T(8,128)(2,1)S(1)}, u32[]{:S(2)}, u32[]{:S(2)}) collective-permute-start(bf16[32,3072]{1,0:T(8,128)(2,1)S(1)} %add_convert_fusion.39), channel_id=1, source_target_pairs={{1,2},{2,1},{5,6},{6,5},{9,10},{10,9},{13,14},{14,13},{17,18},{18,... | collective-permute-start | bytes 589832 | tf_op jit(solution)/shard_map/ppermute | solution.py:147
  78.1 10.5 %shard_map.83 = (bf16[32,3072]{1,0:T(8,128)(2,1)S(1)}, bf16[32,3072]{1,0:T(8,128)(2,1)S(1)}, bf16[32,3072]{1,0:T(8,128)(2,1)S(1)}, bf16[32,3072]{1,0:T(8,128)(2,...) custom-call(s32[3]{0:T(128)S(1)} %pad_add_fusion.8.info, bf16[32,3072]{1,0:T(8,128)(2,1)S(1)} %fusion.refs_0_, ...), custom_call_target="tpu_custom_call" | custom-call | flops 1308622848 | bytes 9437184 | tf_op jit(solution)/shard_map/pallas_call | solution.py:117
  93.8 3.4 %collective-permute-done.18 = bf16[32,3072]{1,0:T(8,128)(2,1)S(1)} collective-permute-done((bf16[32,3072]{1,0:T(8,128)(2,1)S(1)}, bf16[32,3072]{1,0:T(8,128)(2,1)S(1)}, u32[]{:S(2)}, u32[]{:S(2)}) %collective-permute-start.18) | collective-permute-done | bytes 196640 | tf_op jit(solution)/shard_map/ppermute | solution.py:147
  99.6 3.6 %collective-permute-start.22 = (bf16[32,3072]{1,0:T(8,128)(2,1)S(1)}, bf16[32,3072]{1,0:T(8,128)(2,1)S(1)}, u32[]{:S(2)}, u32[]{:S(2)}) collective-permute-start(bf16[32,3072]{1,0:T(8,128)(2,1)S(1)} %add_convert_fusion.35), channel_id=1, source_target_pairs={{1,2},{2,1},{5,6},{6,5},{9,10},{10,9},{13,14},{14,13},{17,18},{18,... | collective-permute-start | bytes 589832 | tf_op jit(solution)/shard_map/ppermute | solution.py:147
  105.6 3.6 %collective-permute-start.28 = (bf16[32,3072]{1,0:T(8,128)(2,1)S(1)}, bf16[32,3072]{1,0:T(8,128)(2,1)S(1)}, u32[]{:S(2)}, u32[]{:S(2)}) collective-permute-start(bf16[32,3072]{1,0:T(8,128)(2,1)S(1)} %add_convert_fusion.31), channel_id=1, source_target_pairs={{1,2},{2,1},{5,6},{6,5},{9,10},{10,9},{13,14},{14,13},{17,18},{18,... | collective-permute-start | bytes 589832 | tf_op jit(solution)/shard_map/ppermute | solution.py:147
  127.6 8.5 %shard_map.84 = (bf16[32,3072]{1,0:T(8,128)(2,1)S(1)}, bf16[32,3072]{1,0:T(8,128)(2,1)S(1)}, bf16[32,3072]{1,0:T(8,128)(2,1)S(1)}, bf16[32,3072]{1,0:T(8,128)(2,...) custom-call(s32[3]{0:T(128)S(1)} %pad_add_fusion.4.info, ...), custom_call_target="tpu_custom_call" | custom-call | flops 1308622848 | bytes 9437184 | tf_op jit(solution)/shard_map/pallas_call | solution.py:117
  141.3 4.5 %collective-permute-done.34 = bf16[32,3072]{1,0:T(8,128)(2,1)S(1)} collective-permute-done((bf16[32,3072]{1,0:T(8,128)(2,1)S(1)}, bf16[32,3072]{1,0:T(8,128)(2,1)S(1)}, u32[]{:S(2)}, u32[]{:S(2)}) %collective-permute-start.34) | collective-permute-done | bytes 196640 | tf_op jit(solution)/shard_map/ppermute | solution.py:147
  157.0 3.3 collective-permute-start.41
  167.0 4.2 %collective-permute-done.43.refs_5_ = bf16[32,3072]{1,0:T(8,128)(2,1)S(1)} collective-permute-done((bf16[32,3072]{1,0:T(8,128)(2,1)S(1)}, bf16[32,3072]{1,0:T(8,128)(2,1)S(1)}, u32[]{:S(2)}, u32[]{:S(2)}) %collective-permute-start.43) | collective-permute-done | bytes 196640 | tf_op jit(solution)/shard_map/ppermute | solution.py:147
  171.2 3.1 collective-permute-done.44.refs_6_
  176.4 10.7 %shard_map.85 = (bf16[32,3072]{1,0:T(8,128)(2,1)S(1)}, bf16[32,3072]{1,0:T(8,128)(2,1)S(1)}, bf16[32,3072]{1,0:T(8,128)(2,1)S(1)}, bf16[32,3072]{1,0:T(8,128)(2,...) custom-call(s32[3]{0:T(128)S(1)} %pad_add_fusion.7.info, bf16[32,3072]{1,0:T(8,128)(2,1)S(1)} %fusion.8.refs_0_, ...), custom_call_target="tpu_custom_call" | custom-call | flops 1308622848 | bytes 9437184 | tf_op jit(solution)/shard_map/pallas_call | solution.py:117
  192.3 4.5 %collective-permute-done.46 = bf16[32,3072]{1,0:T(8,128)(2,1)S(1)} collective-permute-done((bf16[32,3072]{1,0:T(8,128)(2,1)S(1)}, bf16[32,3072]{1,0:T(8,128)(2,1)S(1)}, u32[]{:S(2)}, u32[]{:S(2)}) %collective-permute-start.46) | collective-permute-done | bytes 196640 | tf_op jit(solution)/shard_map/ppermute | solution.py:147
  203.6 3.4 %collective-permute-start.53 = (bf16[32,3072]{1,0:T(8,128)(2,1)S(1)}, bf16[32,3072]{1,0:T(8,128)(2,1)S(1)}, u32[]{:S(2)}, u32[]{:S(2)}) collective-permute-start(bf16[32,3072]{1,0:T(8,128)(2,1)S(1)} %add_convert_fusion.17), channel_id=1, source_target_pairs={{1,2},{2,1},{5,6},{6,5},{9,10},{10,9},{13,14},{14,13},{17,18},{18,... | collective-permute-start | bytes 589832 | tf_op jit(solution)/shard_map/ppermute | solution.py:147
  217.7 4.0 %collective-permute-start.54 = (bf16[32,3072]{1,0:T(8,128)(2,1)S(1)}, bf16[32,3072]{1,0:T(8,128)(2,1)S(1)}, u32[]{:S(2)}, u32[]{:S(2)}) collective-permute-start(bf16[32,3072]{1,0:T(8,128)(2,1)S(1)} %fusion.14), channel_id=1, source_target_pairs={{1,5},{2,6},{5,9},{6,10},{9,13},{10,14},{13,17},{14,18},{17,21},{1... | collective-permute-start | bytes 589832 | tf_op jit(solution)/shard_map/ppermute | solution.py:147
  223.1 4.4 %collective-permute-start.57 = (bf16[32,3072]{1,0:T(8,128)(2,1)S(1)}, bf16[32,3072]{1,0:T(8,128)(2,1)S(1)}, u32[]{:S(2)}, u32[]{:S(2)}) collective-permute-start(bf16[32,3072]{1,0:T(8,128)(2,1)S(1)} %fusion.15), channel_id=1, source_target_pairs={{1,5},{2,6},{5,9},{6,10},{9,13},{10,14},{13,17},{14,18},{17,21},{1... | collective-permute-start | bytes 589832 | tf_op jit(solution)/shard_map/ppermute | solution.py:147
  230.1 8.5 %shard_map.86 = (bf16[32,3072]{1,0:T(8,128)(2,1)S(1)}, bf16[32,3072]{1,0:T(8,128)(2,1)S(1)}, bf16[32,3072]{1,0:T(8,128)(2,1)S(1)}, bf16[32,3072]{1,0:T(8,128)(2,...) custom-call(s32[3]{0:T(128)S(1)} %pad_add_fusion.3.info, ...), custom_call_target="tpu_custom_call" | custom-call | flops 1308622848 | bytes 9437184 | tf_op jit(solution)/shard_map/pallas_call | solution.py:117
  243.8 4.4 %collective-permute-done.62 = bf16[32,3072]{1,0:T(8,128)(2,1)S(1)} collective-permute-done((bf16[32,3072]{1,0:T(8,128)(2,1)S(1)}, bf16[32,3072]{1,0:T(8,128)(2,1)S(1)}, u32[]{:S(2)}, u32[]{:S(2)}) %collective-permute-start.62) | collective-permute-done | bytes 196640 | tf_op jit(solution)/shard_map/ppermute | solution.py:147
  270.6 3.8 %collective-permute-done.73.refs_7_ = bf16[32,3072]{1,0:T(8,128)(2,1)S(1)} collective-permute-done((bf16[32,3072]{1,0:T(8,128)(2,1)S(1)}, bf16[32,3072]{1,0:T(8,128)(2,1)S(1)}, u32[]{:S(2)}, u32[]{:S(2)}) %collective-permute-start.73) | collective-permute-done | bytes 196640 | tf_op jit(solution)/shard_map/ppermute | solution.py:147
  274.4 4.2 %collective-permute-done.71.refs_5_ = bf16[32,3072]{1,0:T(8,128)(2,1)S(1)} collective-permute-done((bf16[32,3072]{1,0:T(8,128)(2,1)S(1)}, bf16[32,3072]{1,0:T(8,128)(2,1)S(1)}, u32[]{:S(2)}, u32[]{:S(2)}) %collective-permute-start.71) | collective-permute-done | bytes 196640 | tf_op jit(solution)/shard_map/ppermute | solution.py:147
  278.6 3.1 collective-permute-done.72.refs_6_
  281.7 9.8 %shard_map.87 = (bf16[32,3072]{1,0:T(8,128)(2,1)S(1)}, bf16[32,3072]{1,0:T(8,128)(2,1)S(1)}, bf16[32,3072]{1,0:T(8,128)(2,1)S(1)}, bf16[32,3072]{1,0:T(8,128)(2,...) custom-call(s32[3]{0:T(128)S(1)} %pad_add_fusion.6.info, bf16[32,3072]{1,0:T(8,128)(2,1)S(1)} %fusion.16.refs_0_, ...), custom_call_target="tpu_custom_call" | custom-call | flops 1308622848 | bytes 9437184 | tf_op jit(solution)/shard_map/pallas_call | solution.py:117
  296.7 4.5 %collective-permute-done.74 = bf16[32,3072]{1,0:T(8,128)(2,1)S(1)} collective-permute-done((bf16[32,3072]{1,0:T(8,128)(2,1)S(1)}, bf16[32,3072]{1,0:T(8,128)(2,1)S(1)}, u32[]{:S(2)}, u32[]{:S(2)}) %collective-permute-start.74) | collective-permute-done | bytes 196640 | tf_op jit(solution)/shard_map/ppermute | solution.py:147
  301.2 4.2 %collective-permute-done.75 = bf16[32,3072]{1,0:T(8,128)(2,1)S(1)} collective-permute-done((bf16[32,3072]{1,0:T(8,128)(2,1)S(1)}, bf16[32,3072]{1,0:T(8,128)(2,1)S(1)}, u32[]{:S(2)}, u32[]{:S(2)}) %collective-permute-start.75) | collective-permute-done | bytes 196640 | tf_op jit(solution)/shard_map/ppermute | solution.py:147
  316.4 3.2 collective-permute-done.80
  321.7 5.0 %collective-permute-done.81 = bf16[32,3072]{1,0:T(8,128)(2,1)S(1)} collective-permute-done((bf16[32,3072]{1,0:T(8,128)(2,1)S(1)}, bf16[32,3072]{1,0:T(8,128)(2,1)S(1)}, u32[]{:S(2)}, u32[]{:S(2)}) %collective-permute-start.81) | collective-permute-done | bytes 196640 | tf_op jit(solution)/shard_map/ppermute | solution.py:147
  (207 shorter events, 164.2 us)
Async XLA Ops:
  40.5 14.7 %collective-permute-start.8 = (bf16[32,3072]{1,0:T(8,128)(2,1)S(1)}, bf16[32,3072]{1,0:T(8,128)(2,1)S(1)}, u32[]{:S(2)}, u32[]{:S(2)}) collective-permute-start(bf16[32,3072]{1,0:T(8,128)(2,1)S(1)} %get-tuple-element.40), channel_id=1, source_target_pairs={{0,1},{3,2},{4,5},{7,6},{8,9},{11,10},{12,13},{15,14},{16,17},{19,... | collective-permute-start | bytes 589832 | tf_op jit(solution)/shard_map/ppermute | solution.py:147
  41.8 17.6 %collective-permute-start.10 = (bf16[32,3072]{1,0:T(8,128)(2,1)S(1)}, bf16[32,3072]{1,0:T(8,128)(2,1)S(1)}, u32[]{:S(2)}, u32[]{:S(2)}) collective-permute-start(bf16[32,3072]{1,0:T(8,128)(2,1)S(1)} %get-tuple-element.41), channel_id=1, source_target_pairs={{0,1},{3,2},{4,5},{7,6},{8,9},{11,10},{12,13},{15,14},{16,17},{19,... | collective-permute-start | bytes 589832 | tf_op jit(solution)/shard_map/ppermute | solution.py:147
  43.1 18.5 %collective-permute-start.12 = (bf16[32,3072]{1,0:T(8,128)(2,1)S(1)}, bf16[32,3072]{1,0:T(8,128)(2,1)S(1)}, u32[]{:S(2)}, u32[]{:S(2)}) collective-permute-start(bf16[32,3072]{1,0:T(8,128)(2,1)S(1)} %get-tuple-element.42), channel_id=1, source_target_pairs={{0,1},{3,2},{4,5},{7,6},{8,9},{11,10},{12,13},{15,14},{16,17},{19,... | collective-permute-start | bytes 589832 | tf_op jit(solution)/shard_map/ppermute | solution.py:147
  49.0 16.4 %collective-permute-start.7 = (bf16[32,3072]{1,0:T(8,128)(2,1)S(1)}, bf16[32,3072]{1,0:T(8,128)(2,1)S(1)}, u32[]{:S(2)}, u32[]{:S(2)}) collective-permute-start(bf16[32,3072]{1,0:T(8,128)(2,1)S(1)} %add_convert_fusion.45), channel_id=1, source_target_pairs={{1,2},{2,1},{5,6},{6,5},{9,10},{10,9},{13,14},{14,13},{17,18},{18,... | collective-permute-start | bytes 589832 | tf_op jit(solution)/shard_map/ppermute | solution.py:147
  55.2 11.6 %collective-permute-start.9 = (bf16[32,3072]{1,0:T(8,128)(2,1)S(1)}, bf16[32,3072]{1,0:T(8,128)(2,1)S(1)}, u32[]{:S(2)}, u32[]{:S(2)}) collective-permute-start(bf16[32,3072]{1,0:T(8,128)(2,1)S(1)} %add_convert_fusion.43), channel_id=1, source_target_pairs={{1,2},{2,1},{5,6},{6,5},{9,10},{10,9},{13,14},{14,13},{17,18},{18,... | collective-permute-start | bytes 589832 | tf_op jit(solution)/shard_map/ppermute | solution.py:147
  91.2 12.0 %collective-permute-start.24 = (bf16[32,3072]{1,0:T(8,128)(2,1)S(1)}, bf16[32,3072]{1,0:T(8,128)(2,1)S(1)}, u32[]{:S(2)}, u32[]{:S(2)}) collective-permute-start(bf16[32,3072]{1,0:T(8,128)(2,1)S(1)} %get-tuple-element.47), channel_id=1, source_target_pairs={{0,1},{3,2},{4,5},{7,6},{8,9},{11,10},{12,13},{15,14},{16,17},{19,... | collective-permute-start | bytes 589832 | tf_op jit(solution)/shard_map/ppermute | solution.py:147
  92.5 13.0 %collective-permute-start.27 = (bf16[32,3072]{1,0:T(8,128)(2,1)S(1)}, bf16[32,3072]{1,0:T(8,128)(2,1)S(1)}, u32[]{:S(2)}, u32[]{:S(2)}) collective-permute-start(bf16[32,3072]{1,0:T(8,128)(2,1)S(1)} %get-tuple-element.48), channel_id=1, source_target_pairs={{0,1},{3,2},{4,5},{7,6},{8,9},{11,10},{12,13},{15,14},{16,17},{19,... | collective-permute-start | bytes 589832 | tf_op jit(solution)/shard_map/ppermute | solution.py:147
  97.2 11.9 %collective-permute-start.19 = (bf16[32,3072]{1,0:T(8,128)(2,1)S(1)}, bf16[32,3072]{1,0:T(8,128)(2,1)S(1)}, u32[]{:S(2)}, u32[]{:S(2)}) collective-permute-start(bf16[32,3072]{1,0:T(8,128)(2,1)S(1)} %add_convert_fusion.37), channel_id=1, source_target_pairs={{1,2},{2,1},{5,6},{6,5},{9,10},{10,9},{13,14},{14,13},{17,18},{18,... | collective-permute-start | bytes 589832 | tf_op jit(solution)/shard_map/ppermute | solution.py:147
  99.6 12.9 %collective-permute-start.22 = (bf16[32,3072]{1,0:T(8,128)(2,1)S(1)}, bf16[32,3072]{1,0:T(8,128)(2,1)S(1)}, u32[]{:S(2)}, u32[]{:S(2)}) collective-permute-start(bf16[32,3072]{1,0:T(8,128)(2,1)S(1)} %add_convert_fusion.35), channel_id=1, source_target_pairs={{1,2},{2,1},{5,6},{6,5},{9,10},{10,9},{13,14},{14,13},{17,18},{18,... | collective-permute-start | bytes 589832 | tf_op jit(solution)/shard_map/ppermute | solution.py:147
  137.4 12.6 %collective-permute-start.36 = (bf16[32,3072]{1,0:T(8,128)(2,1)S(1)}, bf16[32,3072]{1,0:T(8,128)(2,1)S(1)}, u32[]{:S(2)}, u32[]{:S(2)}) collective-permute-start(bf16[32,3072]{1,0:T(8,128)(2,1)S(1)} %get-tuple-element.52), channel_id=1, source_target_pairs={{0,1},{3,2},{4,5},{7,6},{8,9},{11,10},{12,13},{15,14},{16,17},{19,... | collective-permute-start | bytes 589832 | tf_op jit(solution)/shard_map/ppermute | solution.py:147
  138.7 15.6 %collective-permute-start.38 = (bf16[32,3072]{1,0:T(8,128)(2,1)S(1)}, bf16[32,3072]{1,0:T(8,128)(2,1)S(1)}, u32[]{:S(2)}, u32[]{:S(2)}) collective-permute-start(bf16[32,3072]{1,0:T(8,128)(2,1)S(1)} %get-tuple-element.53), channel_id=1, source_target_pairs={{0,1},{3,2},{4,5},{7,6},{8,9},{11,10},{12,13},{15,14},{16,17},{19,... | collective-permute-start | bytes 589832 | tf_op jit(solution)/shard_map/ppermute | solution.py:147
  140.0 16.9 %collective-permute-start.40 = (bf16[32,3072]{1,0:T(8,128)(2,1)S(1)}, bf16[32,3072]{1,0:T(8,128)(2,1)S(1)}, u32[]{:S(2)}, u32[]{:S(2)}) collective-permute-start(bf16[32,3072]{1,0:T(8,128)(2,1)S(1)} %get-tuple-element.54), channel_id=1, source_target_pairs={{0,1},{3,2},{4,5},{7,6},{8,9},{11,10},{12,13},{15,14},{16,17},{19,... | collective-permute-start | bytes 589832 | tf_op jit(solution)/shard_map/ppermute | solution.py:147
  145.9 14.4 %collective-permute-start.35 = (bf16[32,3072]{1,0:T(8,128)(2,1)S(1)}, bf16[32,3072]{1,0:T(8,128)(2,1)S(1)}, u32[]{:S(2)}, u32[]{:S(2)}) collective-permute-start(bf16[32,3072]{1,0:T(8,128)(2,1)S(1)} %add_convert_fusion.29), channel_id=1, source_target_pairs={{1,2},{2,1},{5,6},{6,5},{9,10},{10,9},{13,14},{14,13},{17,18},{18,... | collective-permute-start | bytes 589832 | tf_op jit(solution)/shard_map/ppermute | solution.py:147
  150.1 11.6 %collective-permute-start.37 = (bf16[32,3072]{1,0:T(8,128)(2,1)S(1)}, bf16[32,3072]{1,0:T(8,128)(2,1)S(1)}, u32[]{:S(2)}, u32[]{:S(2)}) collective-permute-start(bf16[32,3072]{1,0:T(8,128)(2,1)S(1)} %add_convert_fusion.27), channel_id=1, source_target_pairs={{1,2},{2,1},{5,6},{6,5},{9,10},{10,9},{13,14},{14,13},{17,18},{18,... | collective-permute-start | bytes 589832 | tf_op jit(solution)/shard_map/ppermute | solution.py:147
  163.4 10.9 %collective-permute-start.44 = (bf16[32,3072]{1,0:T(8,128)(2,1)S(1)}, bf16[32,3072]{1,0:T(8,128)(2,1)S(1)}, u32[]{:S(2)}, u32[]{:S(2)}) collective-permute-start(bf16[32,3072]{1,0:T(8,128)(2,1)S(1)} %fusion.10.refs_2_), channel_id=1, source_target_pairs={{1,0},{2,3},{5,4},{6,7},{9,8},{10,11},{13,12},{14,15},{17,16},{18,... | collective-permute-start | bytes 589832 | tf_op jit(solution)/shard_map/ppermute | solution.py:147
  188.4 12.6 %collective-permute-start.49 = (bf16[32,3072]{1,0:T(8,128)(2,1)S(1)}, bf16[32,3072]{1,0:T(8,128)(2,1)S(1)}, u32[]{:S(2)}, u32[]{:S(2)}) collective-permute-start(bf16[32,3072]{1,0:T(8,128)(2,1)S(1)} %get-tuple-element.58), channel_id=1, source_target_pairs={{0,1},{3,2},{4,5},{7,6},{8,9},{11,10},{12,13},{15,14},{16,17},{19,... | collective-permute-start | bytes 589832 | tf_op jit(solution)/shard_map/ppermute | solution.py:147
  189.7 13.8 %collective-permute-start.52 = (bf16[32,3072]{1,0:T(8,128)(2,1)S(1)}, bf16[32,3072]{1,0:T(8,128)(2,1)S(1)}, u32[]{:S(2)}, u32[]{:S(2)}) collective-permute-start(bf16[32,3072]{1,0:T(8,128)(2,1)S(1)} %get-tuple-element.59), channel_id=1, source_target_pairs={{0,1},{3,2},{4,5},{7,6},{8,9},{11,10},{12,13},{15,14},{16,17},{19,... | collective-permute-start | bytes 589832 | tf_op jit(solution)/shard_map/ppermute | solution.py:147
  191.0 16.0 %collective-permute-start.55 = (bf16[32,3072]{1,0:T(8,128)(2,1)S(1)}, bf16[32,3072]{1,0:T(8,128)(2,1)S(1)}, u32[]{:S(2)}, u32[]{:S(2)}) collective-permute-start(bf16[32,3072]{1,0:T(8,128)(2,1)S(1)} %get-tuple-element.60), channel_id=1, source_target_pairs={{0,1},{3,2},{4,5},{7,6},{8,9},{11,10},{12,13},{15,14},{16,17},{19,... | collective-permute-start | bytes 589832 | tf_op jit(solution)/shard_map/ppermute | solution.py:147
  196.9 12.6 %collective-permute-start.47 = (bf16[32,3072]{1,0:T(8,128)(2,1)S(1)}, bf16[32,3072]{1,0:T(8,128)(2,1)S(1)}, u32[]{:S(2)}, u32[]{:S(2)}) collective-permute-start(bf16[32,3072]{1,0:T(8,128)(2,1)S(1)} %add_convert_fusion.21), channel_id=1, source_target_pairs={{1,2},{2,1},{5,6},{6,5},{9,10},{10,9},{13,14},{14,13},{17,18},{18,... | collective-permute-start | bytes 589832 | tf_op jit(solution)/shard_map/ppermute | solution.py:147
  201.1 11.8 %collective-permute-start.50 = (bf16[32,3072]{1,0:T(8,128)(2,1)S(1)}, bf16[32,3072]{1,0:T(8,128)(2,1)S(1)}, u32[]{:S(2)}, u32[]{:S(2)}) collective-permute-start(bf16[32,3072]{1,0:T(8,128)(2,1)S(1)} %add_convert_fusion.19), channel_id=1, source_target_pairs={{1,2},{2,1},{5,6},{6,5},{9,10},{10,9},{13,14},{14,13},{17,18},{18,... | collective-permute-start | bytes 589832 | tf_op jit(solution)/shard_map/ppermute | solution.py:147
  214.3 13.9 %collective-permute-start.51 = (bf16[32,3072]{1,0:T(8,128)(2,1)S(1)}, bf16[32,3072]{1,0:T(8,128)(2,1)S(1)}, u32[]{:S(2)}, u32[]{:S(2)}) collective-permute-start(bf16[32,3072]{1,0:T(8,128)(2,1)S(1)} %fusion.13), channel_id=1, source_target_pairs={{1,5},{2,6},{5,9},{6,10},{9,13},{10,14},{13,17},{14,18},{17,21},{1... | collective-permute-start | bytes 589832 | tf_op jit(solution)/shard_map/ppermute | solution.py:147
  216.3 11.8 %collective-permute-start.60 = (bf16[32,3072]{1,0:T(8,128)(2,1)S(1)}, bf16[32,3072]{1,0:T(8,128)(2,1)S(1)}, u32[]{:S(2)}, u32[]{:S(2)}) collective-permute-start(bf16[32,3072]{1,0:T(8,128)(2,1)S(1)} %fusion.14), channel_id=1, source_target_pairs={{1,4},{2,7},{5,8},{6,11},{9,12},{10,15},{13,16},{14,19},{17,20},{1... | collective-permute-start | bytes 589832 | tf_op jit(solution)/shard_map/ppermute | solution.py:147
  239.9 12.5 %collective-permute-start.64 = (bf16[32,3072]{1,0:T(8,128)(2,1)S(1)}, bf16[32,3072]{1,0:T(8,128)(2,1)S(1)}, u32[]{:S(2)}, u32[]{:S(2)}) collective-permute-start(bf16[32,3072]{1,0:T(8,128)(2,1)S(1)} %get-tuple-element.64), channel_id=1, source_target_pairs={{0,1},{3,2},{4,5},{7,6},{8,9},{11,10},{12,13},{15,14},{16,17},{19,... | collective-permute-start | bytes 589832 | tf_op jit(solution)/shard_map/ppermute | solution.py:147
  241.2 15.4 %collective-permute-start.66 = (bf16[32,3072]{1,0:T(8,128)(2,1)S(1)}, bf16[32,3072]{1,0:T(8,128)(2,1)S(1)}, u32[]{:S(2)}, u32[]{:S(2)}) collective-permute-start(bf16[32,3072]{1,0:T(8,128)(2,1)S(1)} %get-tuple-element.65), channel_id=1, source_target_pairs={{0,1},{3,2},{4,5},{7,6},{8,9},{11,10},{12,13},{15,14},{16,17},{19,... | collective-permute-start | bytes 589832 | tf_op jit(solution)/shard_map/ppermute | solution.py:147
  242.5 18.0 %collective-permute-start.68 = (bf16[32,3072]{1,0:T(8,128)(2,1)S(1)}, bf16[32,3072]{1,0:T(8,128)(2,1)S(1)}, u32[]{:S(2)}, u32[]{:S(2)}) collective-permute-start(bf16[32,3072]{1,0:T(8,128)(2,1)S(1)} %get-tuple-element.66), channel_id=1, source_target_pairs={{0,1},{3,2},{4,5},{7,6},{8,9},{11,10},{12,13},{15,14},{16,17},{19,... | collective-permute-start | bytes 589832 | tf_op jit(solution)/shard_map/ppermute | solution.py:147
  248.2 15.3 %collective-permute-start.63 = (bf16[32,3072]{1,0:T(8,128)(2,1)S(1)}, bf16[32,3072]{1,0:T(8,128)(2,1)S(1)}, u32[]{:S(2)}, u32[]{:S(2)}) collective-permute-start(bf16[32,3072]{1,0:T(8,128)(2,1)S(1)} %add_convert_fusion.13), channel_id=1, source_target_pairs={{1,2},{2,1},{5,6},{6,5},{9,10},{10,9},{13,14},{14,13},{17,18},{18,... | collective-permute-start | bytes 589832 | tf_op jit(solution)/shard_map/ppermute | solution.py:147
  252.4 12.5 %collective-permute-start.65 = (bf16[32,3072]{1,0:T(8,128)(2,1)S(1)}, bf16[32,3072]{1,0:T(8,128)(2,1)S(1)}, u32[]{:S(2)}, u32[]{:S(2)}) collective-permute-start(bf16[32,3072]{1,0:T(8,128)(2,1)S(1)} %add_convert_fusion.11), channel_id=1, source_target_pairs={{1,2},{2,1},{5,6},{6,5},{9,10},{10,9},{13,14},{14,13},{17,18},{18,... | collective-permute-start | bytes 589832 | tf_op jit(solution)/shard_map/ppermute | solution.py:147
  266.4 12.2 %collective-permute-start.71 = (bf16[32,3072]{1,0:T(8,128)(2,1)S(1)}, bf16[32,3072]{1,0:T(8,128)(2,1)S(1)}, u32[]{:S(2)}, u32[]{:S(2)}) collective-permute-start(bf16[32,3072]{1,0:T(8,128)(2,1)S(1)} %fusion.18.refs_1_), channel_id=1, source_target_pairs={{1,0},{2,3},{5,4},{6,7},{9,8},{10,11},{13,12},{14,15},{17,16},{18,... | collective-permute-start | bytes 589832 | tf_op jit(solution)/shard_map/ppermute | solution.py:147
  269.2 12.5 %collective-permute-start.72 = (bf16[32,3072]{1,0:T(8,128)(2,1)S(1)}, bf16[32,3072]{1,0:T(8,128)(2,1)S(1)}, u32[]{:S(2)}, u32[]{:S(2)}) collective-permute-start(bf16[32,3072]{1,0:T(8,128)(2,1)S(1)} %fusion.19.refs_2_), channel_id=1, source_target_pairs={{1,0},{2,3},{5,4},{6,7},{9,8},{10,11},{13,12},{14,15},{17,16},{18,... | collective-permute-start | bytes 589832 | tf_op jit(solution)/shard_map/ppermute | solution.py:147
  292.8 12.6 %collective-permute-start.75 = (bf16[32,3072]{1,0:T(8,128)(2,1)S(1)}, bf16[32,3072]{1,0:T(8,128)(2,1)S(1)}, u32[]{:S(2)}, u32[]{:S(2)}) collective-permute-start(bf16[32,3072]{1,0:T(8,128)(2,1)S(1)} %get-tuple-element.70), channel_id=1, source_target_pairs={{0,1},{3,2},{4,5},{7,6},{8,9},{11,10},{12,13},{15,14},{16,17},{19,... | collective-permute-start | bytes 589832 | tf_op jit(solution)/shard_map/ppermute | solution.py:147
  294.1 15.6 %collective-permute-start.78 = (bf16[32,3072]{1,0:T(8,128)(2,1)S(1)}, bf16[32,3072]{1,0:T(8,128)(2,1)S(1)}, u32[]{:S(2)}, u32[]{:S(2)}) collective-permute-start(bf16[32,3072]{1,0:T(8,128)(2,1)S(1)} %get-tuple-element.71), channel_id=1, source_target_pairs={{0,1},{3,2},{4,5},{7,6},{8,9},{11,10},{12,13},{15,14},{16,17},{19,... | collective-permute-start | bytes 589832 | tf_op jit(solution)/shard_map/ppermute | solution.py:147
  295.4 16.5 %collective-permute-start.79 = (bf16[32,3072]{1,0:T(8,128)(2,1)S(1)}, bf16[32,3072]{1,0:T(8,128)(2,1)S(1)}, u32[]{:S(2)}, u32[]{:S(2)}) collective-permute-start(bf16[32,3072]{1,0:T(8,128)(2,1)S(1)} %get-tuple-element.72), channel_id=1, source_target_pairs={{0,1},{3,2},{4,5},{7,6},{8,9},{11,10},{12,13},{15,14},{16,17},{19,... | collective-permute-start | bytes 589832 | tf_op jit(solution)/shard_map/ppermute | solution.py:147
  (58 other events, 574.7 us)

commit v2 on v1

v2 whole, which is shorter than its diff:
```python
import functools

import jax
import jax.numpy as jnp
from jax import lax
from jax.experimental import pallas as pl
from jax.experimental.pallas import tpu as pltpu
from jax.sharding import PartitionSpec as P

HD = 128
TICKS = 3
PASSES = 2
VMEM_LIMIT = 24 * 2**20


def block_kernel(chunks, info, *refs):
    mids = refs[:chunks]
    ends = refs[chunks:2 * chunks]
    gain, w, wo, kc_in, vc_in = refs[2 * chunks:2 * chunks + 5]
    outs = refs[2 * chunks + 5:]
    terms = outs[:chunks]
    kc, vc, normed, attended = outs[chunks:]
    rows = mids[0].shape[0]
    total_rows = rows * chunks
    heads = kc.shape[1] // HD
    applies = info[2] > 0

    @pl.when(applies)
    def _():
        is_end = info[1] > 0
        gain_row = gain[...].astype(jnp.float32)
        for c in range(chunks):
            span = pl.ds(c * rows, rows)

            def put(ref, span=span):
                wide = ref[...].astype(jnp.float32)
                mean_square = jnp.mean(wide * wide, axis=-1, keepdims=True)
                normed[span, :] = (
                    wide * lax.rsqrt(mean_square + 1e-06) * gain_row
                ).astype(jnp.bfloat16)

            @pl.when(is_end)
            def _(put=put, c=c):
                put(ends[c])

            @pl.when(jnp.logical_not(is_end))
            def _(put=put, c=c):
                put(mids[c])

        query, key, value = [
            jnp.dot(normed[...], w[part], preferred_element_type=jnp.float32).astype(jnp.bfloat16)
            for part in range(3)
        ]
        start = pl.multiple_of(info[0], total_rows)
        kc[pl.ds(start, total_rows), :] = key
        vc[pl.ds(start, total_rows), :] = value
        for h in range(heads):
            cols = pl.ds(h * HD, HD)
            scores = lax.dot_general(
                query[:, h * HD:(h + 1) * HD],
                kc[:, cols],
                (((1,), (1,)), ((), ())),
                preferred_element_type=jnp.float32,
            ) * HD ** (-0.5)
            top = jnp.max(scores, axis=-1, keepdims=True)
            weights = jnp.exp(scores - top)
            probs = (weights / jnp.sum(weights, axis=-1, keepdims=True)).astype(jnp.bfloat16)
            attended[:, cols] = jnp.dot(
                probs, vc[:, cols], preferred_element_type=jnp.float32
            ).astype(jnp.bfloat16)
        for c in range(chunks):
            terms[c][...] = jnp.dot(
                attended[pl.ds(c * rows, rows), :], wo[...], preferred_element_type=jnp.float32
            ).astype(jnp.bfloat16)


def load_kernel(*refs):
    count = len(refs) // 2
    sems = refs[-1]
    pairs = list(zip(refs[:count], refs[count:2 * count]))
    copies = [pltpu.make_async_copy(a, b, sems.at[i]) for i, (a, b) in enumerate(pairs)]
    for copy in copies:
        copy.start()
    for copy in copies:
        copy.wait()


def loaded(*arrays):
    return pl.pallas_call(
        load_kernel,
        out_shape=[pltpu.VMEM(a.shape, a.dtype) for a in arrays],
        in_specs=[pl.BlockSpec(memory_space=pl.ANY)] * len(arrays),
        out_specs=[pl.BlockSpec(memory_space=pltpu.VMEM)] * len(arrays),
        scratch_shapes=[pltpu.SemaphoreType.DMA((len(arrays),))],
        compiler_params=pltpu.CompilerParams(vmem_limit_bytes=VMEM_LIMIT),
        cost_estimate=pl.CostEstimate(
            flops=0, bytes_accessed=2 * sum(a.size for a in arrays), transcendentals=0
        ),
    )(*[pltpu.with_memory_space_constraint(a, pltpu.HBM) for a in arrays])


def block_terms(info, mids, ends, gain, w, wo, kc, vc):
    chunks = len(mids)
    rows, width = mids[0].shape
    vmem = pl.BlockSpec(memory_space=pltpu.VMEM)
    row_count = rows * chunks
    flops = 2 * row_count * (w.size + wo.size + 2 * kc.size)
    held = [pltpu.with_memory_space_constraint(x, pltpu.VMEM) for x in (w, wo, kc, vc)]
    cache = pltpu.VMEM(kc.shape, kc.dtype)
    out = pl.pallas_call(
        functools.partial(block_kernel, chunks),
        out_shape=[jax.ShapeDtypeStruct((rows, width), jnp.bfloat16)] * chunks + [cache] * 2,
        in_specs=[pl.BlockSpec(memory_space=pltpu.SMEM)] + [vmem] * (2 * chunks + 5),
        out_specs=[vmem] * (chunks + 2),
        input_output_aliases={2 * chunks + 4: chunks, 2 * chunks + 5: chunks + 1},
        scratch_shapes=[
            pltpu.VMEM((row_count, width), jnp.bfloat16),
            pltpu.VMEM((row_count, kc.shape[1]), jnp.bfloat16),
        ],
        compiler_params=pltpu.CompilerParams(vmem_limit_bytes=VMEM_LIMIT),
        cost_estimate=pl.CostEstimate(
            flops=flops, bytes_accessed=2 * (w.size + wo.size), transcendentals=0
        ),
    )(info, *mids, *ends, gain, *held)
    return out[:chunks], out[chunks], out[chunks + 1]


def send(block, pairs, hop):
    sections = lax.axis_size("section")
    n = lax.axis_size("uly")
    route = [
        (s * n + a, (s + hop) % sections * n + b) for s in range(sections) for a, b in pairs
    ]
    return lax.ppermute(block, ("section", "uly"), route)


def added(*blocks):
    total = blocks[0].astype(jnp.float32)
    for block in blocks[1:]:
        total = total + block.astype(jnp.float32)
    return total.astype(jnp.bfloat16)


INWARD = ((0, 1), (3, 2))
ACROSS = ((1, 2), (2, 1))
OUTWARD = ((1, 0), (2, 3))
STAY = ((1, 1), (2, 2))


def behind(block, *others):
    return lax.optimization_barrier((block, *others))[0]


def gathered(own, place):
    n = lax.axis_size("uly")
    turned = [own] + [send(own, [(i, (i + k) % n) for i in range(n)], 0) for k in range(1, n)]
    shards_in_order = []
    for j in range(n):
        block = turned[0]
        for k in range(1, n):
            block = jnp.where((place - k) % n == j, turned[k], block)
        shards_in_order.append(block)
    return shards_in_order


def shards(
    state, patch_slot, section_active, qkv_weight, out_weight, norm_gain, stale_keys, stale_values
):
    section_count = lax.axis_size("section")
    section_index = lax.axis_index("section")
    place = lax.axis_index("uly")
    w = jnp.transpose(qkv_weight[0], (1, 0, 2))
    wo = out_weight[0]
    block_count = section_active[0]
    w, wo, kc, vc = loaded(w, wo, stale_keys[0], stale_values[0])
    patch_rows = state.shape[1] * lax.axis_size("uly")
    is_end = ((place == 0) | (place == 3)).astype(jnp.int32)
    lower = place <= 1
    mids = gathered(state[0], place)
    ends = mids
    for tick in range(TICKS):
        slot = patch_slot[(section_index - tick) % section_count]
        for index in range(PASSES):
            applies = block_count > index
            info = jnp.stack([slot * patch_rows, is_end, applies.astype(jnp.int32)])
            terms, kc, vc = block_terms(info, mids, ends, norm_gain, w, wo, kc, vc)
            last = index == PASSES - 1
            if last and tick == TICKS - 1:
                sums = [None] * 4
                for c in (0, 3, 1, 2):
                    sums[c] = added(terms[c], send(terms[c], INWARD, 0))
                results = []
                for near, far in ((0, 3), (1, 2)):
                    arrived = send(jnp.where(lower, sums[far], sums[near]), ACROSS, 0)
                    own = jnp.where(lower, sums[near], sums[far])
                    before = jnp.where(lower, mids[near], mids[far])
                    after = jnp.where(applies, added(before, own, arrived), before)
                    results.append(send(after, OUTWARD if near == 0 else STAY, 1))
                return jnp.where(is_end > 0, results[0], results[1])[None]
            count = len(terms)
            next_mids, next_ends = [None] * count, [None] * count
            firsts, inners, seconds = [None] * count, [None] * count, [None] * count
            for step in range(count + 2):
                c = step
                if c < count:
                    block = terms[c] if c < 2 else behind(terms[c], inners[c - 2])
                    firsts[c] = send(block, INWARD, 0)
                c = step - 1
                if 0 <= c < count:
                    arrived = firsts[c] if c < 2 else behind(firsts[c], next_mids[c - 2])
                    inners[c] = added(terms[c], arrived)
                    seconds[c] = send(inners[c], ACROSS, 0)
                c = step - 2
                if 0 <= c < count:
                    updated = added(mids[c], inners[c], seconds[c])
                    updated = jnp.where(applies, updated, mids[c])
                    next_ends[c] = send(updated, OUTWARD, 1 if last else 0)
                    next_mids[c] = updated
            if last:
                next_mids = [
                    send(
                        behind(next_mids[c], next_mids[c + 1] if c + 2 < count else next_ends[c - 1]),
                        STAY,
                        1,
                    )
                    for c in range(count)
                ]
            mids, ends = next_mids, next_ends


def solution(mesh):
    return jax.shard_map(
        shards,
        mesh=mesh,
        in_specs=(
            P("section", "uly", None),
            P(),
            P("section"),
            P("section", None, None, "uly"),
            P("section", "uly", None),
            P("section", None),
            P("section", None, "uly"),
            P("section", None, "uly"),
        ),
        out_specs=P("section", "uly", None),
        check_vma=False,
    )
```

time: 332 us -> 305 us (0.919)
  Pallas kernels: 56.3 us -> 35.6 us
  local copies, waits for them, and re-layouts: 8.81 us -> 1.44 us
  waiting for transfers between devices: 90.1 us -> 95.6 us
    pallas_call x6, Pallas kernels: 56.3 us -> 31.7 us  [block_terms(): pl.pallas_call(functools.partial(block_kernel, chunks), out_shape=[jax.Sh...]
    unnamed x16 -> x4, local copies, waits for them, and re-layouts: 7.38 us -> 0.01 us
    ppermute x82 -> x79, waiting for transfers between devices: 90.1 us -> 95.6 us  [send(): return lax.ppermute(block, ('section', 'uly'), route)]
    pallas_call x0 -> x1, Pallas kernels: none -> 3.91 us  [loaded(): pl.pallas_call(load_kernel, out_shape=[pltpu.VMEM(a.shape, a.dtype) for a...]
    ppermute x82 -> x79, starting transfers between devices: 163 us -> 162 us  [send(): return lax.ppermute(block, ('section', 'uly'), route)]
  transfers between devices with their start and end apart: 82 -> 79, of which waited for: 36 -> 33; matrix products, arithmetic and copies ran while one was open for 2% -> 2% of each run, Pallas kernels for 0% -> 1%
where the time goes in v2:
time: 305 us; the launch traced here: 303 us
  starting transfers between devices  162 us (53%)
  waiting for transfers between devices  95.6 us (31%)
  Pallas kernels  35.6 us (12%)
  other arithmetic  4.6 us (2%)
  between operations  3.81 us (1%)
    ppermute x79, starting transfers between devices, send(): return lax.ppermute(block, ('section', 'uly'), route)  162 us
    ppermute x79, waiting for transfers between devices, send(): return lax.ppermute(block, ('section', 'uly'), route)  95.6 us
    pallas_call x6, Pallas kernels, block_terms(): pl.pallas_call(functools.partial(block_kernel, chunks), out_shape=[jax.Sh...  31.7 us
  transfers between devices with their start and end apart: 79, of which 33 were waited for; matrix products, arithmetic and copies ran while one was open for 2% of the time, Pallas kernels for 1%

profile of v2, /device:TPU:14, one launch (start us, length us, event | category | flops | bytes accessed | tf_op | source)
XLA Modules:
  0.0 302.8 jit_solution(15652847858965295031)
XLA Ops:
  7.4 3.9 %shard_map.82 = (bf16[3,3072,384]{2,1,0:T(8,128)(2,1)S(1)}, bf16[384,3072]{1,0:T(8,128)(2,1)S(1)}, bf16[512,384]{1,0:T(8,128)(2,1)S(1)}, bf16[512,384]{1,0:T(8,128)(2,1)S(1)}) custom-call(bf16[3,3072,384]{2,1,0:T(8,128)(2,1)} %bitcast.16, bf16[384,3072]{1,0:T(8,128)(2,1)} %bitcast.17, bf16[512,384]{1,0:T(8,128)(2,1)} %bitcast.18, bf16[512,384]{1,0:T(8,128)(2,1)} %bitcast.19), custom_call_target="tpu_custom_call" | custom-call | bytes 10223616 | tf_op jit(solution)/shard_map/pallas_call | solution.py:89
  11.4 4.3 %collective-permute-done.2 = bf16[32,3072]{1,0:T(8,128)(2,1)S(1)} collective-permute-done((bf16[32,3072]{1,0:T(8,128)(2,1)}, bf16[32,3072]{1,0:T(8,128)(2,1)S(1)}, u32[]{:S(2)}, u32[]{:S(2)}) %collective-permute-start.2) | collective-permute-done | bytes 196640 | tf_op jit(solution)/shard_map/ppermute | solution.py:134
  20.5 5.3 %shard_map.83 = (bf16[32,3072]{1,0:T(8,128)(2,1)S(1)}, bf16[32,3072]{1,0:T(8,128)(2,1)S(1)}, bf16[32,3072]{1,0:T(8,128)(2,1)S(1)}, bf16[32,3072]{1,0:T(8,128)(2,...) custom-call(s32[3]{0:T(128)S(1)} %pad_add_fusion.5.info, ...), custom_call_target="tpu_custom_call", output_to_operand_aliasing={{4}: (12, {}), {5}: (13, {})} | custom-call | flops 1308622848 | bytes 9437184 | tf_op jit(solution)/shard_map/pallas_call | solution.py:110
  28.4 7.1 %collective-permute-done.3 = bf16[32,3072]{1,0:T(8,128)(2,1)S(1)} collective-permute-done((bf16[32,3072]{1,0:T(8,128)(2,1)S(1)}, bf16[32,3072]{1,0:T(8,128)(2,1)S(1)}, u32[]{:S(2)}, u32[]{:S(2)}) %collective-permute-start.3) | collective-permute-done | bytes 196640 | tf_op jit(solution)/shard_map/ppermute | solution.py:134
  38.9 3.9 %collective-permute-start.6 = (bf16[32,3072]{1,0:T(8,128)(2,1)S(1)}, bf16[32,3072]{1,0:T(8,128)(2,1)S(1)}, u32[]{:S(2)}, u32[]{:S(2)}) collective-permute-start(bf16[32,3072]{1,0:T(8,128)(2,1)S(1)} %add_convert_fusion.43), channel_id=1, source_target_pairs={{1,2},{2,1},{5,6},{6,5},{9,10},{10,9},{13,14},{14,13},{17,18},{18,... | collective-permute-start | bytes 589832 | tf_op jit(solution)/shard_map/ppermute | solution.py:134
  44.2 4.6 %collective-permute-start.11 = (bf16[32,3072]{1,0:T(8,128)(2,1)S(1)}, bf16[32,3072]{1,0:T(8,128)(2,1)S(1)}, u32[]{:S(2)}, u32[]{:S(2)}) collective-permute-start(bf16[32,3072]{1,0:T(8,128)(2,1)S(1)} %fusion.refs_0_), channel_id=1, source_target_pairs={{1,0},{2,3},{5,4},{6,7},{9,8},{10,11},{13,12},{14,15},{17,16},{18,... | collective-permute-start | bytes 589832 | tf_op jit(solution)/shard_map/ppermute | solution.py:134
  52.2 3.9 %collective-permute-start.10 = (bf16[32,3072]{1,0:T(8,128)(2,1)S(1)}, bf16[32,3072]{1,0:T(8,128)(2,1)S(1)}, u32[]{:S(2)}, u32[]{:S(2)}) collective-permute-start(bf16[32,3072]{1,0:T(8,128)(2,1)S(1)} %add_convert_fusion.39), channel_id=1, source_target_pairs={{1,2},{2,1},{5,6},{6,5},{9,10},{10,9},{13,14},{14,13},{17,18},{18,... | collective-permute-start | bytes 589832 | tf_op jit(solution)/shard_map/ppermute | solution.py:134
  66.9 5.3 %shard_map.84 = (bf16[32,3072]{1,0:T(8,128)(2,1)S(1)}, bf16[32,3072]{1,0:T(8,128)(2,1)S(1)}, bf16[32,3072]{1,0:T(8,128)(2,1)S(1)}, bf16[32,3072]{1,0:T(8,128)(2,...) custom-call(s32[3]{0:T(128)S(1)} %pad_add_fusion.8.info, ...), custom_call_target="tpu_custom_call", output_to_operand_aliasing={{4}: (12, {}), {5}: (13, {})} | custom-call | flops 1308622848 | bytes 9437184 | tf_op jit(solution)/shard_map/pallas_call | solution.py:110
  74.8 6.1 %collective-permute-done.15 = bf16[32,3072]{1,0:T(8,128)(2,1)S(1)} collective-permute-done((bf16[32,3072]{1,0:T(8,128)(2,1)S(1)}, bf16[32,3072]{1,0:T(8,128)(2,1)S(1)}, u32[]{:S(2)}, u32[]{:S(2)}) %collective-permute-start.15) | collective-permute-done | bytes 196640 | tf_op jit(solution)/shard_map/ppermute | solution.py:134
  84.5 3.6 %collective-permute-start.18 = (bf16[32,3072]{1,0:T(8,128)(2,1)S(1)}, bf16[32,3072]{1,0:T(8,128)(2,1)S(1)}, u32[]{:S(2)}, u32[]{:S(2)}) collective-permute-start(bf16[32,3072]{1,0:T(8,128)(2,1)S(1)} %add_convert_fusion.35), channel_id=1, source_target_pairs={{1,2},{2,1},{5,6},{6,5},{9,10},{10,9},{13,14},{14,13},{17,18},{18,... | collective-permute-start | bytes 589832 | tf_op jit(solution)/shard_map/ppermute | solution.py:134
  90.9 3.5 %collective-permute-start.21 = (bf16[32,3072]{1,0:T(8,128)(2,1)S(1)}, bf16[32,3072]{1,0:T(8,128)(2,1)S(1)}, u32[]{:S(2)}, u32[]{:S(2)}) collective-permute-start(bf16[32,3072]{1,0:T(8,128)(2,1)S(1)} %add_convert_fusion.33), channel_id=1, source_target_pairs={{1,2},{2,1},{5,6},{6,5},{9,10},{10,9},{13,14},{14,13},{17,18},{18,... | collective-permute-start | bytes 589832 | tf_op jit(solution)/shard_map/ppermute | solution.py:134
  95.8 3.7 %collective-permute-start.19 = (bf16[32,3072]{1,0:T(8,128)(2,1)S(1)}, bf16[32,3072]{1,0:T(8,128)(2,1)S(1)}, u32[]{:S(2)}, u32[]{:S(2)}) collective-permute-start(bf16[32,3072]{1,0:T(8,128)(2,1)S(1)} %fusion.4), channel_id=1, source_target_pairs={{1,5},{2,6},{5,9},{6,10},{9,13},{10,14},{13,17},{14,18},{17,21},{1... | collective-permute-start | bytes 589832 | tf_op jit(solution)/shard_map/ppermute | solution.py:134
  99.5 3.6 %collective-permute-start.26 = (bf16[32,3072]{1,0:T(8,128)(2,1)S(1)}, bf16[32,3072]{1,0:T(8,128)(2,1)S(1)}, u32[]{:S(2)}, u32[]{:S(2)}) collective-permute-start(bf16[32,3072]{1,0:T(8,128)(2,1)S(1)} %add_convert_fusion.31), channel_id=1, source_target_pairs={{1,2},{2,1},{5,6},{6,5},{9,10},{10,9},{13,14},{14,13},{17,18},{18,... | collective-permute-start | bytes 589832 | tf_op jit(solution)/shard_map/ppermute | solution.py:134
  104.5 3.7 %collective-permute-done.26 = bf16[32,3072]{1,0:T(8,128)(2,1)S(1)} collective-permute-done((bf16[32,3072]{1,0:T(8,128)(2,1)S(1)}, bf16[32,3072]{1,0:T(8,128)(2,1)S(1)}, u32[]{:S(2)}, u32[]{:S(2)}) %collective-permute-start.26) | collective-permute-done | bytes 196640 | tf_op jit(solution)/shard_map/ppermute | solution.py:134
  120.8 5.3 %shard_map.85 = (bf16[32,3072]{1,0:T(8,128)(2,1)S(1)}, bf16[32,3072]{1,0:T(8,128)(2,1)S(1)}, bf16[32,3072]{1,0:T(8,128)(2,1)S(1)}, bf16[32,3072]{1,0:T(8,128)(2,...) custom-call(s32[3]{0:T(128)S(1)} %pad_add_fusion.4.info, ...), custom_call_target="tpu_custom_call", output_to_operand_aliasing={{4}: (12, {}), {5}: (13, {})} | custom-call | flops 1308622848 | bytes 9437184 | tf_op jit(solution)/shard_map/pallas_call | solution.py:110
  128.7 7.0 %collective-permute-done.31 = bf16[32,3072]{1,0:T(8,128)(2,1)S(1)} collective-permute-done((bf16[32,3072]{1,0:T(8,128)(2,1)S(1)}, bf16[32,3072]{1,0:T(8,128)(2,1)S(1)}, u32[]{:S(2)}, u32[]{:S(2)}) %collective-permute-start.31) | collective-permute-done | bytes 196640 | tf_op jit(solution)/shard_map/ppermute | solution.py:134
  135.7 3.6 %collective-permute-start.32 = (bf16[32,3072]{1,0:T(8,128)(2,1)S(1)}, bf16[32,3072]{1,0:T(8,128)(2,1)S(1)}, u32[]{:S(2)}, u32[]{:S(2)}) collective-permute-start(bf16[32,3072]{1,0:T(8,128)(2,1)S(1)} %add_convert_fusion.29), channel_id=1, source_target_pairs={{1,2},{2,1},{5,6},{6,5},{9,10},{10,9},{13,14},{14,13},{17,18},{18,... | collective-permute-start | bytes 589832 | tf_op jit(solution)/shard_map/ppermute | solution.py:134
  144.7 4.6 %collective-permute-start.39 = (bf16[32,3072]{1,0:T(8,128)(2,1)S(1)}, bf16[32,3072]{1,0:T(8,128)(2,1)S(1)}, u32[]{:S(2)}, u32[]{:S(2)}) collective-permute-start(bf16[32,3072]{1,0:T(8,128)(2,1)S(1)} %fusion.8.refs_0_), channel_id=1, source_target_pairs={{1,0},{2,3},{5,4},{6,7},{9,8},{10,11},{13,12},{14,15},{17,16},{18,... | collective-permute-start | bytes 589832 | tf_op jit(solution)/shard_map/ppermute | solution.py:134
  149.3 3.3 %collective-permute-start.36 = (bf16[32,3072]{1,0:T(8,128)(2,1)S(1)}, bf16[32,3072]{1,0:T(8,128)(2,1)S(1)}, u32[]{:S(2)}, u32[]{:S(2)}) collective-permute-start(bf16[32,3072]{1,0:T(8,128)(2,1)S(1)} %add_convert_fusion.25), channel_id=1, source_target_pairs={{1,2},{2,1},{5,6},{6,5},{9,10},{10,9},{13,14},{14,13},{17,18},{18,... | collective-permute-start | bytes 589832 | tf_op jit(solution)/shard_map/ppermute | solution.py:134
  166.2 5.3 %shard_map.86 = (bf16[32,3072]{1,0:T(8,128)(2,1)S(1)}, bf16[32,3072]{1,0:T(8,128)(2,1)S(1)}, bf16[32,3072]{1,0:T(8,128)(2,1)S(1)}, bf16[32,3072]{1,0:T(8,128)(2,...) custom-call(s32[3]{0:T(128)S(1)} %pad_add_fusion.7.info, ...), custom_call_target="tpu_custom_call", output_to_operand_aliasing={{4}: (12, {}), {5}: (13, {})} | custom-call | flops 1308622848 | bytes 9437184 | tf_op jit(solution)/shard_map/pallas_call | solution.py:110
  174.1 5.3 %collective-permute-done.43 = bf16[32,3072]{1,0:T(8,128)(2,1)S(1)} collective-permute-done((bf16[32,3072]{1,0:T(8,128)(2,1)S(1)}, bf16[32,3072]{1,0:T(8,128)(2,1)S(1)}, u32[]{:S(2)}, u32[]{:S(2)}) %collective-permute-start.43) | collective-permute-done | bytes 196640 | tf_op jit(solution)/shard_map/ppermute | solution.py:134
  179.5 3.5 %collective-permute-start.44 = (bf16[32,3072]{1,0:T(8,128)(2,1)S(1)}, bf16[32,3072]{1,0:T(8,128)(2,1)S(1)}, u32[]{:S(2)}, u32[]{:S(2)}) collective-permute-start(bf16[32,3072]{1,0:T(8,128)(2,1)S(1)} %add_convert_fusion.21), channel_id=1, source_target_pairs={{1,2},{2,1},{5,6},{6,5},{9,10},{10,9},{13,14},{14,13},{17,18},{18,... | collective-permute-start | bytes 589832 | tf_op jit(solution)/shard_map/ppermute | solution.py:134
  194.5 7.7 %collective-permute-start.47 = (bf16[32,3072]{1,0:T(8,128)(2,1)S(1)}, bf16[32,3072]{1,0:T(8,128)(2,1)S(1)}, u32[]{:S(2)}, u32[]{:S(2)}) collective-permute-start(bf16[32,3072]{1,0:T(8,128)(2,1)S(1)} %fusion.12), channel_id=1, source_target_pairs={{1,5},{2,6},{5,9},{6,10},{9,13},{10,14},{13,17},{14,18},{17,21},{1... | collective-permute-start | bytes 589832 | tf_op jit(solution)/shard_map/ppermute | solution.py:134
  202.2 3.6 %collective-permute-start.54 = (bf16[32,3072]{1,0:T(8,128)(2,1)S(1)}, bf16[32,3072]{1,0:T(8,128)(2,1)S(1)}, u32[]{:S(2)}, u32[]{:S(2)}) collective-permute-start(bf16[32,3072]{1,0:T(8,128)(2,1)S(1)} %add_convert_fusion.15), channel_id=1, source_target_pairs={{1,2},{2,1},{5,6},{6,5},{9,10},{10,9},{13,14},{14,13},{17,18},{18,... | collective-permute-start | bytes 589832 | tf_op jit(solution)/shard_map/ppermute | solution.py:134
  207.2 3.6 %collective-permute-done.54 = bf16[32,3072]{1,0:T(8,128)(2,1)S(1)} collective-permute-done((bf16[32,3072]{1,0:T(8,128)(2,1)S(1)}, bf16[32,3072]{1,0:T(8,128)(2,1)S(1)}, u32[]{:S(2)}, u32[]{:S(2)}) %collective-permute-start.54) | collective-permute-done | bytes 196640 | tf_op jit(solution)/shard_map/ppermute | solution.py:134
  223.3 5.3 %shard_map.87 = (bf16[32,3072]{1,0:T(8,128)(2,1)S(1)}, bf16[32,3072]{1,0:T(8,128)(2,1)S(1)}, bf16[32,3072]{1,0:T(8,128)(2,1)S(1)}, bf16[32,3072]{1,0:T(8,128)(2,...) custom-call(s32[3]{0:T(128)S(1)} %pad_add_fusion.3.info, ...), custom_call_target="tpu_custom_call", output_to_operand_aliasing={{4}: (12, {}), {5}: (13, {})} | custom-call | flops 1308622848 | bytes 9437184 | tf_op jit(solution)/shard_map/pallas_call | solution.py:110
  231.2 6.2 %collective-permute-done.59 = bf16[32,3072]{1,0:T(8,128)(2,1)S(1)} collective-permute-done((bf16[32,3072]{1,0:T(8,128)(2,1)S(1)}, bf16[32,3072]{1,0:T(8,128)(2,1)S(1)}, u32[]{:S(2)}, u32[]{:S(2)}) %collective-permute-start.59) | collective-permute-done | bytes 196640 | tf_op jit(solution)/shard_map/ppermute | solution.py:134
  237.5 3.6 %collective-permute-start.60 = (bf16[32,3072]{1,0:T(8,128)(2,1)S(1)}, bf16[32,3072]{1,0:T(8,128)(2,1)S(1)}, u32[]{:S(2)}, u32[]{:S(2)}) collective-permute-start(bf16[32,3072]{1,0:T(8,128)(2,1)S(1)} %add_convert_fusion.13), channel_id=1, source_target_pairs={{1,2},{2,1},{5,6},{6,5},{9,10},{10,9},{13,14},{14,13},{17,18},{18,... | collective-permute-start | bytes 589832 | tf_op jit(solution)/shard_map/ppermute | solution.py:134
  246.6 4.1 %collective-permute-start.67 = (bf16[32,3072]{1,0:T(8,128)(2,1)S(1)}, bf16[32,3072]{1,0:T(8,128)(2,1)S(1)}, u32[]{:S(2)}, u32[]{:S(2)}) collective-permute-start(bf16[32,3072]{1,0:T(8,128)(2,1)S(1)} %fusion.16.refs_0_), channel_id=1, source_target_pairs={{1,0},{2,3},{5,4},{6,7},{9,8},{10,11},{13,12},{14,15},{17,16},{18,... | collective-permute-start | bytes 589832 | tf_op jit(solution)/shard_map/ppermute | solution.py:134
  250.8 3.6 %collective-permute-start.66 = (bf16[32,3072]{1,0:T(8,128)(2,1)S(1)}, bf16[32,3072]{1,0:T(8,128)(2,1)S(1)}, u32[]{:S(2)}, u32[]{:S(2)}) collective-permute-start(bf16[32,3072]{1,0:T(8,128)(2,1)S(1)} %add_convert_fusion.7), channel_id=1, source_target_pairs={{1,2},{2,1},{5,6},{6,5},{9,10},{10,9},{13,14},{14,13},{17,18},{18,... | collective-permute-start | bytes 589832 | tf_op jit(solution)/shard_map/ppermute | solution.py:134
  268.0 5.3 %shard_map.88 = (bf16[32,3072]{1,0:T(8,128)(2,1)S(1)}, bf16[32,3072]{1,0:T(8,128)(2,1)S(1)}, bf16[32,3072]{1,0:T(8,128)(2,1)S(1)}, bf16[32,3072]{1,0:T(8,128)(2,...) custom-call(s32[3]{0:T(128)S(1)} %pad_add_fusion.6.info, ...), custom_call_target="tpu_custom_call", output_to_operand_aliasing={{4}: (12, {}), {5}: (13, {})} | custom-call | flops 1308622848 | bytes 9437184 | tf_op jit(solution)/shard_map/pallas_call | solution.py:110
  297.0 5.0 %collective-permute-done.78 = bf16[32,3072]{1,0:T(8,128)(2,1)S(1)} collective-permute-done((bf16[32,3072]{1,0:T(8,128)(2,1)S(1)}, bf16[32,3072]{1,0:T(8,128)(2,1)S(1)}, u32[]{:S(2)}, u32[]{:S(2)}) %collective-permute-start.78) | collective-permute-done | bytes 196640 | tf_op jit(solution)/shard_map/ppermute | solution.py:134
  (190 shorter events, 150.7 us)
Async XLA Ops:
  0.0 15.6 %collective-permute-start.2 = (bf16[32,3072]{1,0:T(8,128)(2,1)}, bf16[32,3072]{1,0:T(8,128)(2,1)S(1)}, u32[]{:S(2)}, u32[]{:S(2)}) collective-permute-start(bf16[32,3072]{1,0:T(8,128)(2,1)} %bitcast.20), channel_id=1, source_target_pairs={{0,1},{1,2},{2,3},{3,0},{4,5},{5,6},{6,7},{7,4},{8,9},{9,10},{10,1... | collective-permute-start | bytes 589832 | tf_op jit(solution)/shard_map/ppermute | solution.py:134
  1.6 17.1 %collective-permute-start.1 = (bf16[32,3072]{1,0:T(8,128)(2,1)}, bf16[32,3072]{1,0:T(8,128)(2,1)S(1)}, u32[]{:S(2)}, u32[]{:S(2)}) collective-permute-start(bf16[32,3072]{1,0:T(8,128)(2,1)} %bitcast.21), channel_id=1, source_target_pairs={{0,2},{1,3},{2,0},{3,1},{4,6},{5,7},{6,4},{7,5},{8,10},{9,11},{10,... | collective-permute-start | bytes 589832 | tf_op jit(solution)/shard_map/ppermute | solution.py:134
  2.8 17.6 %collective-permute-start = (bf16[32,3072]{1,0:T(8,128)(2,1)}, bf16[32,3072]{1,0:T(8,128)(2,1)S(1)}, u32[]{:S(2)}, u32[]{:S(2)}) collective-permute-start(bf16[32,3072]{1,0:T(8,128)(2,1)} %bitcast.22), channel_id=1, source_target_pairs={{0,3},{1,0},{2,1},{3,2},{4,7},{5,4},{6,5},{7,6},{8,11},{9,8},{10,9... | collective-permute-start | bytes 589832 | tf_op jit(solution)/shard_map/ppermute | solution.py:134
  25.8 9.7 %collective-permute-start.3 = (bf16[32,3072]{1,0:T(8,128)(2,1)S(1)}, bf16[32,3072]{1,0:T(8,128)(2,1)S(1)}, u32[]{:S(2)}, u32[]{:S(2)}) collective-permute-start(bf16[32,3072]{1,0:T(8,128)(2,1)S(1)} %get-tuple-element.75), channel_id=1, source_target_pairs={{0,1},{3,2},{4,5},{7,6},{8,9},{11,10},{12,13},{15,14},{16,17},{19,... | collective-permute-start | bytes 589832 | tf_op jit(solution)/shard_map/ppermute | solution.py:134
  27.1 11.6 %collective-permute-start.5 = (bf16[32,3072]{1,0:T(8,128)(2,1)S(1)}, bf16[32,3072]{1,0:T(8,128)(2,1)S(1)}, u32[]{:S(2)}, u32[]{:S(2)}) collective-permute-start(bf16[32,3072]{1,0:T(8,128)(2,1)S(1)} %get-tuple-element.76), channel_id=1, source_target_pairs={{0,1},{3,2},{4,5},{7,6},{8,9},{11,10},{12,13},{15,14},{16,17},{19,... | collective-permute-start | bytes 589832 | tf_op jit(solution)/shard_map/ppermute | solution.py:134
  37.5 11.3 %collective-permute-start.7 = (bf16[32,3072]{1,0:T(8,128)(2,1)S(1)}, bf16[32,3072]{1,0:T(8,128)(2,1)S(1)}, u32[]{:S(2)}, u32[]{:S(2)}) collective-permute-start(bf16[32,3072]{1,0:T(8,128)(2,1)S(1)} %get-tuple-element.78), channel_id=1, source_target_pairs={{0,1},{3,2},{4,5},{7,6},{8,9},{11,10},{12,13},{15,14},{16,17},{19,... | collective-permute-start | bytes 589832 | tf_op jit(solution)/shard_map/ppermute | solution.py:134
  38.9 11.9 %collective-permute-start.6 = (bf16[32,3072]{1,0:T(8,128)(2,1)S(1)}, bf16[32,3072]{1,0:T(8,128)(2,1)S(1)}, u32[]{:S(2)}, u32[]{:S(2)}) collective-permute-start(bf16[32,3072]{1,0:T(8,128)(2,1)S(1)} %add_convert_fusion.43), channel_id=1, source_target_pairs={{1,2},{2,1},{5,6},{6,5},{9,10},{10,9},{13,14},{14,13},{17,18},{18,... | collective-permute-start | bytes 589832 | tf_op jit(solution)/shard_map/ppermute | solution.py:134
  44.2 17.9 %collective-permute-start.11 = (bf16[32,3072]{1,0:T(8,128)(2,1)S(1)}, bf16[32,3072]{1,0:T(8,128)(2,1)S(1)}, u32[]{:S(2)}, u32[]{:S(2)}) collective-permute-start(bf16[32,3072]{1,0:T(8,128)(2,1)S(1)} %fusion.refs_0_), channel_id=1, source_target_pairs={{1,0},{2,3},{5,4},{6,7},{9,8},{10,11},{13,12},{14,15},{17,16},{18,... | collective-permute-start | bytes 589832 | tf_op jit(solution)/shard_map/ppermute | solution.py:134
  50.9 11.2 %collective-permute-start.12 = (bf16[32,3072]{1,0:T(8,128)(2,1)S(1)}, bf16[32,3072]{1,0:T(8,128)(2,1)S(1)}, u32[]{:S(2)}, u32[]{:S(2)}) collective-permute-start(bf16[32,3072]{1,0:T(8,128)(2,1)S(1)} %fusion.1.refs_1_), channel_id=1, source_target_pairs={{1,0},{2,3},{5,4},{6,7},{9,8},{10,11},{13,12},{14,15},{17,16},{18,... | collective-permute-start | bytes 589832 | tf_op jit(solution)/shard_map/ppermute | solution.py:134
  73.5 11.0 %collective-permute-start.17 = (bf16[32,3072]{1,0:T(8,128)(2,1)S(1)}, bf16[32,3072]{1,0:T(8,128)(2,1)S(1)}, u32[]{:S(2)}, u32[]{:S(2)}) collective-permute-start(bf16[32,3072]{1,0:T(8,128)(2,1)S(1)} %get-tuple-element.86), channel_id=1, source_target_pairs={{0,1},{3,2},{4,5},{7,6},{8,9},{11,10},{12,13},{15,14},{16,17},{19,... | collective-permute-start | bytes 589832 | tf_op jit(solution)/shard_map/ppermute | solution.py:134
  84.5 9.9 %collective-permute-start.18 = (bf16[32,3072]{1,0:T(8,128)(2,1)S(1)}, bf16[32,3072]{1,0:T(8,128)(2,1)S(1)}, u32[]{:S(2)}, u32[]{:S(2)}) collective-permute-start(bf16[32,3072]{1,0:T(8,128)(2,1)S(1)} %add_convert_fusion.35), channel_id=1, source_target_pairs={{1,2},{2,1},{5,6},{6,5},{9,10},{10,9},{13,14},{14,13},{17,18},{18,... | collective-permute-start | bytes 589832 | tf_op jit(solution)/shard_map/ppermute | solution.py:134
  89.5 24.2 %collective-permute-start.29 = (bf16[32,3072]{1,0:T(8,128)(2,1)S(1)}, bf16[32,3072]{1,0:T(8,128)(2,1)S(1)}, u32[]{:S(2)}, u32[]{:S(2)}) collective-permute-start(bf16[32,3072]{1,0:T(8,128)(2,1)S(1)} %fusion.4), channel_id=1, source_target_pairs={{1,4},{2,7},{5,8},{6,11},{9,12},{10,15},{13,16},{14,19},{17,20},{1... | collective-permute-start | bytes 589832 | tf_op jit(solution)/shard_map/ppermute | solution.py:134
  90.9 12.2 %collective-permute-start.21 = (bf16[32,3072]{1,0:T(8,128)(2,1)S(1)}, bf16[32,3072]{1,0:T(8,128)(2,1)S(1)}, u32[]{:S(2)}, u32[]{:S(2)}) collective-permute-start(bf16[32,3072]{1,0:T(8,128)(2,1)S(1)} %add_convert_fusion.33), channel_id=1, source_target_pairs={{1,2},{2,1},{5,6},{6,5},{9,10},{10,9},{13,14},{14,13},{17,18},{18,... | collective-permute-start | bytes 589832 | tf_op jit(solution)/shard_map/ppermute | solution.py:134
  94.5 15.9 %collective-permute-start.23 = (bf16[32,3072]{1,0:T(8,128)(2,1)S(1)}, bf16[32,3072]{1,0:T(8,128)(2,1)S(1)}, u32[]{:S(2)}, u32[]{:S(2)}) collective-permute-start(bf16[32,3072]{1,0:T(8,128)(2,1)S(1)} %fusion.5), channel_id=1, source_target_pairs={{1,4},{2,7},{5,8},{6,11},{9,12},{10,15},{13,16},{14,19},{17,20},{1... | collective-permute-start | bytes 589832 | tf_op jit(solution)/shard_map/ppermute | solution.py:134
  95.8 20.5 %collective-permute-start.19 = (bf16[32,3072]{1,0:T(8,128)(2,1)S(1)}, bf16[32,3072]{1,0:T(8,128)(2,1)S(1)}, u32[]{:S(2)}, u32[]{:S(2)}) collective-permute-start(bf16[32,3072]{1,0:T(8,128)(2,1)S(1)} %fusion.4), channel_id=1, source_target_pairs={{1,5},{2,6},{5,9},{6,10},{9,13},{10,14},{13,17},{14,18},{17,21},{1... | collective-permute-start | bytes 589832 | tf_op jit(solution)/shard_map/ppermute | solution.py:134
  127.4 13.2 %collective-permute-start.33 = (bf16[32,3072]{1,0:T(8,128)(2,1)S(1)}, bf16[32,3072]{1,0:T(8,128)(2,1)S(1)}, u32[]{:S(2)}, u32[]{:S(2)}) collective-permute-start(bf16[32,3072]{1,0:T(8,128)(2,1)S(1)} %get-tuple-element.100), channel_id=1, source_target_pairs={{0,1},{3,2},{4,5},{7,6},{8,9},{11,10},{12,13},{15,14},{16,17},{19,... | collective-permute-start | bytes 589832 | tf_op jit(solution)/shard_map/ppermute | solution.py:134
  139.3 9.9 %collective-permute-start.35 = (bf16[32,3072]{1,0:T(8,128)(2,1)S(1)}, bf16[32,3072]{1,0:T(8,128)(2,1)S(1)}, u32[]{:S(2)}, u32[]{:S(2)}) collective-permute-start(bf16[32,3072]{1,0:T(8,128)(2,1)S(1)} %get-tuple-element.102), channel_id=1, source_target_pairs={{0,1},{3,2},{4,5},{7,6},{8,9},{11,10},{12,13},{15,14},{16,17},{19,... | collective-permute-start | bytes 589832 | tf_op jit(solution)/shard_map/ppermute | solution.py:134
  140.7 11.9 %collective-permute-start.34 = (bf16[32,3072]{1,0:T(8,128)(2,1)S(1)}, bf16[32,3072]{1,0:T(8,128)(2,1)S(1)}, u32[]{:S(2)}, u32[]{:S(2)}) collective-permute-start(bf16[32,3072]{1,0:T(8,128)(2,1)S(1)} %add_convert_fusion.27), channel_id=1, source_target_pairs={{1,2},{2,1},{5,6},{6,5},{9,10},{10,9},{13,14},{14,13},{17,18},{18,... | collective-permute-start | bytes 589832 | tf_op jit(solution)/shard_map/ppermute | solution.py:134
  143.3 10.7 %collective-permute-start.37 = (bf16[32,3072]{1,0:T(8,128)(2,1)S(1)}, bf16[32,3072]{1,0:T(8,128)(2,1)S(1)}, u32[]{:S(2)}, u32[]{:S(2)}) collective-permute-start(bf16[32,3072]{1,0:T(8,128)(2,1)S(1)} %get-tuple-element.105), channel_id=1, source_target_pairs={{0,1},{3,2},{4,5},{7,6},{8,9},{11,10},{12,13},{15,14},{16,17},{19,... | collective-permute-start | bytes 589832 | tf_op jit(solution)/shard_map/ppermute | solution.py:134
  144.7 18.5 %collective-permute-start.39 = (bf16[32,3072]{1,0:T(8,128)(2,1)S(1)}, bf16[32,3072]{1,0:T(8,128)(2,1)S(1)}, u32[]{:S(2)}, u32[]{:S(2)}) collective-permute-start(bf16[32,3072]{1,0:T(8,128)(2,1)S(1)} %fusion.8.refs_0_), channel_id=1, source_target_pairs={{1,0},{2,3},{5,4},{6,7},{9,8},{10,11},{13,12},{14,15},{17,16},{18,... | collective-permute-start | bytes 589832 | tf_op jit(solution)/shard_map/ppermute | solution.py:134
  152.7 10.4 %collective-permute-start.40 = (bf16[32,3072]{1,0:T(8,128)(2,1)S(1)}, bf16[32,3072]{1,0:T(8,128)(2,1)S(1)}, u32[]{:S(2)}, u32[]{:S(2)}) collective-permute-start(bf16[32,3072]{1,0:T(8,128)(2,1)S(1)} %fusion.9.refs_1_), channel_id=1, source_target_pairs={{1,0},{2,3},{5,4},{6,7},{9,8},{10,11},{13,12},{14,15},{17,16},{18,... | collective-permute-start | bytes 589832 | tf_op jit(solution)/shard_map/ppermute | solution.py:134
  172.8 11.5 %collective-permute-start.45 = (bf16[32,3072]{1,0:T(8,128)(2,1)S(1)}, bf16[32,3072]{1,0:T(8,128)(2,1)S(1)}, u32[]{:S(2)}, u32[]{:S(2)}) collective-permute-start(bf16[32,3072]{1,0:T(8,128)(2,1)S(1)} %get-tuple-element.110), channel_id=1, source_target_pairs={{0,1},{3,2},{4,5},{7,6},{8,9},{11,10},{12,13},{15,14},{16,17},{19,... | collective-permute-start | bytes 589832 | tf_op jit(solution)/shard_map/ppermute | solution.py:134
  188.2 27.9 %collective-permute-start.57 = (bf16[32,3072]{1,0:T(8,128)(2,1)S(1)}, bf16[32,3072]{1,0:T(8,128)(2,1)S(1)}, u32[]{:S(2)}, u32[]{:S(2)}) collective-permute-start(bf16[32,3072]{1,0:T(8,128)(2,1)S(1)} %fusion.12), channel_id=1, source_target_pairs={{1,4},{2,7},{5,8},{6,11},{9,12},{10,15},{13,16},{14,19},{17,20},{1... | collective-permute-start | bytes 589832 | tf_op jit(solution)/shard_map/ppermute | solution.py:134
  190.6 15.2 %collective-permute-start.49 = (bf16[32,3072]{1,0:T(8,128)(2,1)S(1)}, bf16[32,3072]{1,0:T(8,128)(2,1)S(1)}, u32[]{:S(2)}, u32[]{:S(2)}) collective-permute-start(bf16[32,3072]{1,0:T(8,128)(2,1)S(1)} %add_convert_fusion.17), channel_id=1, source_target_pairs={{1,2},{2,1},{5,6},{6,5},{9,10},{10,9},{13,14},{14,13},{17,18},{18,... | collective-permute-start | bytes 589832 | tf_op jit(solution)/shard_map/ppermute | solution.py:134
  193.1 19.8 %collective-permute-start.51 = (bf16[32,3072]{1,0:T(8,128)(2,1)S(1)}, bf16[32,3072]{1,0:T(8,128)(2,1)S(1)}, u32[]{:S(2)}, u32[]{:S(2)}) collective-permute-start(bf16[32,3072]{1,0:T(8,128)(2,1)S(1)} %fusion.13), channel_id=1, source_target_pairs={{1,4},{2,7},{5,8},{6,11},{9,12},{10,15},{13,16},{14,19},{17,20},{1... | collective-permute-start | bytes 589832 | tf_op jit(solution)/shard_map/ppermute | solution.py:134
  194.5 24.5 %collective-permute-start.47 = (bf16[32,3072]{1,0:T(8,128)(2,1)S(1)}, bf16[32,3072]{1,0:T(8,128)(2,1)S(1)}, u32[]{:S(2)}, u32[]{:S(2)}) collective-permute-start(bf16[32,3072]{1,0:T(8,128)(2,1)S(1)} %fusion.12), channel_id=1, source_target_pairs={{1,5},{2,6},{5,9},{6,10},{9,13},{10,14},{13,17},{14,18},{17,21},{1... | collective-permute-start | bytes 589832 | tf_op jit(solution)/shard_map/ppermute | solution.py:134
  229.9 12.6 %collective-permute-start.61 = (bf16[32,3072]{1,0:T(8,128)(2,1)S(1)}, bf16[32,3072]{1,0:T(8,128)(2,1)S(1)}, u32[]{:S(2)}, u32[]{:S(2)}) collective-permute-start(bf16[32,3072]{1,0:T(8,128)(2,1)S(1)} %get-tuple-element.125), channel_id=1, source_target_pairs={{0,1},{3,2},{4,5},{7,6},{8,9},{11,10},{12,13},{15,14},{16,17},{19,... | collective-permute-start | bytes 589832 | tf_op jit(solution)/shard_map/ppermute | solution.py:134
  242.5 11.9 %collective-permute-start.63 = (bf16[32,3072]{1,0:T(8,128)(2,1)S(1)}, bf16[32,3072]{1,0:T(8,128)(2,1)S(1)}, u32[]{:S(2)}, u32[]{:S(2)}) collective-permute-start(bf16[32,3072]{1,0:T(8,128)(2,1)S(1)} %add_convert_fusion.11), channel_id=1, source_target_pairs={{1,2},{2,1},{5,6},{6,5},{9,10},{10,9},{13,14},{14,13},{17,18},{18,... | collective-permute-start | bytes 589832 | tf_op jit(solution)/shard_map/ppermute | solution.py:134
  244.7 11.1 %collective-permute-start.62 = (bf16[32,3072]{1,0:T(8,128)(2,1)S(1)}, bf16[32,3072]{1,0:T(8,128)(2,1)S(1)}, u32[]{:S(2)}, u32[]{:S(2)}) collective-permute-start(bf16[32,3072]{1,0:T(8,128)(2,1)S(1)} %get-tuple-element.126), channel_id=1, source_target_pairs={{0,1},{3,2},{4,5},{7,6},{8,9},{11,10},{12,13},{15,14},{16,17},{19,... | collective-permute-start | bytes 589832 | tf_op jit(solution)/shard_map/ppermute | solution.py:134
  246.6 18.3 %collective-permute-start.67 = (bf16[32,3072]{1,0:T(8,128)(2,1)S(1)}, bf16[32,3072]{1,0:T(8,128)(2,1)S(1)}, u32[]{:S(2)}, u32[]{:S(2)}) collective-permute-start(bf16[32,3072]{1,0:T(8,128)(2,1)S(1)} %fusion.16.refs_0_), channel_id=1, source_target_pairs={{1,0},{2,3},{5,4},{6,7},{9,8},{10,11},{13,12},{14,15},{17,16},{18,... | collective-permute-start | bytes 589832 | tf_op jit(solution)/shard_map/ppermute | solution.py:134
  254.5 10.4 %collective-permute-start.68 = (bf16[32,3072]{1,0:T(8,128)(2,1)S(1)}, bf16[32,3072]{1,0:T(8,128)(2,1)S(1)}, u32[]{:S(2)}, u32[]{:S(2)}) collective-permute-start(bf16[32,3072]{1,0:T(8,128)(2,1)S(1)} %fusion.17.refs_1_), channel_id=1, source_target_pairs={{1,0},{2,3},{5,4},{6,7},{9,8},{10,11},{13,12},{14,15},{17,16},{18,... | collective-permute-start | bytes 589832 | tf_op jit(solution)/shard_map/ppermute | solution.py:134
  277.2 10.0 %collective-permute-start.76 = (bf16[32,3072]{1,0:T(8,128)(2,1)S(1)}, bf16[32,3072]{1,0:T(8,128)(2,1)S(1)}, u32[]{:S(2)}, u32[]{:S(2)}) collective-permute-start(bf16[32,3072]{1,0:T(8,128)(2,1)S(1)} %get-tuple-element.136), channel_id=1, source_target_pairs={{0,1},{3,2},{4,5},{7,6},{8,9},{11,10},{12,13},{15,14},{16,17},{19,... | collective-permute-start | bytes 589832 | tf_op jit(solution)/shard_map/ppermute | solution.py:134
  (49 other events, 404.5 us)

commit v3 on v2

v3 whole, which is shorter than its diff:
```python
import functools

import jax
import jax.numpy as jnp
from jax import lax
from jax.experimental import pallas as pl
from jax.experimental.pallas import tpu as pltpu
from jax.sharding import PartitionSpec as P

HD = 128
TICKS = 3
PASSES = 2
VMEM_LIMIT = 24 * 2**20


def block_kernel(chunks, info, *refs):
    blocks = refs[:chunks]
    gain, w, wo, _, _ = refs[chunks:chunks + 5]
    terms = refs[chunks + 5:2 * chunks + 5]
    kc, vc, normed, attended = refs[2 * chunks + 5:]
    rows = blocks[0].shape[0]
    total_rows = rows * chunks
    heads = kc.shape[1] // HD

    @pl.when(info[1] > 0)
    def _():
        gain_row = gain[...].astype(jnp.float32)
        for c in range(chunks):
            wide = blocks[c][...].astype(jnp.float32)
            mean_square = jnp.mean(wide * wide, axis=-1, keepdims=True)
            normed[pl.ds(c * rows, rows), :] = (
                wide * lax.rsqrt(mean_square + 1e-06) * gain_row
            ).astype(jnp.bfloat16)
        query, key, value = [
            jnp.dot(normed[...], w[part], preferred_element_type=jnp.float32).astype(jnp.bfloat16)
            for part in range(3)
        ]
        start = pl.multiple_of(info[0], total_rows)
        kc[pl.ds(start, total_rows), :] = key
        vc[pl.ds(start, total_rows), :] = value
        for h in range(heads):
            cols = pl.ds(h * HD, HD)
            scores = lax.dot_general(
                query[:, h * HD:(h + 1) * HD],
                kc[:, cols],
                (((1,), (1,)), ((), ())),
                preferred_element_type=jnp.float32,
            ) * HD ** (-0.5)
            top = jnp.max(scores, axis=-1, keepdims=True)
            weights = jnp.exp(scores - top)
            probs = (weights / jnp.sum(weights, axis=-1, keepdims=True)).astype(jnp.bfloat16)
            attended[:, cols] = jnp.dot(
                probs, vc[:, cols], preferred_element_type=jnp.float32
            ).astype(jnp.bfloat16)
        for c in range(chunks):
            terms[c][...] = jnp.dot(
                attended[pl.ds(c * rows, rows), :], wo[...], preferred_element_type=jnp.float32
            ).astype(jnp.bfloat16)


def load_kernel(*refs):
    count = len(refs) // 2
    sems = refs[-1]
    pairs = list(zip(refs[:count], refs[count:2 * count]))
    copies = [pltpu.make_async_copy(a, b, sems.at[i]) for i, (a, b) in enumerate(pairs)]
    for copy in copies:
        copy.start()
    for copy in copies:
        copy.wait()


def loaded(*arrays):
    return pl.pallas_call(
        load_kernel,
        out_shape=[pltpu.VMEM(a.shape, a.dtype) for a in arrays],
        in_specs=[pl.BlockSpec(memory_space=pl.ANY)] * len(arrays),
        out_specs=[pl.BlockSpec(memory_space=pltpu.VMEM)] * len(arrays),
        scratch_shapes=[pltpu.SemaphoreType.DMA((len(arrays),))],
        compiler_params=pltpu.CompilerParams(vmem_limit_bytes=VMEM_LIMIT),
        cost_estimate=pl.CostEstimate(
            flops=0, bytes_accessed=2 * sum(a.size for a in arrays), transcendentals=0
        ),
    )(*[pltpu.with_memory_space_constraint(a, pltpu.HBM) for a in arrays])


def block_terms(info, blocks, gain, w, wo, kc, vc):
    chunks = len(blocks)
    rows, width = blocks[0].shape
    vmem = pl.BlockSpec(memory_space=pltpu.VMEM)
    row_count = rows * chunks
    flops = 2 * row_count * (w.size + wo.size + 2 * kc.size)
    held = [pltpu.with_memory_space_constraint(x, pltpu.VMEM) for x in (w, wo, kc, vc)]
    cache = pltpu.VMEM(kc.shape, kc.dtype)
    out = pl.pallas_call(
        functools.partial(block_kernel, chunks),
        out_shape=[jax.ShapeDtypeStruct((rows, width), jnp.bfloat16)] * chunks + [cache] * 2,
        in_specs=[pl.BlockSpec(memory_space=pltpu.SMEM)] + [vmem] * (chunks + 5),
        out_specs=[vmem] * (chunks + 2),
        input_output_aliases={chunks + 4: chunks, chunks + 5: chunks + 1},
        scratch_shapes=[
            pltpu.VMEM((row_count, width), jnp.bfloat16),
            pltpu.VMEM((row_count, kc.shape[1]), jnp.bfloat16),
        ],
        compiler_params=pltpu.CompilerParams(vmem_limit_bytes=VMEM_LIMIT),
        cost_estimate=pl.CostEstimate(
            flops=flops, bytes_accessed=2 * (w.size + wo.size), transcendentals=0
        ),
    )(info, *blocks, gain, *held)
    return out[:chunks], out[chunks], out[chunks + 1]


def send(block, turn, hop):
    sections = lax.axis_size("section")
    n = lax.axis_size("uly")
    route = [
        (s * n + i, (s + hop) % sections * n + (i + turn) % n)
        for s in range(sections)
        for i in range(n)
    ]
    return lax.ppermute(block, ("section", "uly"), route)


def gathered(own, hop):
    n = lax.axis_size("uly")
    first = own if hop == 0 else send(own, 0, hop)
    return [first] + [send(own, k, hop) for k in range(1, n)]


def summed(blocks):
    total = blocks[0].astype(jnp.float32)
    for block in blocks[1:]:
        total = total + block.astype(jnp.float32)
    return total


def shards(
    state, patch_slot, section_active, qkv_weight, out_weight, norm_gain, stale_keys, stale_values
):
    section_count = lax.axis_size("section")
    section_index = lax.axis_index("section")
    w = jnp.transpose(qkv_weight[0], (1, 0, 2))
    wo = out_weight[0]
    w, wo, kc, vc = loaded(w, wo, stale_keys[0], stale_values[0])
    block_count = section_active[0]
    n = lax.axis_size("uly")
    patch_rows = state.shape[1] * n
    own = state[0]
    blocks = gathered(own, 0)
    for tick in range(TICKS):
        slot = patch_slot[(section_index - tick) % section_count]
        for index in range(PASSES):
            applies = block_count > index
            info = jnp.stack([slot * patch_rows, applies.astype(jnp.int32)])
            terms, kc, vc = block_terms(info, blocks, norm_gain, w, wo, kc, vc)
            arrived = [send(terms[k], n - k, 0) for k in range(1, n)]
            updated = own.astype(jnp.float32) + summed([terms[0]] + arrived)
            updated = jnp.where(applies, updated.astype(jnp.bfloat16), own)
            last = index == PASSES - 1
            if last and tick == TICKS - 1:
                return send(updated, 0, 1)[None]
            blocks = gathered(updated, 1 if last else 0)
            own = blocks[0]


def solution(mesh):
    return jax.shard_map(
        shards,
        mesh=mesh,
        in_specs=(
            P("section", "uly", None),
            P(),
            P("section"),
            P("section", None, None, "uly"),
            P("section", "uly", None),
            P("section", None),
            P("section", None, "uly"),
            P("section", None, "uly"),
        ),
        out_specs=P("section", "uly", None),
        check_vma=False,
    )
```

time: 305 us -> 261 us (0.86)
  the two profiles are of different devices: /device:TPU:14 before, /device:TPU:0 now
where the time goes in v3:
time: 261 us; the launch traced here: 257 us
  waiting for transfers between devices  176 us (67%)
  starting transfers between devices  54.1 us (21%)
  Pallas kernels  20.5 us (8%)
  between operations  2.78 us (1%)
    ppermute x39, waiting for transfers between devices, send(): return lax.ppermute(block, ('section', 'uly'), route)  176 us
    ppermute x39, starting transfers between devices, send(): return lax.ppermute(block, ('section', 'uly'), route)  54.1 us
    pallas_call x6, Pallas kernels, block_terms(): pl.pallas_call(functools.partial(block_kernel, chunks), out_shape=[jax.Sh...  16.6 us
  transfers between devices with their start and end apart: 39, of which 24 were waited for; matrix products, arithmetic and copies ran while one was open for 1% of the time, Pallas kernels for 2%

profile of v3, /device:TPU:0, one launch (start us, length us, event | category | flops | bytes accessed | tf_op | source)
XLA Modules:
  0.0 256.7 jit_solution(10686399008946571966)
XLA Ops:
  0.0 5.0 %collective-permute-start.2 = (bf16[32,3072]{1,0:T(8,128)(2,1)}, bf16[32,3072]{1,0:T(8,128)(2,1)S(1)}, u32[]{:S(2)}, u32[]{:S(2)}) collective-permute-start(bf16[32,3072]{1,0:T(8,128)(2,1)} %bitcast.11), channel_id=1, source_target_pairs={{0,3},{1,0},{2,1},{3,2},{4,7},{5,4},{6,5},{7,6},{8,11},{9,8},{10,9... | collective-permute-start | bytes 589832 | tf_op jit(solution)/shard_map/ppermute | solution.py:120
  8.8 3.9 %shard_map.82 = (bf16[3,3072,384]{2,1,0:T(8,128)(2,1)S(1)}, bf16[384,3072]{1,0:T(8,128)(2,1)S(1)}, bf16[512,384]{1,0:T(8,128)(2,1)S(1)}, bf16[512,384]{1,0:T(8,128)(2,1)S(1)}) custom-call(bf16[3,3072,384]{2,1,0:T(8,128)(2,1)} %bitcast.15, bf16[384,3072]{1,0:T(8,128)(2,1)} %bitcast.16, bf16[512,384]{1,0:T(8,128)(2,1)} %bitcast.17, bf16[512,384]{1,0:T(8,128)(2,1)} %bitcast.18), custom_call_target="tpu_custom_call" | custom-call | bytes 10223616 | tf_op jit(solution)/shard_map/pallas_call | solution.py:73
  12.8 9.2 %collective-permute-done.1.refs_2_ = bf16[32,3072]{1,0:T(8,128)(2,1)S(1)} collective-permute-done((bf16[32,3072]{1,0:T(8,128)(2,1)}, bf16[32,3072]{1,0:T(8,128)(2,1)S(1)}, u32[]{:S(2)}, u32[]{:S(2)}) %collective-permute-start.1) | collective-permute-done | bytes 196640 | tf_op jit(solution)/shard_map/ppermute | solution.py:120
  22.0 4.9 %shard_map.83 = (bf16[32,3072]{1,0:T(8,128)(2,1)S(1)}, bf16[32,3072]{1,0:T(8,128)(2,1)S(1)}, bf16[32,3072]{1,0:T(8,128)(2,1)S(1)}, bf16[32,3072]{1,0:T(8,128)(2,...) custom-call(s32[2]{0:T(128)S(1)} %pad_add_fusion.1.info, ...), custom_call_target="tpu_custom_call", output_to_operand_aliasing={{4}: (8, {}), {5}: (9, {})} | custom-call | flops 1308622848 | bytes 9437184 | tf_op jit(solution)/shard_map/pallas_call | solution.py:94
  27.3 2.5 collective-permute-start.4
  33.3 13.4 %collective-permute-done.4 = bf16[32,3072]{1,0:T(8,128)(2,1)S(1)} collective-permute-done((bf16[32,3072]{1,0:T(8,128)(2,1)S(1)}, bf16[32,3072]{1,0:T(8,128)(2,1)S(1)}, u32[]{:S(2)}, u32[]{:S(2)}) %collective-permute-start.4) | collective-permute-done | bytes 196640 | tf_op jit(solution)/shard_map/ppermute | solution.py:120
  49.0 4.3 %collective-permute-done.8.refs_3_ = bf16[32,3072]{1,0:T(8,128)(2,1)S(1)} collective-permute-done((bf16[32,3072]{1,0:T(8,128)(2,1)S(1)}, bf16[32,3072]{1,0:T(8,128)(2,1)S(1)}, u32[]{:S(2)}, u32[]{:S(2)}) %collective-permute-start.8) | collective-permute-done | bytes 196640 | tf_op jit(solution)/shard_map/ppermute | solution.py:120
  53.3 11.4 %collective-permute-done.7.refs_2_ = bf16[32,3072]{1,0:T(8,128)(2,1)S(1)} collective-permute-done((bf16[32,3072]{1,0:T(8,128)(2,1)S(1)}, bf16[32,3072]{1,0:T(8,128)(2,1)S(1)}, u32[]{:S(2)}, u32[]{:S(2)}) %collective-permute-start.7) | collective-permute-done | bytes 196640 | tf_op jit(solution)/shard_map/ppermute | solution.py:120
  68.7 4.1 %collective-permute-done.9 = bf16[32,3072]{1,0:T(8,128)(2,1)S(1)} collective-permute-done((bf16[32,3072]{1,0:T(8,128)(2,1)S(1)}, bf16[32,3072]{1,0:T(8,128)(2,1)S(1)}, u32[]{:S(2)}, u32[]{:S(2)}) %collective-permute-start.9) | collective-permute-done | bytes 196640 | tf_op jit(solution)/shard_map/ppermute | solution.py:120
  72.9 2.6 %collective-permute-done.10 = bf16[32,3072]{1,0:T(8,128)(2,1)S(1)} collective-permute-done((bf16[32,3072]{1,0:T(8,128)(2,1)S(1)}, bf16[32,3072]{1,0:T(8,128)(2,1)S(1)}, u32[]{:S(2)}, u32[]{:S(2)}) %collective-permute-start.10) | collective-permute-done | bytes 196640 | tf_op jit(solution)/shard_map/ppermute | solution.py:120
  75.5 3.5 %collective-permute-done.11 = bf16[32,3072]{1,0:T(8,128)(2,1)S(1)} collective-permute-done((bf16[32,3072]{1,0:T(8,128)(2,1)S(1)}, bf16[32,3072]{1,0:T(8,128)(2,1)S(1)}, u32[]{:S(2)}, u32[]{:S(2)}) %collective-permute-start.11) | collective-permute-done | bytes 196640 | tf_op jit(solution)/shard_map/ppermute | solution.py:120
  79.2 4.2 %collective-permute-start.15 = (bf16[32,3072]{1,0:T(8,128)(2,1)S(1)}, bf16[32,3072]{1,0:T(8,128)(2,1)S(1)}, u32[]{:S(2)}, u32[]{:S(2)}) collective-permute-start(bf16[32,3072]{1,0:T(8,128)(2,1)S(1)} %fusion.1), channel_id=1, source_target_pairs={{0,7},{1,4},{2,5},{3,6},{4,11},{5,8},{6,9},{7,10},{8,15},{9,12},{1... | collective-permute-start | bytes 589832 | tf_op jit(solution)/shard_map/ppermute | solution.py:120
  83.3 3.2 %collective-permute-start.14 = (bf16[32,3072]{1,0:T(8,128)(2,1)S(1)}, bf16[32,3072]{1,0:T(8,128)(2,1)S(1)}, u32[]{:S(2)}, u32[]{:S(2)}) collective-permute-start(bf16[32,3072]{1,0:T(8,128)(2,1)S(1)} %fusion.1), channel_id=1, source_target_pairs={{0,6},{1,7},{2,4},{3,5},{4,10},{5,11},{6,8},{7,9},{8,14},{9,15},{1... | collective-permute-start | bytes 589832 | tf_op jit(solution)/shard_map/ppermute | solution.py:120
  90.0 15.8 %collective-permute-done.14.refs_2_ = bf16[32,3072]{1,0:T(8,128)(2,1)S(1)} collective-permute-done((bf16[32,3072]{1,0:T(8,128)(2,1)S(1)}, bf16[32,3072]{1,0:T(8,128)(2,1)S(1)}, u32[]{:S(2)}, u32[]{:S(2)}) %collective-permute-start.14) | collective-permute-done | bytes 196640 | tf_op jit(solution)/shard_map/ppermute | solution.py:120
  105.9 5.1 %shard_map.85 = (bf16[32,3072]{1,0:T(8,128)(2,1)S(1)}, bf16[32,3072]{1,0:T(8,128)(2,1)S(1)}, bf16[32,3072]{1,0:T(8,128)(2,1)S(1)}, bf16[32,3072]{1,0:T(8,128)(2,...) custom-call(s32[2]{0:T(128)S(1)} %pad_add_fusion.3.info, ...), custom_call_target="tpu_custom_call", output_to_operand_aliasing={{4}: (8, {}), {5}: (9, {})} | custom-call | flops 1308622848 | bytes 9437184 | tf_op jit(solution)/shard_map/pallas_call | solution.py:94
  113.8 4.2 %collective-permute-done.16 = bf16[32,3072]{1,0:T(8,128)(2,1)S(1)} collective-permute-done((bf16[32,3072]{1,0:T(8,128)(2,1)S(1)}, bf16[32,3072]{1,0:T(8,128)(2,1)S(1)}, u32[]{:S(2)}, u32[]{:S(2)}) %collective-permute-start.16) | collective-permute-done | bytes 196640 | tf_op jit(solution)/shard_map/ppermute | solution.py:120
  118.1 10.0 %collective-permute-done.17 = bf16[32,3072]{1,0:T(8,128)(2,1)S(1)} collective-permute-done((bf16[32,3072]{1,0:T(8,128)(2,1)S(1)}, bf16[32,3072]{1,0:T(8,128)(2,1)S(1)}, u32[]{:S(2)}, u32[]{:S(2)}) %collective-permute-start.17) | collective-permute-done | bytes 196640 | tf_op jit(solution)/shard_map/ppermute | solution.py:120
  128.3 2.5 collective-permute-start.20
  133.9 14.5 %collective-permute-done.20.refs_2_ = bf16[32,3072]{1,0:T(8,128)(2,1)S(1)} collective-permute-done((bf16[32,3072]{1,0:T(8,128)(2,1)S(1)}, bf16[32,3072]{1,0:T(8,128)(2,1)S(1)}, u32[]{:S(2)}, u32[]{:S(2)}) %collective-permute-start.20) | collective-permute-done | bytes 196640 | tf_op jit(solution)/shard_map/ppermute | solution.py:120
  151.1 4.5 %collective-permute-done.22 = bf16[32,3072]{1,0:T(8,128)(2,1)S(1)} collective-permute-done((bf16[32,3072]{1,0:T(8,128)(2,1)S(1)}, bf16[32,3072]{1,0:T(8,128)(2,1)S(1)}, u32[]{:S(2)}, u32[]{:S(2)}) %collective-permute-start.22) | collective-permute-done | bytes 196640 | tf_op jit(solution)/shard_map/ppermute | solution.py:120
  155.5 10.7 %collective-permute-done.23 = bf16[32,3072]{1,0:T(8,128)(2,1)S(1)} collective-permute-done((bf16[32,3072]{1,0:T(8,128)(2,1)S(1)}, bf16[32,3072]{1,0:T(8,128)(2,1)S(1)}, u32[]{:S(2)}, u32[]{:S(2)}) %collective-permute-start.23) | collective-permute-done | bytes 196640 | tf_op jit(solution)/shard_map/ppermute | solution.py:120
  167.0 3.3 %collective-permute-start.27 = (bf16[32,3072]{1,0:T(8,128)(2,1)S(1)}, bf16[32,3072]{1,0:T(8,128)(2,1)S(1)}, u32[]{:S(2)}, u32[]{:S(2)}) collective-permute-start(bf16[32,3072]{1,0:T(8,128)(2,1)S(1)} %fusion.3), channel_id=1, source_target_pairs={{0,6},{1,7},{2,4},{3,5},{4,10},{5,11},{6,8},{7,9},{8,14},{9,15},{1... | collective-permute-start | bytes 589832 | tf_op jit(solution)/shard_map/ppermute | solution.py:120
  173.1 2.4 collective-permute-done.28.refs_3_
  175.5 13.4 %collective-permute-done.27.refs_2_ = bf16[32,3072]{1,0:T(8,128)(2,1)S(1)} collective-permute-done((bf16[32,3072]{1,0:T(8,128)(2,1)S(1)}, bf16[32,3072]{1,0:T(8,128)(2,1)S(1)}, u32[]{:S(2)}, u32[]{:S(2)}) %collective-permute-start.27) | collective-permute-done | bytes 196640 | tf_op jit(solution)/shard_map/ppermute | solution.py:120
  188.9 4.9 %shard_map.87 = (bf16[32,3072]{1,0:T(8,128)(2,1)S(1)}, bf16[32,3072]{1,0:T(8,128)(2,1)S(1)}, bf16[32,3072]{1,0:T(8,128)(2,1)S(1)}, bf16[32,3072]{1,0:T(8,128)(2,...) custom-call(s32[2]{0:T(128)S(1)} %pad_add_fusion.5.info, ...), custom_call_target="tpu_custom_call", output_to_operand_aliasing={{4}: (8, {}), {5}: (9, {})} | custom-call | flops 1308622848 | bytes 9437184 | tf_op jit(solution)/shard_map/pallas_call | solution.py:94
  196.8 4.9 %collective-permute-done.29 = bf16[32,3072]{1,0:T(8,128)(2,1)S(1)} collective-permute-done((bf16[32,3072]{1,0:T(8,128)(2,1)S(1)}, bf16[32,3072]{1,0:T(8,128)(2,1)S(1)}, u32[]{:S(2)}, u32[]{:S(2)}) %collective-permute-start.29) | collective-permute-done | bytes 196640 | tf_op jit(solution)/shard_map/ppermute | solution.py:120
  201.7 9.5 %collective-permute-done.30 = bf16[32,3072]{1,0:T(8,128)(2,1)S(1)} collective-permute-done((bf16[32,3072]{1,0:T(8,128)(2,1)S(1)}, bf16[32,3072]{1,0:T(8,128)(2,1)S(1)}, u32[]{:S(2)}, u32[]{:S(2)}) %collective-permute-start.30) | collective-permute-done | bytes 196640 | tf_op jit(solution)/shard_map/ppermute | solution.py:120
  211.4 3.0 %collective-permute-start.33 = (bf16[32,3072]{1,0:T(8,128)(2,1)S(1)}, bf16[32,3072]{1,0:T(8,128)(2,1)S(1)}, u32[]{:S(2)}, u32[]{:S(2)}) collective-permute-start(bf16[32,3072]{1,0:T(8,128)(2,1)S(1)} %fusion.4.refs_0_), channel_id=1, source_target_pairs={{0,2},{1,3},{2,0},{3,1},{4,6},{5,7},{6,4},{7,5},{8,10},{9,11},{10,... | collective-permute-start | bytes 589832 | tf_op jit(solution)/shard_map/ppermute | solution.py:120
  217.4 14.6 %collective-permute-done.33.refs_2_ = bf16[32,3072]{1,0:T(8,128)(2,1)S(1)} collective-permute-done((bf16[32,3072]{1,0:T(8,128)(2,1)S(1)}, bf16[32,3072]{1,0:T(8,128)(2,1)S(1)}, u32[]{:S(2)}, u32[]{:S(2)}) %collective-permute-start.33) | collective-permute-done | bytes 196640 | tf_op jit(solution)/shard_map/ppermute | solution.py:120
  234.6 4.5 %collective-permute-done.35 = bf16[32,3072]{1,0:T(8,128)(2,1)S(1)} collective-permute-done((bf16[32,3072]{1,0:T(8,128)(2,1)S(1)}, bf16[32,3072]{1,0:T(8,128)(2,1)S(1)}, u32[]{:S(2)}, u32[]{:S(2)}) %collective-permute-start.35) | collective-permute-done | bytes 196640 | tf_op jit(solution)/shard_map/ppermute | solution.py:120
  239.1 10.7 %collective-permute-done.36 = bf16[32,3072]{1,0:T(8,128)(2,1)S(1)} collective-permute-done((bf16[32,3072]{1,0:T(8,128)(2,1)S(1)}, bf16[32,3072]{1,0:T(8,128)(2,1)S(1)}, u32[]{:S(2)}, u32[]{:S(2)}) %collective-permute-start.36) | collective-permute-done | bytes 196640 | tf_op jit(solution)/shard_map/ppermute | solution.py:120
  251.9 4.1 %collective-permute-done.38 = bf16[32,3072]{1,0:T(8,128)(2,1)S(1)} collective-permute-done((bf16[32,3072]{1,0:T(8,128)(2,1)S(1)}, bf16[32,3072]{1,0:T(8,128)(2,1)S(1)}, u32[]{:S(2)}, u32[]{:S(2)}) %collective-permute-start.38) | collective-permute-done | bytes 196640 | tf_op jit(solution)/shard_map/ppermute | solution.py:120
  (71 shorter events, 39.2 us)
Async XLA Ops:
  0.0 12.8 %collective-permute-start.2 = (bf16[32,3072]{1,0:T(8,128)(2,1)}, bf16[32,3072]{1,0:T(8,128)(2,1)S(1)}, u32[]{:S(2)}, u32[]{:S(2)}) collective-permute-start(bf16[32,3072]{1,0:T(8,128)(2,1)} %bitcast.11), channel_id=1, source_target_pairs={{0,3},{1,0},{2,1},{3,2},{4,7},{5,4},{6,5},{7,6},{8,11},{9,8},{10,9... | collective-permute-start | bytes 589832 | tf_op jit(solution)/shard_map/ppermute | solution.py:120
  5.1 16.9 %collective-permute-start.1 = (bf16[32,3072]{1,0:T(8,128)(2,1)}, bf16[32,3072]{1,0:T(8,128)(2,1)S(1)}, u32[]{:S(2)}, u32[]{:S(2)}) collective-permute-start(bf16[32,3072]{1,0:T(8,128)(2,1)} %bitcast.12), channel_id=1, source_target_pairs={{0,2},{1,3},{2,0},{3,1},{4,6},{5,7},{6,4},{7,5},{8,10},{9,11},{10,... | collective-permute-start | bytes 589832 | tf_op jit(solution)/shard_map/ppermute | solution.py:120
  5.1 16.9 %collective-permute-start = (bf16[32,3072]{1,0:T(8,128)(2,1)}, bf16[32,3072]{1,0:T(8,128)(2,1)S(1)}, u32[]{:S(2)}, u32[]{:S(2)}) collective-permute-start(bf16[32,3072]{1,0:T(8,128)(2,1)} %bitcast.13), channel_id=1, source_target_pairs={{0,1},{1,2},{2,3},{3,0},{4,5},{5,6},{6,7},{7,4},{8,9},{9,10},{10,1... | collective-permute-start | bytes 589832 | tf_op jit(solution)/shard_map/ppermute | solution.py:120
  27.3 19.4 %collective-permute-start.4 = (bf16[32,3072]{1,0:T(8,128)(2,1)S(1)}, bf16[32,3072]{1,0:T(8,128)(2,1)S(1)}, u32[]{:S(2)}, u32[]{:S(2)}) collective-permute-start(bf16[32,3072]{1,0:T(8,128)(2,1)S(1)} %get-tuple-element.49), channel_id=1, source_target_pairs={{0,2},{1,3},{2,0},{3,1},{4,6},{5,7},{6,4},{7,5},{8,10},{9,11},{10,... | collective-permute-start | bytes 589832 | tf_op jit(solution)/shard_map/ppermute | solution.py:120
  29.8 16.9 %collective-permute-start.5 = (bf16[32,3072]{1,0:T(8,128)(2,1)S(1)}, bf16[32,3072]{1,0:T(8,128)(2,1)S(1)}, u32[]{:S(2)}, u32[]{:S(2)}) collective-permute-start(bf16[32,3072]{1,0:T(8,128)(2,1)S(1)} %get-tuple-element.50), channel_id=1, source_target_pairs={{0,1},{1,2},{2,3},{3,0},{4,5},{5,6},{6,7},{7,4},{8,9},{9,10},{10,1... | collective-permute-start | bytes 589832 | tf_op jit(solution)/shard_map/ppermute | solution.py:120
  46.9 17.8 %collective-permute-start.7 = (bf16[32,3072]{1,0:T(8,128)(2,1)S(1)}, bf16[32,3072]{1,0:T(8,128)(2,1)S(1)}, u32[]{:S(2)}, u32[]{:S(2)}) collective-permute-start(bf16[32,3072]{1,0:T(8,128)(2,1)S(1)} %fusion.refs_0_), channel_id=1, source_target_pairs={{0,2},{1,3},{2,0},{3,1},{4,6},{5,7},{6,4},{7,5},{8,10},{9,11},{10,... | collective-permute-start | bytes 589832 | tf_op jit(solution)/shard_map/ppermute | solution.py:120
  47.0 17.6 %collective-permute-start.6 = (bf16[32,3072]{1,0:T(8,128)(2,1)S(1)}, bf16[32,3072]{1,0:T(8,128)(2,1)S(1)}, u32[]{:S(2)}, u32[]{:S(2)}) collective-permute-start(bf16[32,3072]{1,0:T(8,128)(2,1)S(1)} %fusion.refs_0_), channel_id=1, source_target_pairs={{0,1},{1,2},{2,3},{3,0},{4,5},{5,6},{6,7},{7,4},{8,9},{9,10},{10,1... | collective-permute-start | bytes 589832 | tf_op jit(solution)/shard_map/ppermute | solution.py:120
  65.2 7.7 %collective-permute-start.9 = (bf16[32,3072]{1,0:T(8,128)(2,1)S(1)}, bf16[32,3072]{1,0:T(8,128)(2,1)S(1)}, u32[]{:S(2)}, u32[]{:S(2)}) collective-permute-start(bf16[32,3072]{1,0:T(8,128)(2,1)S(1)} %get-tuple-element.54), channel_id=1, source_target_pairs={{0,3},{1,0},{2,1},{3,2},{4,7},{5,4},{6,5},{7,6},{8,11},{9,8},{10,9... | collective-permute-start | bytes 589832 | tf_op jit(solution)/shard_map/ppermute | solution.py:120
  65.3 10.2 %collective-permute-start.10 = (bf16[32,3072]{1,0:T(8,128)(2,1)S(1)}, bf16[32,3072]{1,0:T(8,128)(2,1)S(1)}, u32[]{:S(2)}, u32[]{:S(2)}) collective-permute-start(bf16[32,3072]{1,0:T(8,128)(2,1)S(1)} %get-tuple-element.55), channel_id=1, source_target_pairs={{0,2},{1,3},{2,0},{3,1},{4,6},{5,7},{6,4},{7,5},{8,10},{9,11},{10,... | collective-permute-start | bytes 589832 | tf_op jit(solution)/shard_map/ppermute | solution.py:120
  66.8 12.2 %collective-permute-start.11 = (bf16[32,3072]{1,0:T(8,128)(2,1)S(1)}, bf16[32,3072]{1,0:T(8,128)(2,1)S(1)}, u32[]{:S(2)}, u32[]{:S(2)}) collective-permute-start(bf16[32,3072]{1,0:T(8,128)(2,1)S(1)} %get-tuple-element.56), channel_id=1, source_target_pairs={{0,1},{1,2},{2,3},{3,0},{4,5},{5,6},{6,7},{7,4},{8,9},{9,10},{10,1... | collective-permute-start | bytes 589832 | tf_op jit(solution)/shard_map/ppermute | solution.py:120
  79.2 10.9 %collective-permute-start.15 = (bf16[32,3072]{1,0:T(8,128)(2,1)S(1)}, bf16[32,3072]{1,0:T(8,128)(2,1)S(1)}, u32[]{:S(2)}, u32[]{:S(2)}) collective-permute-start(bf16[32,3072]{1,0:T(8,128)(2,1)S(1)} %fusion.1), channel_id=1, source_target_pairs={{0,7},{1,4},{2,5},{3,6},{4,11},{5,8},{6,9},{7,10},{8,15},{9,12},{1... | collective-permute-start | bytes 589832 | tf_op jit(solution)/shard_map/ppermute | solution.py:120
  83.3 22.5 %collective-permute-start.14 = (bf16[32,3072]{1,0:T(8,128)(2,1)S(1)}, bf16[32,3072]{1,0:T(8,128)(2,1)S(1)}, u32[]{:S(2)}, u32[]{:S(2)}) collective-permute-start(bf16[32,3072]{1,0:T(8,128)(2,1)S(1)} %fusion.1), channel_id=1, source_target_pairs={{0,6},{1,7},{2,4},{3,5},{4,10},{5,11},{6,8},{7,9},{8,14},{9,15},{1... | collective-permute-start | bytes 589832 | tf_op jit(solution)/shard_map/ppermute | solution.py:120
  86.6 19.3 %collective-permute-start.13 = (bf16[32,3072]{1,0:T(8,128)(2,1)S(1)}, bf16[32,3072]{1,0:T(8,128)(2,1)S(1)}, u32[]{:S(2)}, u32[]{:S(2)}) collective-permute-start(bf16[32,3072]{1,0:T(8,128)(2,1)S(1)} %fusion.1), channel_id=1, source_target_pairs={{0,5},{1,6},{2,7},{3,4},{4,9},{5,10},{6,11},{7,8},{8,13},{9,14},{1... | collective-permute-start | bytes 589832 | tf_op jit(solution)/shard_map/ppermute | solution.py:120
  87.9 18.0 %collective-permute-start.12 = (bf16[32,3072]{1,0:T(8,128)(2,1)S(1)}, bf16[32,3072]{1,0:T(8,128)(2,1)S(1)}, u32[]{:S(2)}, u32[]{:S(2)}) collective-permute-start(bf16[32,3072]{1,0:T(8,128)(2,1)S(1)} %fusion.1), channel_id=1, source_target_pairs={{0,4},{1,5},{2,6},{3,7},{4,8},{5,9},{6,10},{7,11},{8,12},{9,13},{1... | collective-permute-start | bytes 589832 | tf_op jit(solution)/shard_map/ppermute | solution.py:120
  111.0 7.1 %collective-permute-start.16 = (bf16[32,3072]{1,0:T(8,128)(2,1)S(1)}, bf16[32,3072]{1,0:T(8,128)(2,1)S(1)}, u32[]{:S(2)}, u32[]{:S(2)}) collective-permute-start(bf16[32,3072]{1,0:T(8,128)(2,1)S(1)} %get-tuple-element.60), channel_id=1, source_target_pairs={{0,3},{1,0},{2,1},{3,2},{4,7},{5,4},{6,5},{7,6},{8,11},{9,8},{10,9... | collective-permute-start | bytes 589832 | tf_op jit(solution)/shard_map/ppermute | solution.py:120
  111.0 17.0 %collective-permute-start.17 = (bf16[32,3072]{1,0:T(8,128)(2,1)S(1)}, bf16[32,3072]{1,0:T(8,128)(2,1)S(1)}, u32[]{:S(2)}, u32[]{:S(2)}) collective-permute-start(bf16[32,3072]{1,0:T(8,128)(2,1)S(1)} %get-tuple-element.61), channel_id=1, source_target_pairs={{0,2},{1,3},{2,0},{3,1},{4,6},{5,7},{6,4},{7,5},{8,10},{9,11},{10,... | collective-permute-start | bytes 589832 | tf_op jit(solution)/shard_map/ppermute | solution.py:120
  111.9 16.2 %collective-permute-start.18 = (bf16[32,3072]{1,0:T(8,128)(2,1)S(1)}, bf16[32,3072]{1,0:T(8,128)(2,1)S(1)}, u32[]{:S(2)}, u32[]{:S(2)}) collective-permute-start(bf16[32,3072]{1,0:T(8,128)(2,1)S(1)} %get-tuple-element.62), channel_id=1, source_target_pairs={{0,1},{1,2},{2,3},{3,0},{4,5},{5,6},{6,7},{7,4},{8,9},{9,10},{10,1... | collective-permute-start | bytes 589832 | tf_op jit(solution)/shard_map/ppermute | solution.py:120
  128.3 20.1 %collective-permute-start.20 = (bf16[32,3072]{1,0:T(8,128)(2,1)S(1)}, bf16[32,3072]{1,0:T(8,128)(2,1)S(1)}, u32[]{:S(2)}, u32[]{:S(2)}) collective-permute-start(bf16[32,3072]{1,0:T(8,128)(2,1)S(1)} %fusion.2.refs_0_), channel_id=1, source_target_pairs={{0,2},{1,3},{2,0},{3,1},{4,6},{5,7},{6,4},{7,5},{8,10},{9,11},{10,... | collective-permute-start | bytes 589832 | tf_op jit(solution)/shard_map/ppermute | solution.py:120
  130.8 17.6 %collective-permute-start.19 = (bf16[32,3072]{1,0:T(8,128)(2,1)S(1)}, bf16[32,3072]{1,0:T(8,128)(2,1)S(1)}, u32[]{:S(2)}, u32[]{:S(2)}) collective-permute-start(bf16[32,3072]{1,0:T(8,128)(2,1)S(1)} %fusion.2.refs_0_), channel_id=1, source_target_pairs={{0,1},{1,2},{2,3},{3,0},{4,5},{5,6},{6,7},{7,4},{8,9},{9,10},{10,1... | collective-permute-start | bytes 589832 | tf_op jit(solution)/shard_map/ppermute | solution.py:120
  149.1 17.2 %collective-permute-start.23 = (bf16[32,3072]{1,0:T(8,128)(2,1)S(1)}, bf16[32,3072]{1,0:T(8,128)(2,1)S(1)}, u32[]{:S(2)}, u32[]{:S(2)}) collective-permute-start(bf16[32,3072]{1,0:T(8,128)(2,1)S(1)} %get-tuple-element.67), channel_id=1, source_target_pairs={{0,2},{1,3},{2,0},{3,1},{4,6},{5,7},{6,4},{7,5},{8,10},{9,11},{10,... | collective-permute-start | bytes 589832 | tf_op jit(solution)/shard_map/ppermute | solution.py:120
  149.1 17.1 %collective-permute-start.24 = (bf16[32,3072]{1,0:T(8,128)(2,1)S(1)}, bf16[32,3072]{1,0:T(8,128)(2,1)S(1)}, u32[]{:S(2)}, u32[]{:S(2)}) collective-permute-start(bf16[32,3072]{1,0:T(8,128)(2,1)S(1)} %get-tuple-element.68), channel_id=1, source_target_pairs={{0,1},{1,2},{2,3},{3,0},{4,5},{5,6},{6,7},{7,4},{8,9},{9,10},{10,1... | collective-permute-start | bytes 589832 | tf_op jit(solution)/shard_map/ppermute | solution.py:120
  166.4 9.1 %collective-permute-start.28 = (bf16[32,3072]{1,0:T(8,128)(2,1)S(1)}, bf16[32,3072]{1,0:T(8,128)(2,1)S(1)}, u32[]{:S(2)}, u32[]{:S(2)}) collective-permute-start(bf16[32,3072]{1,0:T(8,128)(2,1)S(1)} %fusion.3), channel_id=1, source_target_pairs={{0,7},{1,4},{2,5},{3,6},{4,11},{5,8},{6,9},{7,10},{8,15},{9,12},{1... | collective-permute-start | bytes 589832 | tf_op jit(solution)/shard_map/ppermute | solution.py:120
  167.0 21.9 %collective-permute-start.27 = (bf16[32,3072]{1,0:T(8,128)(2,1)S(1)}, bf16[32,3072]{1,0:T(8,128)(2,1)S(1)}, u32[]{:S(2)}, u32[]{:S(2)}) collective-permute-start(bf16[32,3072]{1,0:T(8,128)(2,1)S(1)} %fusion.3), channel_id=1, source_target_pairs={{0,6},{1,7},{2,4},{3,5},{4,10},{5,11},{6,8},{7,9},{8,14},{9,15},{1... | collective-permute-start | bytes 589832 | tf_op jit(solution)/shard_map/ppermute | solution.py:120
  170.3 18.6 %collective-permute-start.26 = (bf16[32,3072]{1,0:T(8,128)(2,1)S(1)}, bf16[32,3072]{1,0:T(8,128)(2,1)S(1)}, u32[]{:S(2)}, u32[]{:S(2)}) collective-permute-start(bf16[32,3072]{1,0:T(8,128)(2,1)S(1)} %fusion.3), channel_id=1, source_target_pairs={{0,5},{1,6},{2,7},{3,4},{4,9},{5,10},{6,11},{7,8},{8,13},{9,14},{1... | collective-permute-start | bytes 589832 | tf_op jit(solution)/shard_map/ppermute | solution.py:120
  171.2 17.7 %collective-permute-start.25 = (bf16[32,3072]{1,0:T(8,128)(2,1)S(1)}, bf16[32,3072]{1,0:T(8,128)(2,1)S(1)}, u32[]{:S(2)}, u32[]{:S(2)}) collective-permute-start(bf16[32,3072]{1,0:T(8,128)(2,1)S(1)} %fusion.3), channel_id=1, source_target_pairs={{0,4},{1,5},{2,6},{3,7},{4,8},{5,9},{6,10},{7,11},{8,12},{9,13},{1... | collective-permute-start | bytes 589832 | tf_op jit(solution)/shard_map/ppermute | solution.py:120
  193.8 7.9 %collective-permute-start.29 = (bf16[32,3072]{1,0:T(8,128)(2,1)S(1)}, bf16[32,3072]{1,0:T(8,128)(2,1)S(1)}, u32[]{:S(2)}, u32[]{:S(2)}) collective-permute-start(bf16[32,3072]{1,0:T(8,128)(2,1)S(1)} %get-tuple-element.72), channel_id=1, source_target_pairs={{0,3},{1,0},{2,1},{3,2},{4,7},{5,4},{6,5},{7,6},{8,11},{9,8},{10,9... | collective-permute-start | bytes 589832 | tf_op jit(solution)/shard_map/ppermute | solution.py:120
  193.9 17.3 %collective-permute-start.30 = (bf16[32,3072]{1,0:T(8,128)(2,1)S(1)}, bf16[32,3072]{1,0:T(8,128)(2,1)S(1)}, u32[]{:S(2)}, u32[]{:S(2)}) collective-permute-start(bf16[32,3072]{1,0:T(8,128)(2,1)S(1)} %get-tuple-element.73), channel_id=1, source_target_pairs={{0,2},{1,3},{2,0},{3,1},{4,6},{5,7},{6,4},{7,5},{8,10},{9,11},{10,... | collective-permute-start | bytes 589832 | tf_op jit(solution)/shard_map/ppermute | solution.py:120
  194.8 16.3 %collective-permute-start.31 = (bf16[32,3072]{1,0:T(8,128)(2,1)S(1)}, bf16[32,3072]{1,0:T(8,128)(2,1)S(1)}, u32[]{:S(2)}, u32[]{:S(2)}) collective-permute-start(bf16[32,3072]{1,0:T(8,128)(2,1)S(1)} %get-tuple-element.74), channel_id=1, source_target_pairs={{0,1},{1,2},{2,3},{3,0},{4,5},{5,6},{6,7},{7,4},{8,9},{9,10},{10,1... | collective-permute-start | bytes 589832 | tf_op jit(solution)/shard_map/ppermute | solution.py:120
  211.4 20.6 %collective-permute-start.33 = (bf16[32,3072]{1,0:T(8,128)(2,1)S(1)}, bf16[32,3072]{1,0:T(8,128)(2,1)S(1)}, u32[]{:S(2)}, u32[]{:S(2)}) collective-permute-start(bf16[32,3072]{1,0:T(8,128)(2,1)S(1)} %fusion.4.refs_0_), channel_id=1, source_target_pairs={{0,2},{1,3},{2,0},{3,1},{4,6},{5,7},{6,4},{7,5},{8,10},{9,11},{10,... | collective-permute-start | bytes 589832 | tf_op jit(solution)/shard_map/ppermute | solution.py:120
  214.4 17.6 %collective-permute-start.32 = (bf16[32,3072]{1,0:T(8,128)(2,1)S(1)}, bf16[32,3072]{1,0:T(8,128)(2,1)S(1)}, u32[]{:S(2)}, u32[]{:S(2)}) collective-permute-start(bf16[32,3072]{1,0:T(8,128)(2,1)S(1)} %fusion.4.refs_0_), channel_id=1, source_target_pairs={{0,1},{1,2},{2,3},{3,0},{4,5},{5,6},{6,7},{7,4},{8,9},{9,10},{10,1... | collective-permute-start | bytes 589832 | tf_op jit(solution)/shard_map/ppermute | solution.py:120
  232.6 17.2 %collective-permute-start.36 = (bf16[32,3072]{1,0:T(8,128)(2,1)S(1)}, bf16[32,3072]{1,0:T(8,128)(2,1)S(1)}, u32[]{:S(2)}, u32[]{:S(2)}) collective-permute-start(bf16[32,3072]{1,0:T(8,128)(2,1)S(1)} %get-tuple-element.79), channel_id=1, source_target_pairs={{0,2},{1,3},{2,0},{3,1},{4,6},{5,7},{6,4},{7,5},{8,10},{9,11},{10,... | collective-permute-start | bytes 589832 | tf_op jit(solution)/shard_map/ppermute | solution.py:120
  232.7 17.1 %collective-permute-start.37 = (bf16[32,3072]{1,0:T(8,128)(2,1)S(1)}, bf16[32,3072]{1,0:T(8,128)(2,1)S(1)}, u32[]{:S(2)}, u32[]{:S(2)}) collective-permute-start(bf16[32,3072]{1,0:T(8,128)(2,1)S(1)} %get-tuple-element.80), channel_id=1, source_target_pairs={{0,1},{1,2},{2,3},{3,0},{4,5},{5,6},{6,7},{7,4},{8,9},{9,10},{10,1... | collective-permute-start | bytes 589832 | tf_op jit(solution)/shard_map/ppermute | solution.py:120
  (9 other events, 87.9 us)

commit v4 on v3

--- a/solution.py
+++ b/solution.py
@@ -109,28 +109,49 @@
     return out[:chunks], out[chunks], out[chunks + 1]
 
 
-def send(block, turn, hop):
+STAY = ((0, 0), (1, 1), (2, 2), (3, 3))
+SWAP = ((0, 1), (1, 0), (2, 3), (3, 2))
+MID = ((0, 0), (1, 2), (2, 1), (3, 3))
+INWARD = ((0, 2), (3, 1), (1, 0), (2, 3))
+OUTWARD = ((2, 0), (1, 3), (0, 1), (3, 2))
+
+
+def send(block, pairs, hop=0):
     sections = lax.axis_size("section")
     n = lax.axis_size("uly")
     route = [
-        (s * n + i, (s + hop) % sections * n + (i + turn) % n)
-        for s in range(sections)
-        for i in range(n)
+        (s * n + a, (s + hop) % sections * n + b) for s in range(sections) for a, b in pairs
     ]
     return lax.ppermute(block, ("section", "uly"), route)
 
 
-def gathered(own, hop):
-    n = lax.axis_size("uly")
-    first = own if hop == 0 else send(own, 0, hop)
-    return [first] + [send(own, k, hop) for k in range(1, n)]
-
-
-def summed(blocks):
+def summed(*blocks):
     total = blocks[0].astype(jnp.float32)
     for block in blocks[1:]:
         total = total + block.astype(jnp.float32)
     return total
+
+
+def gathered(own, at_end, hop=0):
+    partner = send(own, SWAP, hop)
+    across = send(own, MID, hop)
+    first = send(own, STAY, hop) if hop else own
+    far = send(partner, OUTWARD)
+    far_mid = send(partner, MID)
+    near = send(across, SWAP)
+    return [first, partner, jnp.where(at_end, near, across), jnp.where(at_end, far, far_mid)]
+
+
+def scattered(terms, at_end):
+    own, partner, near, far = terms
+    far_in = send(far, INWARD)
+    far_mid = send(far, MID)
+    near_in = send(near, SWAP)
+    passed = summed(partner, far_in, far_mid).astype(jnp.bfloat16)
+    from_pair = send(jnp.where(at_end, partner, passed), SWAP)
+    from_across = send(summed(near, near_in).astype(jnp.bfloat16), MID)
+    total = summed(own, from_pair)
+    return jnp.where(at_end, total, total + from_across.astype(jnp.float32))
 
 
 def shards(
@@ -145,20 +166,21 @@
     n = lax.axis_size("uly")
     patch_rows = state.shape[1] * n
     own = state[0]
-    blocks = gathered(own, 0)
+    place = lax.axis_index("uly")
+    at_end = (place == 0) | (place == n - 1)
+    blocks = gathered(own, at_end)
     for tick in range(TICKS):
         slot = patch_slot[(section_index - tick) % section_count]
         for index in range(PASSES):
             applies = block_count > index
             info = jnp.stack([slot * patch_rows, applies.astype(jnp.int32)])
             terms, kc, vc = block_terms(info, blocks, norm_gain, w, wo, kc, vc)
-            arrived = [send(terms[k], n - k, 0) for k in range(1, n)]
-            updated = own.astype(jnp.float32) + summed([terms[0]] + arrived)
+            updated = own.astype(jnp.float32) + scattered(terms, at_end)
             updated = jnp.where(applies, updated.astype(jnp.bfloat16), own)
             last = index == PASSES - 1
             if last and tick == TICKS - 1:
-                return send(updated, 0, 1)[None]
-            blocks = gathered(updated, 1 if last else 0)
+                return send(updated, STAY, 1)[None]
+            blocks = gathered(updated, at_end, 1 if last else 0)
             own = blocks[0]
 
 

time: 261 us -> 294 us (1.13)
  the two profiles are of different devices: /device:TPU:0 before, /device:TPU:12 now
where the time goes in v4:
time: 294 us; the launch traced here: 292 us
  waiting for transfers between devices  163 us (55%)
  starting transfers between devices  86.9 us (30%)
  Pallas kernels  33.8 us (11%)
  between operations  3.16 us (1%)
    ppermute x63, waiting for transfers between devices, send(): return lax.ppermute(block, ('section', 'uly'), route)  163 us
    ppermute x63, starting transfers between devices, send(): return lax.ppermute(block, ('section', 'uly'), route)  86.9 us
    pallas_call x6, Pallas kernels, block_terms(): pl.pallas_call(functools.partial(block_kernel, chunks), out_shape=[jax.Sh...  29.9 us
  transfers between devices with their start and end apart: 63, of which 51 were waited for; matrix products, arithmetic and copies ran while one was open for 1% of the time, Pallas kernels for 1%

profile of v4, /device:TPU:12, one launch (start us, length us, event | category | flops | bytes accessed | tf_op | source)
XLA Modules:
  0.0 291.6 jit_solution(4745874752590336026)
XLA Ops:
  0.0 3.6 %collective-permute-start.1 = (bf16[32,3072]{1,0:T(8,128)(2,1)}, bf16[32,3072]{1,0:T(8,128)(2,1)S(1)}, u32[]{:S(2)}, u32[]{:S(2)}) collective-permute-start(bf16[32,3072]{1,0:T(8,128)(2,1)} %bitcast.11), channel_id=1, source_target_pairs={{0,0},{1,2},{2,1},{3,3},{4,4},{5,6},{6,5},{7,7},{8,8},{9,10},{10,9... | collective-permute-start | bytes 589832 | tf_op jit(solution)/shard_map/ppermute | solution.py:125
  3.7 5.2 %collective-permute-done.1 = bf16[32,3072]{1,0:T(8,128)(2,1)S(1)} collective-permute-done((bf16[32,3072]{1,0:T(8,128)(2,1)}, bf16[32,3072]{1,0:T(8,128)(2,1)S(1)}, u32[]{:S(2)}, u32[]{:S(2)}) %collective-permute-start.1) | collective-permute-done | bytes 196640 | tf_op jit(solution)/shard_map/ppermute | solution.py:125
  11.6 3.9 %shard_map.82 = (bf16[3,3072,384]{2,1,0:T(8,128)(2,1)S(1)}, bf16[384,3072]{1,0:T(8,128)(2,1)S(1)}, bf16[512,384]{1,0:T(8,128)(2,1)S(1)}, bf16[512,384]{1,0:T(8,128)(2,1)S(1)}) custom-call(bf16[3,3072,384]{2,1,0:T(8,128)(2,1)} %bitcast.14, bf16[384,3072]{1,0:T(8,128)(2,1)} %bitcast.15, bf16[512,384]{1,0:T(8,128)(2,1)} %bitcast.16, bf16[512,384]{1,0:T(8,128)(2,1)} %bitcast.17), custom_call_target="tpu_custom_call" | custom-call | bytes 10223616 | tf_op jit(solution)/shard_map/pallas_call | solution.py:73
  19.4 5.9 %collective-permute-done.4 = bf16[32,3072]{1,0:T(8,128)(2,1)S(1)} collective-permute-done((bf16[32,3072]{1,0:T(8,128)(2,1)S(1)}, bf16[32,3072]{1,0:T(8,128)(2,1)S(1)}, u32[]{:S(2)}, u32[]{:S(2)}) %collective-permute-start.4) | collective-permute-done | bytes 196640 | tf_op jit(solution)/shard_map/ppermute | solution.py:125
  26.6 4.9 %shard_map.83 = (bf16[32,3072]{1,0:T(8,128)(2,1)S(1)}, bf16[32,3072]{1,0:T(8,128)(2,1)S(1)}, bf16[32,3072]{1,0:T(8,128)(2,1)S(1)}, bf16[32,3072]{1,0:T(8,128)(2,...) custom-call(s32[2]{0:T(128)S(1)} %pad_add_fusion.1.info, ...), custom_call_target="tpu_custom_call", output_to_operand_aliasing={{4}: (8, {}), {5}: (9, {})} | custom-call | flops 1308622848 | bytes 9437184 | tf_op jit(solution)/shard_map/pallas_call | solution.py:94
  37.0 5.5 %collective-permute-done.6 = bf16[32,3072]{1,0:T(8,128)(2,1)S(1)} collective-permute-done((bf16[32,3072]{1,0:T(8,128)(2,1)S(1)}, bf16[32,3072]{1,0:T(8,128)(2,1)S(1)}, u32[]{:S(2)}, u32[]{:S(2)}) %collective-permute-start.6) | collective-permute-done | bytes 196640 | tf_op jit(solution)/shard_map/ppermute | solution.py:125
  48.3 4.7 %collective-permute-done.9 = bf16[32,3072]{1,0:T(8,128)(2,1)S(1)} collective-permute-done((bf16[32,3072]{1,0:T(8,128)(2,1)S(1)}, bf16[32,3072]{1,0:T(8,128)(2,1)S(1)}, u32[]{:S(2)}, u32[]{:S(2)}) %collective-permute-start.9) | collective-permute-done | bytes 196640 | tf_op jit(solution)/shard_map/ppermute | solution.py:125
  53.1 4.4 %collective-permute-start.11 = (bf16[32,3072]{1,0:T(8,128)(2,1)S(1)}, bf16[32,3072]{1,0:T(8,128)(2,1)S(1)}, u32[]{:S(2)}, u32[]{:S(2)}) collective-permute-start(bf16[32,3072]{1,0:T(8,128)(2,1)S(1)} %fusion.23.refs_0_), channel_id=1, source_target_pairs={{0,0},{1,2},{2,1},{3,3},{4,4},{5,6},{6,5},{7,7},{8,8},{9,10},{10,9... | collective-permute-start | bytes 589832 | tf_op jit(solution)/shard_map/ppermute | solution.py:125
  57.6 5.6 %collective-permute-done.11 = bf16[32,3072]{1,0:T(8,128)(2,1)S(1)} collective-permute-done((bf16[32,3072]{1,0:T(8,128)(2,1)S(1)}, bf16[32,3072]{1,0:T(8,128)(2,1)S(1)}, u32[]{:S(2)}, u32[]{:S(2)}) %collective-permute-start.11) | collective-permute-done | bytes 196640 | tf_op jit(solution)/shard_map/ppermute | solution.py:125
  73.0 4.9 %shard_map.84 = (bf16[32,3072]{1,0:T(8,128)(2,1)S(1)}, bf16[32,3072]{1,0:T(8,128)(2,1)S(1)}, bf16[32,3072]{1,0:T(8,128)(2,1)S(1)}, bf16[32,3072]{1,0:T(8,128)(2,...) custom-call(s32[2]{0:T(128)S(1)} %pad_add_fusion.info, ...), custom_call_target="tpu_custom_call", output_to_operand_aliasing={{4}: (8, {}), {5}: (9, {})} | custom-call | flops 1308622848 | bytes 9437184 | tf_op jit(solution)/shard_map/pallas_call | solution.py:94
  83.3 6.0 %collective-permute-done.16 = bf16[32,3072]{1,0:T(8,128)(2,1)S(1)} collective-permute-done((bf16[32,3072]{1,0:T(8,128)(2,1)S(1)}, bf16[32,3072]{1,0:T(8,128)(2,1)S(1)}, u32[]{:S(2)}, u32[]{:S(2)}) %collective-permute-start.16) | collective-permute-done | bytes 196640 | tf_op jit(solution)/shard_map/ppermute | solution.py:125
  97.4 8.8 %collective-permute-done.22 = bf16[32,3072]{1,0:T(8,128)(2,1)S(1)} collective-permute-done((bf16[32,3072]{1,0:T(8,128)(2,1)S(1)}, bf16[32,3072]{1,0:T(8,128)(2,1)S(1)}, u32[]{:S(2)}, u32[]{:S(2)}) %collective-permute-start.22) | collective-permute-done | bytes 196640 | tf_op jit(solution)/shard_map/ppermute | solution.py:125
  111.9 4.7 %collective-permute-done.25 = bf16[32,3072]{1,0:T(8,128)(2,1)S(1)} collective-permute-done((bf16[32,3072]{1,0:T(8,128)(2,1)S(1)}, bf16[32,3072]{1,0:T(8,128)(2,1)S(1)}, u32[]{:S(2)}, u32[]{:S(2)}) %collective-permute-start.25) | collective-permute-done | bytes 196640 | tf_op jit(solution)/shard_map/ppermute | solution.py:125
  119.5 5.1 %shard_map.85 = (bf16[32,3072]{1,0:T(8,128)(2,1)S(1)}, bf16[32,3072]{1,0:T(8,128)(2,1)S(1)}, bf16[32,3072]{1,0:T(8,128)(2,1)S(1)}, bf16[32,3072]{1,0:T(8,128)(2,...) custom-call(s32[2]{0:T(128)S(1)} %pad_add_fusion.3.info, ...), custom_call_target="tpu_custom_call", output_to_operand_aliasing={{4}: (8, {}), {5}: (9, {})} | custom-call | flops 1308622848 | bytes 9437184 | tf_op jit(solution)/shard_map/pallas_call | solution.py:94
  130.0 7.4 %collective-permute-done.27 = bf16[32,3072]{1,0:T(8,128)(2,1)S(1)} collective-permute-done((bf16[32,3072]{1,0:T(8,128)(2,1)S(1)}, bf16[32,3072]{1,0:T(8,128)(2,1)S(1)}, u32[]{:S(2)}, u32[]{:S(2)}) %collective-permute-start.27) | collective-permute-done | bytes 196640 | tf_op jit(solution)/shard_map/ppermute | solution.py:125
  149.2 4.8 %collective-permute-done.32 = bf16[32,3072]{1,0:T(8,128)(2,1)S(1)} collective-permute-done((bf16[32,3072]{1,0:T(8,128)(2,1)S(1)}, bf16[32,3072]{1,0:T(8,128)(2,1)S(1)}, u32[]{:S(2)}, u32[]{:S(2)}) %collective-permute-start.32) | collective-permute-done | bytes 196640 | tf_op jit(solution)/shard_map/ppermute | solution.py:125
  156.7 3.5 %collective-permute-start.35 = (bf16[32,3072]{1,0:T(8,128)(2,1)S(1)}, bf16[32,3072]{1,0:T(8,128)(2,1)S(1)}, u32[]{:S(2)}, u32[]{:S(2)}) collective-permute-start(bf16[32,3072]{1,0:T(8,128)(2,1)S(1)} %collective-permute-done.31.refs_1_), channel_id=1, source_target_pairs={{0,0},{1,2},{2,1},{3,3},{4,4},{5,6},{6,5},{7,7},{8,8},{9,10},{10,9... | collective-permute-start | bytes 589832 | tf_op jit(solution)/shard_map/ppermute | solution.py:125
  165.9 4.9 %shard_map.86 = (bf16[32,3072]{1,0:T(8,128)(2,1)S(1)}, bf16[32,3072]{1,0:T(8,128)(2,1)S(1)}, bf16[32,3072]{1,0:T(8,128)(2,1)S(1)}, bf16[32,3072]{1,0:T(8,128)(2,...) custom-call(s32[2]{0:T(128)S(1)} %pad_add_fusion.2.info, ...), custom_call_target="tpu_custom_call", output_to_operand_aliasing={{4}: (8, {}), {5}: (9, {})} | custom-call | flops 1308622848 | bytes 9437184 | tf_op jit(solution)/shard_map/pallas_call | solution.py:94
  191.1 8.8 %collective-permute-done.43 = bf16[32,3072]{1,0:T(8,128)(2,1)S(1)} collective-permute-done((bf16[32,3072]{1,0:T(8,128)(2,1)S(1)}, bf16[32,3072]{1,0:T(8,128)(2,1)S(1)}, u32[]{:S(2)}, u32[]{:S(2)}) %collective-permute-start.43) | collective-permute-done | bytes 196640 | tf_op jit(solution)/shard_map/ppermute | solution.py:125
  205.7 4.7 %collective-permute-done.46 = bf16[32,3072]{1,0:T(8,128)(2,1)S(1)} collective-permute-done((bf16[32,3072]{1,0:T(8,128)(2,1)S(1)}, bf16[32,3072]{1,0:T(8,128)(2,1)S(1)}, u32[]{:S(2)}, u32[]{:S(2)}) %collective-permute-start.46) | collective-permute-done | bytes 196640 | tf_op jit(solution)/shard_map/ppermute | solution.py:125
  212.8 5.1 %shard_map.87 = (bf16[32,3072]{1,0:T(8,128)(2,1)S(1)}, bf16[32,3072]{1,0:T(8,128)(2,1)S(1)}, bf16[32,3072]{1,0:T(8,128)(2,1)S(1)}, bf16[32,3072]{1,0:T(8,128)(2,...) custom-call(s32[2]{0:T(128)S(1)} %pad_add_fusion.5.info, ...), custom_call_target="tpu_custom_call", output_to_operand_aliasing={{4}: (8, {}), {5}: (9, {})} | custom-call | flops 1308622848 | bytes 9437184 | tf_op jit(solution)/shard_map/pallas_call | solution.py:94
  223.4 7.3 %collective-permute-done.48 = bf16[32,3072]{1,0:T(8,128)(2,1)S(1)} collective-permute-done((bf16[32,3072]{1,0:T(8,128)(2,1)S(1)}, bf16[32,3072]{1,0:T(8,128)(2,1)S(1)}, u32[]{:S(2)}, u32[]{:S(2)}) %collective-permute-start.48) | collective-permute-done | bytes 196640 | tf_op jit(solution)/shard_map/ppermute | solution.py:125
  232.0 3.6 %collective-permute-start.51 = (bf16[32,3072]{1,0:T(8,128)(2,1)S(1)}, bf16[32,3072]{1,0:T(8,128)(2,1)S(1)}, u32[]{:S(2)}, u32[]{:S(2)}) collective-permute-start(bf16[32,3072]{1,0:T(8,128)(2,1)S(1)} %add_convert_fusion.2), channel_id=1, source_target_pairs={{0,0},{1,2},{2,1},{3,3},{4,4},{5,6},{6,5},{7,7},{8,8},{9,10},{10,9... | collective-permute-start | bytes 589832 | tf_op jit(solution)/shard_map/ppermute | solution.py:125
  239.8 3.6 %collective-permute-start.53 = (bf16[32,3072]{1,0:T(8,128)(2,1)S(1)}, bf16[32,3072]{1,0:T(8,128)(2,1)S(1)}, u32[]{:S(2)}, u32[]{:S(2)}) collective-permute-start(bf16[32,3072]{1,0:T(8,128)(2,1)S(1)} %fusion.19.refs_0_), channel_id=1, source_target_pairs={{0,0},{1,2},{2,1},{3,3},{4,4},{5,6},{6,5},{7,7},{8,8},{9,10},{10,9... | collective-permute-start | bytes 589832 | tf_op jit(solution)/shard_map/ppermute | solution.py:125
  243.5 3.8 %collective-permute-done.53 = bf16[32,3072]{1,0:T(8,128)(2,1)S(1)} collective-permute-done((bf16[32,3072]{1,0:T(8,128)(2,1)S(1)}, bf16[32,3072]{1,0:T(8,128)(2,1)S(1)}, u32[]{:S(2)}, u32[]{:S(2)}) %collective-permute-start.53) | collective-permute-done | bytes 196640 | tf_op jit(solution)/shard_map/ppermute | solution.py:125
  247.4 3.8 %collective-permute-done.52.refs_1_ = bf16[32,3072]{1,0:T(8,128)(2,1)S(1)} collective-permute-done((bf16[32,3072]{1,0:T(8,128)(2,1)S(1)}, bf16[32,3072]{1,0:T(8,128)(2,1)S(1)}, u32[]{:S(2)}, u32[]{:S(2)}) %collective-permute-start.52) | collective-permute-done | bytes 196640 | tf_op jit(solution)/shard_map/ppermute | solution.py:125
  255.3 3.5 %collective-permute-done.56 = bf16[32,3072]{1,0:T(8,128)(2,1)S(1)} collective-permute-done((bf16[32,3072]{1,0:T(8,128)(2,1)S(1)}, bf16[32,3072]{1,0:T(8,128)(2,1)S(1)}, u32[]{:S(2)}, u32[]{:S(2)}) %collective-permute-start.56) | collective-permute-done | bytes 196640 | tf_op jit(solution)/shard_map/ppermute | solution.py:125
  258.9 4.9 %shard_map.88 = (bf16[32,3072]{1,0:T(8,128)(2,1)S(1)}, bf16[32,3072]{1,0:T(8,128)(2,1)S(1)}, bf16[32,3072]{1,0:T(8,128)(2,1)S(1)}, bf16[32,3072]{1,0:T(8,128)(2,...) custom-call(s32[2]{0:T(128)S(1)} %pad_add_fusion.4.info, ...), custom_call_target="tpu_custom_call", output_to_operand_aliasing={{4}: (8, {}), {5}: (9, {})} | custom-call | flops 1308622848 | bytes 9437184 | tf_op jit(solution)/shard_map/pallas_call | solution.py:94
  263.8 3.9 %collective-permute-start.58 = (bf16[32,3072]{1,0:T(8,128)(2,1)S(1)}, bf16[32,3072]{1,0:T(8,128)(2,1)S(1)}, u32[]{:S(2)}, u32[]{:S(2)}) collective-permute-start(bf16[32,3072]{1,0:T(8,128)(2,1)S(1)} %get-tuple-element.79), channel_id=1, source_target_pairs={{0,0},{1,2},{2,1},{3,3},{4,4},{5,6},{6,5},{7,7},{8,8},{9,10},{10,9... | collective-permute-start | bytes 589832 | tf_op jit(solution)/shard_map/ppermute | solution.py:125
  272.4 4.0 %collective-permute-done.57 = bf16[32,3072]{1,0:T(8,128)(2,1)S(1)} collective-permute-done((bf16[32,3072]{1,0:T(8,128)(2,1)S(1)}, bf16[32,3072]{1,0:T(8,128)(2,1)S(1)}, u32[]{:S(2)}, u32[]{:S(2)}) %collective-permute-start.57) | collective-permute-done | bytes 196640 | tf_op jit(solution)/shard_map/ppermute | solution.py:125
  277.2 3.7 %collective-permute-start.61 = (bf16[32,3072]{1,0:T(8,128)(2,1)S(1)}, bf16[32,3072]{1,0:T(8,128)(2,1)S(1)}, u32[]{:S(2)}, u32[]{:S(2)}) collective-permute-start(bf16[32,3072]{1,0:T(8,128)(2,1)S(1)} %add_convert_fusion), channel_id=1, source_target_pairs={{0,0},{1,2},{2,1},{3,3},{4,4},{5,6},{6,5},{7,7},{8,8},{9,10},{10,9... | collective-permute-start | bytes 589832 | tf_op jit(solution)/shard_map/ppermute | solution.py:125
  285.0 6.0 %collective-permute-done.62 = bf16[32,3072]{1,0:T(8,128)(2,1)S(1)} collective-permute-done((bf16[32,3072]{1,0:T(8,128)(2,1)S(1)}, bf16[32,3072]{1,0:T(8,128)(2,1)S(1)}, u32[]{:S(2)}, u32[]{:S(2)}) %collective-permute-start.62) | collective-permute-done | bytes 196640 | tf_op jit(solution)/shard_map/ppermute | solution.py:125
  (143 shorter events, 127.5 us)
Async XLA Ops:
  0.0 8.9 %collective-permute-start.1 = (bf16[32,3072]{1,0:T(8,128)(2,1)}, bf16[32,3072]{1,0:T(8,128)(2,1)S(1)}, u32[]{:S(2)}, u32[]{:S(2)}) collective-permute-start(bf16[32,3072]{1,0:T(8,128)(2,1)} %bitcast.11), channel_id=1, source_target_pairs={{0,0},{1,2},{2,1},{3,3},{4,4},{5,6},{6,5},{7,7},{8,8},{9,10},{10,9... | collective-permute-start | bytes 589832 | tf_op jit(solution)/shard_map/ppermute | solution.py:125
  3.6 12.0 %collective-permute-start = (bf16[32,3072]{1,0:T(8,128)(2,1)}, bf16[32,3072]{1,0:T(8,128)(2,1)S(1)}, u32[]{:S(2)}, u32[]{:S(2)}) collective-permute-start(bf16[32,3072]{1,0:T(8,128)(2,1)} %bitcast.12), channel_id=1, source_target_pairs={{0,1},{1,0},{2,3},{3,2},{4,5},{5,4},{6,7},{7,6},{8,9},{9,8},{10,11... | collective-permute-start | bytes 589832 | tf_op jit(solution)/shard_map/ppermute | solution.py:125
  8.9 10.5 %collective-permute-start.2 = (bf16[32,3072]{1,0:T(8,128)(2,1)S(1)}, bf16[32,3072]{1,0:T(8,128)(2,1)S(1)}, u32[]{:S(2)}, u32[]{:S(2)}) collective-permute-start(bf16[32,3072]{1,0:T(8,128)(2,1)S(1)} %collective-permute-done.1), channel_id=1, source_target_pairs={{0,1},{1,0},{2,3},{3,2},{4,5},{5,4},{6,7},{7,6},{8,9},{9,8},{10,11... | collective-permute-start | bytes 589832 | tf_op jit(solution)/shard_map/ppermute | solution.py:125
  15.6 9.7 %collective-permute-start.4 = (bf16[32,3072]{1,0:T(8,128)(2,1)S(1)}, bf16[32,3072]{1,0:T(8,128)(2,1)S(1)}, u32[]{:S(2)}, u32[]{:S(2)}) collective-permute-start(bf16[32,3072]{1,0:T(8,128)(2,1)S(1)} %collective-permute-done.refs_1_), channel_id=1, source_target_pairs={{0,0},{1,2},{2,1},{3,3},{4,4},{5,6},{6,5},{7,7},{8,8},{9,10},{10,9... | collective-permute-start | bytes 589832 | tf_op jit(solution)/shard_map/ppermute | solution.py:125
  31.5 11.0 %collective-permute-start.6 = (bf16[32,3072]{1,0:T(8,128)(2,1)S(1)}, bf16[32,3072]{1,0:T(8,128)(2,1)S(1)}, u32[]{:S(2)}, u32[]{:S(2)}) collective-permute-start(bf16[32,3072]{1,0:T(8,128)(2,1)S(1)} %get-tuple-element.49), channel_id=1, source_target_pairs={{0,0},{1,2},{2,1},{3,3},{4,4},{5,6},{6,5},{7,7},{8,8},{9,10},{10,9... | collective-permute-start | bytes 589832 | tf_op jit(solution)/shard_map/ppermute | solution.py:125
  33.9 8.6 %collective-permute-start.5 = (bf16[32,3072]{1,0:T(8,128)(2,1)S(1)}, bf16[32,3072]{1,0:T(8,128)(2,1)S(1)}, u32[]{:S(2)}, u32[]{:S(2)}) collective-permute-start(bf16[32,3072]{1,0:T(8,128)(2,1)S(1)} %get-tuple-element.49), channel_id=1, source_target_pairs={{0,2},{3,1},{1,0},{2,3},{4,6},{7,5},{5,4},{6,7},{8,10},{11,9},{9,8... | collective-permute-start | bytes 589832 | tf_op jit(solution)/shard_map/ppermute | solution.py:125
  34.6 10.3 %collective-permute-start.8 = (bf16[32,3072]{1,0:T(8,128)(2,1)S(1)}, bf16[32,3072]{1,0:T(8,128)(2,1)S(1)}, u32[]{:S(2)}, u32[]{:S(2)}) collective-permute-start(bf16[32,3072]{1,0:T(8,128)(2,1)S(1)} %get-tuple-element.50), channel_id=1, source_target_pairs={{0,1},{1,0},{2,3},{3,2},{4,5},{5,4},{6,7},{7,6},{8,9},{9,8},{10,11... | collective-permute-start | bytes 589832 | tf_op jit(solution)/shard_map/ppermute | solution.py:125
  53.1 10.1 %collective-permute-start.11 = (bf16[32,3072]{1,0:T(8,128)(2,1)S(1)}, bf16[32,3072]{1,0:T(8,128)(2,1)S(1)}, u32[]{:S(2)}, u32[]{:S(2)}) collective-permute-start(bf16[32,3072]{1,0:T(8,128)(2,1)S(1)} %fusion.23.refs_0_), channel_id=1, source_target_pairs={{0,0},{1,2},{2,1},{3,3},{4,4},{5,6},{6,5},{7,7},{8,8},{9,10},{10,9... | collective-permute-start | bytes 589832 | tf_op jit(solution)/shard_map/ppermute | solution.py:125
  77.9 11.4 %collective-permute-start.16 = (bf16[32,3072]{1,0:T(8,128)(2,1)S(1)}, bf16[32,3072]{1,0:T(8,128)(2,1)S(1)}, u32[]{:S(2)}, u32[]{:S(2)}) collective-permute-start(bf16[32,3072]{1,0:T(8,128)(2,1)S(1)} %get-tuple-element.55), channel_id=1, source_target_pairs={{0,0},{1,2},{2,1},{3,3},{4,4},{5,6},{6,5},{7,7},{8,8},{9,10},{10,9... | collective-permute-start | bytes 589832 | tf_op jit(solution)/shard_map/ppermute | solution.py:125
  80.9 8.4 %collective-permute-start.15 = (bf16[32,3072]{1,0:T(8,128)(2,1)S(1)}, bf16[32,3072]{1,0:T(8,128)(2,1)S(1)}, u32[]{:S(2)}, u32[]{:S(2)}) collective-permute-start(bf16[32,3072]{1,0:T(8,128)(2,1)S(1)} %get-tuple-element.55), channel_id=1, source_target_pairs={{0,2},{3,1},{1,0},{2,3},{4,6},{7,5},{5,4},{6,7},{8,10},{11,9},{9,8... | collective-permute-start | bytes 589832 | tf_op jit(solution)/shard_map/ppermute | solution.py:125
  97.3 9.0 %collective-permute-start.22 = (bf16[32,3072]{1,0:T(8,128)(2,1)S(1)}, bf16[32,3072]{1,0:T(8,128)(2,1)S(1)}, u32[]{:S(2)}, u32[]{:S(2)}) collective-permute-start(bf16[32,3072]{1,0:T(8,128)(2,1)S(1)} %fusion.22), channel_id=1, source_target_pairs={{0,4},{1,6},{2,5},{3,7},{4,8},{5,10},{6,9},{7,11},{8,12},{9,14},{1... | collective-permute-start | bytes 589832 | tf_op jit(solution)/shard_map/ppermute | solution.py:125
  97.3 9.6 %collective-permute-start.21 = (bf16[32,3072]{1,0:T(8,128)(2,1)S(1)}, bf16[32,3072]{1,0:T(8,128)(2,1)S(1)}, u32[]{:S(2)}, u32[]{:S(2)}) collective-permute-start(bf16[32,3072]{1,0:T(8,128)(2,1)S(1)} %fusion.22), channel_id=1, source_target_pairs={{0,5},{1,4},{2,7},{3,6},{4,9},{5,8},{6,11},{7,10},{8,13},{9,12},{1... | collective-permute-start | bytes 589832 | tf_op jit(solution)/shard_map/ppermute | solution.py:125
  106.9 12.6 %collective-permute-start.20 = (bf16[32,3072]{1,0:T(8,128)(2,1)S(1)}, bf16[32,3072]{1,0:T(8,128)(2,1)S(1)}, u32[]{:S(2)}, u32[]{:S(2)}) collective-permute-start(bf16[32,3072]{1,0:T(8,128)(2,1)S(1)} %fusion.22), channel_id=1, source_target_pairs={{0,4},{1,5},{2,6},{3,7},{4,8},{5,9},{6,10},{7,11},{8,12},{9,13},{1... | collective-permute-start | bytes 589832 | tf_op jit(solution)/shard_map/ppermute | solution.py:125
  106.9 9.7 %collective-permute-start.25 = (bf16[32,3072]{1,0:T(8,128)(2,1)S(1)}, bf16[32,3072]{1,0:T(8,128)(2,1)S(1)}, u32[]{:S(2)}, u32[]{:S(2)}) collective-permute-start(bf16[32,3072]{1,0:T(8,128)(2,1)S(1)} %collective-permute-done.21.refs_1_), channel_id=1, source_target_pairs={{0,0},{1,2},{2,1},{3,3},{4,4},{5,6},{6,5},{7,7},{8,8},{9,10},{10,9... | collective-permute-start | bytes 589832 | tf_op jit(solution)/shard_map/ppermute | solution.py:125
  110.1 9.3 %collective-permute-start.24 = (bf16[32,3072]{1,0:T(8,128)(2,1)S(1)}, bf16[32,3072]{1,0:T(8,128)(2,1)S(1)}, u32[]{:S(2)}, u32[]{:S(2)}) collective-permute-start(bf16[32,3072]{1,0:T(8,128)(2,1)S(1)} %collective-permute-done.21.refs_1_), channel_id=1, source_target_pairs={{2,0},{1,3},{0,1},{3,2},{6,4},{5,7},{4,5},{7,6},{10,8},{9,11},{8,9... | collective-permute-start | bytes 589832 | tf_op jit(solution)/shard_map/ppermute | solution.py:125
  124.6 12.9 %collective-permute-start.27 = (bf16[32,3072]{1,0:T(8,128)(2,1)S(1)}, bf16[32,3072]{1,0:T(8,128)(2,1)S(1)}, u32[]{:S(2)}, u32[]{:S(2)}) collective-permute-start(bf16[32,3072]{1,0:T(8,128)(2,1)S(1)} %get-tuple-element.61), channel_id=1, source_target_pairs={{0,0},{1,2},{2,1},{3,3},{4,4},{5,6},{6,5},{7,7},{8,8},{9,10},{10,9... | collective-permute-start | bytes 589832 | tf_op jit(solution)/shard_map/ppermute | solution.py:125
  127.2 10.2 %collective-permute-start.26 = (bf16[32,3072]{1,0:T(8,128)(2,1)S(1)}, bf16[32,3072]{1,0:T(8,128)(2,1)S(1)}, u32[]{:S(2)}, u32[]{:S(2)}) collective-permute-start(bf16[32,3072]{1,0:T(8,128)(2,1)S(1)} %get-tuple-element.61), channel_id=1, source_target_pairs={{0,2},{3,1},{1,0},{2,3},{4,6},{7,5},{5,4},{6,7},{8,10},{11,9},{9,8... | collective-permute-start | bytes 589832 | tf_op jit(solution)/shard_map/ppermute | solution.py:125
  128.0 10.8 %collective-permute-start.29 = (bf16[32,3072]{1,0:T(8,128)(2,1)S(1)}, bf16[32,3072]{1,0:T(8,128)(2,1)S(1)}, u32[]{:S(2)}, u32[]{:S(2)}) collective-permute-start(bf16[32,3072]{1,0:T(8,128)(2,1)S(1)} %get-tuple-element.62), channel_id=1, source_target_pairs={{0,1},{1,0},{2,3},{3,2},{4,5},{5,4},{6,7},{7,6},{8,9},{9,8},{10,11... | collective-permute-start | bytes 589832 | tf_op jit(solution)/shard_map/ppermute | solution.py:125
  170.9 8.4 %collective-permute-start.37 = (bf16[32,3072]{1,0:T(8,128)(2,1)S(1)}, bf16[32,3072]{1,0:T(8,128)(2,1)S(1)}, u32[]{:S(2)}, u32[]{:S(2)}) collective-permute-start(bf16[32,3072]{1,0:T(8,128)(2,1)S(1)} %get-tuple-element.67), channel_id=1, source_target_pairs={{0,0},{1,2},{2,1},{3,3},{4,4},{5,6},{6,5},{7,7},{8,8},{9,10},{10,9... | collective-permute-start | bytes 589832 | tf_op jit(solution)/shard_map/ppermute | solution.py:125
  173.2 8.6 %collective-permute-start.36 = (bf16[32,3072]{1,0:T(8,128)(2,1)S(1)}, bf16[32,3072]{1,0:T(8,128)(2,1)S(1)}, u32[]{:S(2)}, u32[]{:S(2)}) collective-permute-start(bf16[32,3072]{1,0:T(8,128)(2,1)S(1)} %get-tuple-element.67), channel_id=1, source_target_pairs={{0,2},{3,1},{1,0},{2,3},{4,6},{7,5},{5,4},{6,7},{8,10},{11,9},{9,8... | collective-permute-start | bytes 589832 | tf_op jit(solution)/shard_map/ppermute | solution.py:125
  173.5 9.8 %collective-permute-start.39 = (bf16[32,3072]{1,0:T(8,128)(2,1)S(1)}, bf16[32,3072]{1,0:T(8,128)(2,1)S(1)}, u32[]{:S(2)}, u32[]{:S(2)}) collective-permute-start(bf16[32,3072]{1,0:T(8,128)(2,1)S(1)} %get-tuple-element.68), channel_id=1, source_target_pairs={{0,1},{1,0},{2,3},{3,2},{4,5},{5,4},{6,7},{7,6},{8,9},{9,8},{10,11... | collective-permute-start | bytes 589832 | tf_op jit(solution)/shard_map/ppermute | solution.py:125
  191.0 9.0 %collective-permute-start.43 = (bf16[32,3072]{1,0:T(8,128)(2,1)S(1)}, bf16[32,3072]{1,0:T(8,128)(2,1)S(1)}, u32[]{:S(2)}, u32[]{:S(2)}) collective-permute-start(bf16[32,3072]{1,0:T(8,128)(2,1)S(1)} %fusion.20), channel_id=1, source_target_pairs={{0,4},{1,6},{2,5},{3,7},{4,8},{5,10},{6,9},{7,11},{8,12},{9,14},{1... | collective-permute-start | bytes 589832 | tf_op jit(solution)/shard_map/ppermute | solution.py:125
  191.1 9.7 %collective-permute-start.42 = (bf16[32,3072]{1,0:T(8,128)(2,1)S(1)}, bf16[32,3072]{1,0:T(8,128)(2,1)S(1)}, u32[]{:S(2)}, u32[]{:S(2)}) collective-permute-start(bf16[32,3072]{1,0:T(8,128)(2,1)S(1)} %fusion.20), channel_id=1, source_target_pairs={{0,5},{1,4},{2,7},{3,6},{4,9},{5,8},{6,11},{7,10},{8,13},{9,12},{1... | collective-permute-start | bytes 589832 | tf_op jit(solution)/shard_map/ppermute | solution.py:125
  200.7 12.0 %collective-permute-start.41 = (bf16[32,3072]{1,0:T(8,128)(2,1)S(1)}, bf16[32,3072]{1,0:T(8,128)(2,1)S(1)}, u32[]{:S(2)}, u32[]{:S(2)}) collective-permute-start(bf16[32,3072]{1,0:T(8,128)(2,1)S(1)} %fusion.20), channel_id=1, source_target_pairs={{0,4},{1,5},{2,6},{3,7},{4,8},{5,9},{6,10},{7,11},{8,12},{9,13},{1... | collective-permute-start | bytes 589832 | tf_op jit(solution)/shard_map/ppermute | solution.py:125
  200.7 9.7 %collective-permute-start.46 = (bf16[32,3072]{1,0:T(8,128)(2,1)S(1)}, bf16[32,3072]{1,0:T(8,128)(2,1)S(1)}, u32[]{:S(2)}, u32[]{:S(2)}) collective-permute-start(bf16[32,3072]{1,0:T(8,128)(2,1)S(1)} %collective-permute-done.42.refs_1_), channel_id=1, source_target_pairs={{0,0},{1,2},{2,1},{3,3},{4,4},{5,6},{6,5},{7,7},{8,8},{9,10},{10,9... | collective-permute-start | bytes 589832 | tf_op jit(solution)/shard_map/ppermute | solution.py:125
  203.9 8.8 %collective-permute-start.45 = (bf16[32,3072]{1,0:T(8,128)(2,1)S(1)}, bf16[32,3072]{1,0:T(8,128)(2,1)S(1)}, u32[]{:S(2)}, u32[]{:S(2)}) collective-permute-start(bf16[32,3072]{1,0:T(8,128)(2,1)S(1)} %collective-permute-done.42.refs_1_), channel_id=1, source_target_pairs={{2,0},{1,3},{0,1},{3,2},{6,4},{5,7},{4,5},{7,6},{10,8},{9,11},{8,9... | collective-permute-start | bytes 589832 | tf_op jit(solution)/shard_map/ppermute | solution.py:125
  217.9 12.7 %collective-permute-start.48 = (bf16[32,3072]{1,0:T(8,128)(2,1)S(1)}, bf16[32,3072]{1,0:T(8,128)(2,1)S(1)}, u32[]{:S(2)}, u32[]{:S(2)}) collective-permute-start(bf16[32,3072]{1,0:T(8,128)(2,1)S(1)} %get-tuple-element.73), channel_id=1, source_target_pairs={{0,0},{1,2},{2,1},{3,3},{4,4},{5,6},{6,5},{7,7},{8,8},{9,10},{10,9... | collective-permute-start | bytes 589832 | tf_op jit(solution)/shard_map/ppermute | solution.py:125
  221.3 9.4 %collective-permute-start.47 = (bf16[32,3072]{1,0:T(8,128)(2,1)S(1)}, bf16[32,3072]{1,0:T(8,128)(2,1)S(1)}, u32[]{:S(2)}, u32[]{:S(2)}) collective-permute-start(bf16[32,3072]{1,0:T(8,128)(2,1)S(1)} %get-tuple-element.73), channel_id=1, source_target_pairs={{0,2},{3,1},{1,0},{2,3},{4,6},{7,5},{5,4},{6,7},{8,10},{11,9},{9,8... | collective-permute-start | bytes 589832 | tf_op jit(solution)/shard_map/ppermute | solution.py:125
  222.0 9.9 %collective-permute-start.50 = (bf16[32,3072]{1,0:T(8,128)(2,1)S(1)}, bf16[32,3072]{1,0:T(8,128)(2,1)S(1)}, u32[]{:S(2)}, u32[]{:S(2)}) collective-permute-start(bf16[32,3072]{1,0:T(8,128)(2,1)S(1)} %get-tuple-element.74), channel_id=1, source_target_pairs={{0,1},{1,0},{2,3},{3,2},{4,5},{5,4},{6,7},{7,6},{8,9},{9,8},{10,11... | collective-permute-start | bytes 589832 | tf_op jit(solution)/shard_map/ppermute | solution.py:125
  263.8 8.5 %collective-permute-start.58 = (bf16[32,3072]{1,0:T(8,128)(2,1)S(1)}, bf16[32,3072]{1,0:T(8,128)(2,1)S(1)}, u32[]{:S(2)}, u32[]{:S(2)}) collective-permute-start(bf16[32,3072]{1,0:T(8,128)(2,1)S(1)} %get-tuple-element.79), channel_id=1, source_target_pairs={{0,0},{1,2},{2,1},{3,3},{4,4},{5,6},{6,5},{7,7},{8,8},{9,10},{10,9... | collective-permute-start | bytes 589832 | tf_op jit(solution)/shard_map/ppermute | solution.py:125
  267.8 8.6 %collective-permute-start.57 = (bf16[32,3072]{1,0:T(8,128)(2,1)S(1)}, bf16[32,3072]{1,0:T(8,128)(2,1)S(1)}, u32[]{:S(2)}, u32[]{:S(2)}) collective-permute-start(bf16[32,3072]{1,0:T(8,128)(2,1)S(1)} %get-tuple-element.79), channel_id=1, source_target_pairs={{0,2},{3,1},{1,0},{2,3},{4,6},{7,5},{5,4},{6,7},{8,10},{11,9},{9,8... | collective-permute-start | bytes 589832 | tf_op jit(solution)/shard_map/ppermute | solution.py:125
  268.1 9.1 %collective-permute-start.60 = (bf16[32,3072]{1,0:T(8,128)(2,1)S(1)}, bf16[32,3072]{1,0:T(8,128)(2,1)S(1)}, u32[]{:S(2)}, u32[]{:S(2)}) collective-permute-start(bf16[32,3072]{1,0:T(8,128)(2,1)S(1)} %get-tuple-element.80), channel_id=1, source_target_pairs={{0,1},{1,0},{2,3},{3,2},{4,5},{5,4},{6,7},{7,6},{8,9},{9,8},{10,11... | collective-permute-start | bytes 589832 | tf_op jit(solution)/shard_map/ppermute | solution.py:125
  (33 other events, 264.7 us)

commit v5 on v3

--- a/solution.py
+++ b/solution.py
@@ -109,28 +109,39 @@
     return out[:chunks], out[chunks], out[chunks + 1]
 
 
-def send(block, turn, hop):
+STAY = ((0, 0), (1, 1), (2, 2), (3, 3))
+NEAR = ((0, 1), (1, 0), (2, 3), (3, 2))
+FAR = ((0, 3), (1, 2), (2, 1), (3, 0))
+
+
+def send(block, pairs, hop=0):
     sections = lax.axis_size("section")
     n = lax.axis_size("uly")
     route = [
-        (s * n + i, (s + hop) % sections * n + (i + turn) % n)
-        for s in range(sections)
-        for i in range(n)
+        (s * n + a, (s + hop) % sections * n + b) for s in range(sections) for a, b in pairs
     ]
     return lax.ppermute(block, ("section", "uly"), route)
 
 
-def gathered(own, hop):
-    n = lax.axis_size("uly")
-    first = own if hop == 0 else send(own, 0, hop)
-    return [first] + [send(own, k, hop) for k in range(1, n)]
-
-
-def summed(blocks):
+def summed(*blocks):
     total = blocks[0].astype(jnp.float32)
     for block in blocks[1:]:
         total = total + block.astype(jnp.float32)
     return total
+
+
+def gathered(own, hop=0):
+    far = send(own, FAR, hop)
+    near = send(own, NEAR, hop)
+    first = send(own, STAY, hop) if hop else own
+    return [first, near, far, send(far, NEAR)]
+
+
+def scattered(terms):
+    own, near, far, last = terms
+    pair = summed(far, send(last, NEAR)).astype(jnp.bfloat16)
+    near, pair = lax.optimization_barrier((near, pair))
+    return summed(own, send(near, NEAR), send(pair, FAR))
 
 
 def shards(
@@ -145,19 +156,18 @@
     n = lax.axis_size("uly")
     patch_rows = state.shape[1] * n
     own = state[0]
-    blocks = gathered(own, 0)
+    blocks = gathered(own)
     for tick in range(TICKS):
         slot = patch_slot[(section_index - tick) % section_count]
         for index in range(PASSES):
             applies = block_count > index
             info = jnp.stack([slot * patch_rows, applies.astype(jnp.int32)])
             terms, kc, vc = block_terms(info, blocks, norm_gain, w, wo, kc, vc)
-            arrived = [send(terms[k], n - k, 0) for k in range(1, n)]
-            updated = own.astype(jnp.float32) + summed([terms[0]] + arrived)
+            updated = own.astype(jnp.float32) + scattered(terms)
             updated = jnp.where(applies, updated.astype(jnp.bfloat16), own)
             last = index == PASSES - 1
             if last and tick == TICKS - 1:
-                return send(updated, 0, 1)[None]
+                return send(updated, STAY, 1)[None]
             blocks = gathered(updated, 1 if last else 0)
             own = blocks[0]
 

time: 261 us -> 233 us (0.89)
  the two profiles are of different devices: /device:TPU:0 before, /device:TPU:14 now
where the time goes in v5:
time: 233 us; the launch traced here: 234 us
  waiting for transfers between devices  134 us (58%)
  starting transfers between devices  59.2 us (25%)
  Pallas kernels  33.7 us (14%)
  between operations  2.82 us (1%)
    ppermute x39, waiting for transfers between devices, send(): return lax.ppermute(block, ('section', 'uly'), route)  134 us
    ppermute x39, starting transfers between devices, send(): return lax.ppermute(block, ('section', 'uly'), route)  59.2 us
    pallas_call x6, Pallas kernels, block_terms(): pl.pallas_call(functools.partial(block_kernel, chunks), out_shape=[jax.Sh...  29.8 us
  transfers between devices with their start and end apart: 39, of which 31 were waited for; matrix products, arithmetic and copies ran while one was open for 1% of the time, Pallas kernels for 2%

profile of v5, /device:TPU:14, one launch (start us, length us, event | category | flops | bytes accessed | tf_op | source)
XLA Modules:
  0.0 233.7 jit_solution(1730300500030590028)
XLA Ops:
  4.1 7.0 %collective-permute-done.1.refs_2_ = bf16[32,3072]{1,0:T(8,128)(2,1)S(1)} collective-permute-done((bf16[32,3072]{1,0:T(8,128)(2,1)}, bf16[32,3072]{1,0:T(8,128)(2,1)S(1)}, u32[]{:S(2)}, u32[]{:S(2)}) %collective-permute-start.1) | collective-permute-done | bytes 196640 | tf_op jit(solution)/shard_map/ppermute | solution.py:123
  13.8 3.9 %shard_map.82 = (bf16[3,3072,384]{2,1,0:T(8,128)(2,1)S(1)}, bf16[384,3072]{1,0:T(8,128)(2,1)S(1)}, bf16[512,384]{1,0:T(8,128)(2,1)S(1)}, bf16[512,384]{1,0:T(8,128)(2,1)S(1)}) custom-call(bf16[3,3072,384]{2,1,0:T(8,128)(2,1)} %bitcast.14, bf16[384,3072]{1,0:T(8,128)(2,1)} %bitcast.15, bf16[512,384]{1,0:T(8,128)(2,1)} %bitcast.16, bf16[512,384]{1,0:T(8,128)(2,1)} %bitcast.17), custom_call_target="tpu_custom_call" | custom-call | bytes 10223616 | tf_op jit(solution)/shard_map/pallas_call | solution.py:73
  17.8 4.9 %shard_map.83 = (bf16[32,3072]{1,0:T(8,128)(2,1)S(1)}, bf16[32,3072]{1,0:T(8,128)(2,1)S(1)}, bf16[32,3072]{1,0:T(8,128)(2,1)S(1)}, bf16[32,3072]{1,0:T(8,128)(2,...) custom-call(s32[2]{0:T(128)S(1)} %pad_add_fusion.1.info, ...), custom_call_target="tpu_custom_call", output_to_operand_aliasing={{4}: (8, {}), {5}: (9, {})} | custom-call | flops 1308622848 | bytes 9437184 | tf_op jit(solution)/shard_map/pallas_call | solution.py:94
  24.8 3.9 %collective-permute-done.3 = bf16[32,3072]{1,0:T(8,128)(2,1)S(1)} collective-permute-done((bf16[32,3072]{1,0:T(8,128)(2,1)S(1)}, bf16[32,3072]{1,0:T(8,128)(2,1)S(1)}, u32[]{:S(2)}, u32[]{:S(2)}) %collective-permute-start.3) | collective-permute-done | bytes 196640 | tf_op jit(solution)/shard_map/ppermute | solution.py:123
  39.5 4.1 %collective-permute-start.7 = (bf16[32,3072]{1,0:T(8,128)(2,1)S(1)}, bf16[32,3072]{1,0:T(8,128)(2,1)S(1)}, u32[]{:S(2)}, u32[]{:S(2)}) collective-permute-start(bf16[32,3072]{1,0:T(8,128)(2,1)S(1)} %fusion.refs_0_), channel_id=1, source_target_pairs={{0,3},{1,2},{2,1},{3,0},{4,7},{5,6},{6,5},{7,4},{8,11},{9,10},{10,... | collective-permute-start | bytes 589832 | tf_op jit(solution)/shard_map/ppermute | solution.py:123
  43.6 4.8 %collective-permute-done.7.refs_2_ = bf16[32,3072]{1,0:T(8,128)(2,1)S(1)} collective-permute-done((bf16[32,3072]{1,0:T(8,128)(2,1)S(1)}, bf16[32,3072]{1,0:T(8,128)(2,1)S(1)}, u32[]{:S(2)}, u32[]{:S(2)}) %collective-permute-start.7) | collective-permute-done | bytes 196640 | tf_op jit(solution)/shard_map/ppermute | solution.py:123
  50.1 3.9 %collective-permute-done.8.refs_3_ = bf16[32,3072]{1,0:T(8,128)(2,1)S(1)} collective-permute-done((bf16[32,3072]{1,0:T(8,128)(2,1)S(1)}, bf16[32,3072]{1,0:T(8,128)(2,1)S(1)}, u32[]{:S(2)}, u32[]{:S(2)}) %collective-permute-start.8) | collective-permute-done | bytes 196640 | tf_op jit(solution)/shard_map/ppermute | solution.py:123
  54.0 4.9 %shard_map.84 = (bf16[32,3072]{1,0:T(8,128)(2,1)S(1)}, bf16[32,3072]{1,0:T(8,128)(2,1)S(1)}, bf16[32,3072]{1,0:T(8,128)(2,1)S(1)}, bf16[32,3072]{1,0:T(8,128)(2,...) custom-call(s32[2]{0:T(128)S(1)} %pad_add_fusion.info, ...), custom_call_target="tpu_custom_call", output_to_operand_aliasing={{4}: (8, {}), {5}: (9, {})} | custom-call | flops 1308622848 | bytes 9437184 | tf_op jit(solution)/shard_map/pallas_call | solution.py:94
  59.0 7.8 %collective-permute-done.9 = bf16[32,3072]{1,0:T(8,128)(2,1)S(1)} collective-permute-done((bf16[32,3072]{1,0:T(8,128)(2,1)S(1)}, bf16[32,3072]{1,0:T(8,128)(2,1)S(1)}, u32[]{:S(2)}, u32[]{:S(2)}) %collective-permute-start.9) | collective-permute-done | bytes 196640 | tf_op jit(solution)/shard_map/ppermute | solution.py:123
  68.1 4.5 %collective-permute-done.10 = bf16[32,3072]{1,0:T(8,128)(2,1)S(1)} collective-permute-done((bf16[32,3072]{1,0:T(8,128)(2,1)S(1)}, bf16[32,3072]{1,0:T(8,128)(2,1)S(1)}, u32[]{:S(2)}, u32[]{:S(2)}) %collective-permute-start.10) | collective-permute-done | bytes 196640 | tf_op jit(solution)/shard_map/ppermute | solution.py:123
  75.7 6.9 %collective-permute-done.14.refs_2_ = bf16[32,3072]{1,0:T(8,128)(2,1)S(1)} collective-permute-done((bf16[32,3072]{1,0:T(8,128)(2,1)S(1)}, bf16[32,3072]{1,0:T(8,128)(2,1)S(1)}, u32[]{:S(2)}, u32[]{:S(2)}) %collective-permute-start.14) | collective-permute-done | bytes 196640 | tf_op jit(solution)/shard_map/ppermute | solution.py:123
  82.6 4.3 %collective-permute-start.15 = (bf16[32,3072]{1,0:T(8,128)(2,1)S(1)}, bf16[32,3072]{1,0:T(8,128)(2,1)S(1)}, u32[]{:S(2)}, u32[]{:S(2)}) collective-permute-start(bf16[32,3072]{1,0:T(8,128)(2,1)S(1)} %collective-permute-done.14.refs_2_), channel_id=1, source_target_pairs={{0,1},{1,0},{2,3},{3,2},{4,5},{5,4},{6,7},{7,6},{8,9},{9,8},{10,11... | collective-permute-start | bytes 589832 | tf_op jit(solution)/shard_map/ppermute | solution.py:123
  90.6 5.1 %shard_map.85 = (bf16[32,3072]{1,0:T(8,128)(2,1)S(1)}, bf16[32,3072]{1,0:T(8,128)(2,1)S(1)}, bf16[32,3072]{1,0:T(8,128)(2,1)S(1)}, bf16[32,3072]{1,0:T(8,128)(2,...) custom-call(s32[2]{0:T(128)S(1)} %pad_add_fusion.3.info, ...), custom_call_target="tpu_custom_call", output_to_operand_aliasing={{4}: (8, {}), {5}: (9, {})} | custom-call | flops 1308622848 | bytes 9437184 | tf_op jit(solution)/shard_map/pallas_call | solution.py:94
  97.7 5.1 %collective-permute-done.16 = bf16[32,3072]{1,0:T(8,128)(2,1)S(1)} collective-permute-done((bf16[32,3072]{1,0:T(8,128)(2,1)S(1)}, bf16[32,3072]{1,0:T(8,128)(2,1)S(1)}, u32[]{:S(2)}, u32[]{:S(2)}) %collective-permute-start.16) | collective-permute-done | bytes 196640 | tf_op jit(solution)/shard_map/ppermute | solution.py:123
  102.9 4.6 %collective-permute-start.17 = (bf16[32,3072]{1,0:T(8,128)(2,1)S(1)}, bf16[32,3072]{1,0:T(8,128)(2,1)S(1)}, u32[]{:S(2)}, u32[]{:S(2)}) collective-permute-start(bf16[32,3072]{1,0:T(8,128)(2,1)S(1)} %get-tuple-element.79), channel_id=1, source_target_pairs={{0,1},{1,0},{2,3},{3,2},{4,5},{5,4},{6,7},{7,6},{8,9},{9,8},{10,11... | collective-permute-start | bytes 589832 | tf_op jit(solution)/shard_map/ppermute | solution.py:123
  107.5 8.8 %collective-permute-done.17 = bf16[32,3072]{1,0:T(8,128)(2,1)S(1)} collective-permute-done((bf16[32,3072]{1,0:T(8,128)(2,1)S(1)}, bf16[32,3072]{1,0:T(8,128)(2,1)S(1)}, u32[]{:S(2)}, u32[]{:S(2)}) %collective-permute-start.17) | collective-permute-done | bytes 196640 | tf_op jit(solution)/shard_map/ppermute | solution.py:123
  122.4 4.2 %collective-permute-start.21 = (bf16[32,3072]{1,0:T(8,128)(2,1)S(1)}, bf16[32,3072]{1,0:T(8,128)(2,1)S(1)}, u32[]{:S(2)}, u32[]{:S(2)}) collective-permute-start(bf16[32,3072]{1,0:T(8,128)(2,1)S(1)} %collective-permute-done.20.refs_2_), channel_id=1, source_target_pairs={{0,1},{1,0},{2,3},{3,2},{4,5},{5,4},{6,7},{7,6},{8,9},{9,8},{10,11... | collective-permute-start | bytes 589832 | tf_op jit(solution)/shard_map/ppermute | solution.py:123
  126.6 4.8 %collective-permute-done.21.refs_3_ = bf16[32,3072]{1,0:T(8,128)(2,1)S(1)} collective-permute-done((bf16[32,3072]{1,0:T(8,128)(2,1)S(1)}, bf16[32,3072]{1,0:T(8,128)(2,1)S(1)}, u32[]{:S(2)}, u32[]{:S(2)}) %collective-permute-start.21) | collective-permute-done | bytes 196640 | tf_op jit(solution)/shard_map/ppermute | solution.py:123
  131.4 4.9 %shard_map.86 = (bf16[32,3072]{1,0:T(8,128)(2,1)S(1)}, bf16[32,3072]{1,0:T(8,128)(2,1)S(1)}, bf16[32,3072]{1,0:T(8,128)(2,1)S(1)}, bf16[32,3072]{1,0:T(8,128)(2,...) custom-call(s32[2]{0:T(128)S(1)} %pad_add_fusion.2.info, ...), custom_call_target="tpu_custom_call", output_to_operand_aliasing={{4}: (8, {}), {5}: (9, {})} | custom-call | flops 1308622848 | bytes 9437184 | tf_op jit(solution)/shard_map/pallas_call | solution.py:94
  138.1 3.9 %collective-permute-done.22 = bf16[32,3072]{1,0:T(8,128)(2,1)S(1)} collective-permute-done((bf16[32,3072]{1,0:T(8,128)(2,1)S(1)}, bf16[32,3072]{1,0:T(8,128)(2,1)S(1)}, u32[]{:S(2)}, u32[]{:S(2)}) %collective-permute-start.22) | collective-permute-done | bytes 196640 | tf_op jit(solution)/shard_map/ppermute | solution.py:123
  147.9 7.9 %collective-permute-done.24 = bf16[32,3072]{1,0:T(8,128)(2,1)S(1)} collective-permute-done((bf16[32,3072]{1,0:T(8,128)(2,1)S(1)}, bf16[32,3072]{1,0:T(8,128)(2,1)S(1)}, u32[]{:S(2)}, u32[]{:S(2)}) %collective-permute-start.24) | collective-permute-done | bytes 196640 | tf_op jit(solution)/shard_map/ppermute | solution.py:123
  156.1 7.8 %collective-permute-done.27.refs_2_ = bf16[32,3072]{1,0:T(8,128)(2,1)S(1)} collective-permute-done((bf16[32,3072]{1,0:T(8,128)(2,1)S(1)}, bf16[32,3072]{1,0:T(8,128)(2,1)S(1)}, u32[]{:S(2)}, u32[]{:S(2)}) %collective-permute-start.27) | collective-permute-done | bytes 196640 | tf_op jit(solution)/shard_map/ppermute | solution.py:123
  165.4 4.2 %collective-permute-done.28.refs_3_ = bf16[32,3072]{1,0:T(8,128)(2,1)S(1)} collective-permute-done((bf16[32,3072]{1,0:T(8,128)(2,1)S(1)}, bf16[32,3072]{1,0:T(8,128)(2,1)S(1)}, u32[]{:S(2)}, u32[]{:S(2)}) %collective-permute-start.28) | collective-permute-done | bytes 196640 | tf_op jit(solution)/shard_map/ppermute | solution.py:123
  169.6 5.1 %shard_map.87 = (bf16[32,3072]{1,0:T(8,128)(2,1)S(1)}, bf16[32,3072]{1,0:T(8,128)(2,1)S(1)}, bf16[32,3072]{1,0:T(8,128)(2,1)S(1)}, bf16[32,3072]{1,0:T(8,128)(2,...) custom-call(s32[2]{0:T(128)S(1)} %pad_add_fusion.5.info, ...), custom_call_target="tpu_custom_call", output_to_operand_aliasing={{4}: (8, {}), {5}: (9, {})} | custom-call | flops 1308622848 | bytes 9437184 | tf_op jit(solution)/shard_map/pallas_call | solution.py:94
  174.8 7.7 %collective-permute-done.29 = bf16[32,3072]{1,0:T(8,128)(2,1)S(1)} collective-permute-done((bf16[32,3072]{1,0:T(8,128)(2,1)S(1)}, bf16[32,3072]{1,0:T(8,128)(2,1)S(1)}, u32[]{:S(2)}, u32[]{:S(2)}) %collective-permute-start.29) | collective-permute-done | bytes 196640 | tf_op jit(solution)/shard_map/ppermute | solution.py:123
  184.1 4.3 %collective-permute-done.30 = bf16[32,3072]{1,0:T(8,128)(2,1)S(1)} collective-permute-done((bf16[32,3072]{1,0:T(8,128)(2,1)S(1)}, bf16[32,3072]{1,0:T(8,128)(2,1)S(1)}, u32[]{:S(2)}, u32[]{:S(2)}) %collective-permute-start.30) | collective-permute-done | bytes 196640 | tf_op jit(solution)/shard_map/ppermute | solution.py:123
  189.9 6.8 %collective-permute-start.32 = (bf16[32,3072]{1,0:T(8,128)(2,1)S(1)}, bf16[32,3072]{1,0:T(8,128)(2,1)S(1)}, u32[]{:S(2)}, u32[]{:S(2)}) collective-permute-start(bf16[32,3072]{1,0:T(8,128)(2,1)S(1)} %fusion.4.refs_0_), channel_id=1, source_target_pairs={{0,1},{1,0},{2,3},{3,2},{4,5},{5,4},{6,7},{7,6},{8,9},{9,8},{10,11... | collective-permute-start | bytes 589832 | tf_op jit(solution)/shard_map/ppermute | solution.py:123
  196.7 5.7 %collective-permute-start.34 = (bf16[32,3072]{1,0:T(8,128)(2,1)S(1)}, bf16[32,3072]{1,0:T(8,128)(2,1)S(1)}, u32[]{:S(2)}, u32[]{:S(2)}) collective-permute-start(bf16[32,3072]{1,0:T(8,128)(2,1)S(1)} %collective-permute-done.33.refs_2_), channel_id=1, source_target_pairs={{0,1},{1,0},{2,3},{3,2},{4,5},{5,4},{6,7},{7,6},{8,9},{9,8},{10,11... | collective-permute-start | bytes 589832 | tf_op jit(solution)/shard_map/ppermute | solution.py:123
  202.4 4.4 %collective-permute-done.34.refs_3_ = bf16[32,3072]{1,0:T(8,128)(2,1)S(1)} collective-permute-done((bf16[32,3072]{1,0:T(8,128)(2,1)S(1)}, bf16[32,3072]{1,0:T(8,128)(2,1)S(1)}, u32[]{:S(2)}, u32[]{:S(2)}) %collective-permute-start.34) | collective-permute-done | bytes 196640 | tf_op jit(solution)/shard_map/ppermute | solution.py:123
  206.8 4.9 %shard_map.88 = (bf16[32,3072]{1,0:T(8,128)(2,1)S(1)}, bf16[32,3072]{1,0:T(8,128)(2,1)S(1)}, bf16[32,3072]{1,0:T(8,128)(2,1)S(1)}, bf16[32,3072]{1,0:T(8,128)(2,...) custom-call(s32[2]{0:T(128)S(1)} %pad_add_fusion.4.info, ...), custom_call_target="tpu_custom_call", output_to_operand_aliasing={{4}: (8, {}), {5}: (9, {})} | custom-call | flops 1308622848 | bytes 9437184 | tf_op jit(solution)/shard_map/pallas_call | solution.py:94
  223.6 4.1 %collective-permute-done.37 = bf16[32,3072]{1,0:T(8,128)(2,1)S(1)} collective-permute-done((bf16[32,3072]{1,0:T(8,128)(2,1)S(1)}, bf16[32,3072]{1,0:T(8,128)(2,1)S(1)}, u32[]{:S(2)}, u32[]{:S(2)}) %collective-permute-start.37) | collective-permute-done | bytes 196640 | tf_op jit(solution)/shard_map/ppermute | solution.py:123
  227.9 5.1 %collective-permute-done.38 = bf16[32,3072]{1,0:T(8,128)(2,1)S(1)} collective-permute-done((bf16[32,3072]{1,0:T(8,128)(2,1)S(1)}, bf16[32,3072]{1,0:T(8,128)(2,1)S(1)}, u32[]{:S(2)}, u32[]{:S(2)}) %collective-permute-start.38) | collective-permute-done | bytes 196640 | tf_op jit(solution)/shard_map/ppermute | solution.py:123
  (77 shorter events, 60.7 us)
Async XLA Ops:
  0.0 11.1 %collective-permute-start.1 = (bf16[32,3072]{1,0:T(8,128)(2,1)}, bf16[32,3072]{1,0:T(8,128)(2,1)S(1)}, u32[]{:S(2)}, u32[]{:S(2)}) collective-permute-start(bf16[32,3072]{1,0:T(8,128)(2,1)} %bitcast.11), channel_id=1, source_target_pairs={{0,3},{1,2},{2,1},{3,0},{4,7},{5,6},{6,5},{7,4},{8,11},{9,10},{10,... | collective-permute-start | bytes 589832 | tf_op jit(solution)/shard_map/ppermute | solution.py:123
  1.6 16.2 %collective-permute-start = (bf16[32,3072]{1,0:T(8,128)(2,1)}, bf16[32,3072]{1,0:T(8,128)(2,1)S(1)}, u32[]{:S(2)}, u32[]{:S(2)}) collective-permute-start(bf16[32,3072]{1,0:T(8,128)(2,1)} %bitcast.12), channel_id=1, source_target_pairs={{0,1},{1,0},{2,3},{3,2},{4,5},{5,4},{6,7},{7,6},{8,9},{9,8},{10,11... | collective-permute-start | bytes 589832 | tf_op jit(solution)/shard_map/ppermute | solution.py:123
  11.1 6.7 %collective-permute-start.2 = (bf16[32,3072]{1,0:T(8,128)(2,1)S(1)}, bf16[32,3072]{1,0:T(8,128)(2,1)S(1)}, u32[]{:S(2)}, u32[]{:S(2)}) collective-permute-start(bf16[32,3072]{1,0:T(8,128)(2,1)S(1)} %collective-permute-done.1.refs_2_), channel_id=1, source_target_pairs={{0,1},{1,0},{2,3},{3,2},{4,5},{5,4},{6,7},{7,6},{8,9},{9,8},{10,11... | collective-permute-start | bytes 589832 | tf_op jit(solution)/shard_map/ppermute | solution.py:123
  22.7 6.0 %collective-permute-start.3 = (bf16[32,3072]{1,0:T(8,128)(2,1)S(1)}, bf16[32,3072]{1,0:T(8,128)(2,1)S(1)}, u32[]{:S(2)}, u32[]{:S(2)}) collective-permute-start(bf16[32,3072]{1,0:T(8,128)(2,1)S(1)} %get-tuple-element.62), channel_id=1, source_target_pairs={{0,1},{1,0},{2,3},{3,2},{4,5},{5,4},{6,7},{7,6},{8,9},{9,8},{10,11... | collective-permute-start | bytes 589832 | tf_op jit(solution)/shard_map/ppermute | solution.py:123
  28.7 7.1 %collective-permute-start.4 = (bf16[32,3072]{1,0:T(8,128)(2,1)S(1)}, bf16[32,3072]{1,0:T(8,128)(2,1)S(1)}, u32[]{:S(2)}, u32[]{:S(2)}) collective-permute-start(bf16[32,3072]{1,0:T(8,128)(2,1)S(1)} %get-tuple-element.63), channel_id=1, source_target_pairs={{0,1},{1,0},{2,3},{3,2},{4,5},{5,4},{6,7},{7,6},{8,9},{9,8},{10,11... | collective-permute-start | bytes 589832 | tf_op jit(solution)/shard_map/ppermute | solution.py:123
  30.6 8.8 %collective-permute-start.5 = (bf16[32,3072]{1,0:T(8,128)(2,1)S(1)}, bf16[32,3072]{1,0:T(8,128)(2,1)S(1)}, u32[]{:S(2)}, u32[]{:S(2)}) collective-permute-start(bf16[32,3072]{1,0:T(8,128)(2,1)S(1)} %add_convert_fusion.11), channel_id=1, source_target_pairs={{0,3},{1,2},{2,1},{3,0},{4,7},{5,6},{6,5},{7,4},{8,11},{9,10},{10,... | collective-permute-start | bytes 589832 | tf_op jit(solution)/shard_map/ppermute | solution.py:123
  39.5 8.9 %collective-permute-start.7 = (bf16[32,3072]{1,0:T(8,128)(2,1)S(1)}, bf16[32,3072]{1,0:T(8,128)(2,1)S(1)}, u32[]{:S(2)}, u32[]{:S(2)}) collective-permute-start(bf16[32,3072]{1,0:T(8,128)(2,1)S(1)} %fusion.refs_0_), channel_id=1, source_target_pairs={{0,3},{1,2},{2,1},{3,0},{4,7},{5,6},{6,5},{7,4},{8,11},{9,10},{10,... | collective-permute-start | bytes 589832 | tf_op jit(solution)/shard_map/ppermute | solution.py:123
  43.6 6.5 %collective-permute-start.6 = (bf16[32,3072]{1,0:T(8,128)(2,1)S(1)}, bf16[32,3072]{1,0:T(8,128)(2,1)S(1)}, u32[]{:S(2)}, u32[]{:S(2)}) collective-permute-start(bf16[32,3072]{1,0:T(8,128)(2,1)S(1)} %fusion.refs_0_), channel_id=1, source_target_pairs={{0,1},{1,0},{2,3},{3,2},{4,5},{5,4},{6,7},{7,6},{8,9},{9,8},{10,11... | collective-permute-start | bytes 589832 | tf_op jit(solution)/shard_map/ppermute | solution.py:123
  58.9 7.8 %collective-permute-start.9 = (bf16[32,3072]{1,0:T(8,128)(2,1)S(1)}, bf16[32,3072]{1,0:T(8,128)(2,1)S(1)}, u32[]{:S(2)}, u32[]{:S(2)}) collective-permute-start(bf16[32,3072]{1,0:T(8,128)(2,1)S(1)} %get-tuple-element.70), channel_id=1, source_target_pairs={{0,1},{1,0},{2,3},{3,2},{4,5},{5,4},{6,7},{7,6},{8,9},{9,8},{10,11... | collective-permute-start | bytes 589832 | tf_op jit(solution)/shard_map/ppermute | solution.py:123
  66.9 8.5 %collective-permute-start.11 = (bf16[32,3072]{1,0:T(8,128)(2,1)S(1)}, bf16[32,3072]{1,0:T(8,128)(2,1)S(1)}, u32[]{:S(2)}, u32[]{:S(2)}) collective-permute-start(bf16[32,3072]{1,0:T(8,128)(2,1)S(1)} %add_convert_fusion.9), channel_id=1, source_target_pairs={{0,3},{1,2},{2,1},{3,0},{4,7},{5,6},{6,5},{7,4},{8,11},{9,10},{10,... | collective-permute-start | bytes 589832 | tf_op jit(solution)/shard_map/ppermute | solution.py:123
  75.5 7.1 %collective-permute-start.14 = (bf16[32,3072]{1,0:T(8,128)(2,1)S(1)}, bf16[32,3072]{1,0:T(8,128)(2,1)S(1)}, u32[]{:S(2)}, u32[]{:S(2)}) collective-permute-start(bf16[32,3072]{1,0:T(8,128)(2,1)S(1)} %fusion.1), channel_id=1, source_target_pairs={{0,7},{1,6},{2,5},{3,4},{4,11},{5,10},{6,9},{7,8},{8,15},{9,14},{1... | collective-permute-start | bytes 589832 | tf_op jit(solution)/shard_map/ppermute | solution.py:123
  75.6 12.0 %collective-permute-start.13 = (bf16[32,3072]{1,0:T(8,128)(2,1)S(1)}, bf16[32,3072]{1,0:T(8,128)(2,1)S(1)}, u32[]{:S(2)}, u32[]{:S(2)}) collective-permute-start(bf16[32,3072]{1,0:T(8,128)(2,1)S(1)} %fusion.1), channel_id=1, source_target_pairs={{0,5},{1,4},{2,7},{3,6},{4,9},{5,8},{6,11},{7,10},{8,13},{9,12},{1... | collective-permute-start | bytes 589832 | tf_op jit(solution)/shard_map/ppermute | solution.py:123
  75.7 12.0 %collective-permute-start.12 = (bf16[32,3072]{1,0:T(8,128)(2,1)S(1)}, bf16[32,3072]{1,0:T(8,128)(2,1)S(1)}, u32[]{:S(2)}, u32[]{:S(2)}) collective-permute-start(bf16[32,3072]{1,0:T(8,128)(2,1)S(1)} %fusion.1), channel_id=1, source_target_pairs={{0,4},{1,5},{2,6},{3,7},{4,8},{5,9},{6,10},{7,11},{8,12},{9,13},{1... | collective-permute-start | bytes 589832 | tf_op jit(solution)/shard_map/ppermute | solution.py:123
  82.6 7.9 %collective-permute-start.15 = (bf16[32,3072]{1,0:T(8,128)(2,1)S(1)}, bf16[32,3072]{1,0:T(8,128)(2,1)S(1)}, u32[]{:S(2)}, u32[]{:S(2)}) collective-permute-start(bf16[32,3072]{1,0:T(8,128)(2,1)S(1)} %collective-permute-done.14.refs_2_), channel_id=1, source_target_pairs={{0,1},{1,0},{2,3},{3,2},{4,5},{5,4},{6,7},{7,6},{8,9},{9,8},{10,11... | collective-permute-start | bytes 589832 | tf_op jit(solution)/shard_map/ppermute | solution.py:123
  95.6 7.2 %collective-permute-start.16 = (bf16[32,3072]{1,0:T(8,128)(2,1)S(1)}, bf16[32,3072]{1,0:T(8,128)(2,1)S(1)}, u32[]{:S(2)}, u32[]{:S(2)}) collective-permute-start(bf16[32,3072]{1,0:T(8,128)(2,1)S(1)} %get-tuple-element.78), channel_id=1, source_target_pairs={{0,1},{1,0},{2,3},{3,2},{4,5},{5,4},{6,7},{7,6},{8,9},{9,8},{10,11... | collective-permute-start | bytes 589832 | tf_op jit(solution)/shard_map/ppermute | solution.py:123
  102.9 13.4 %collective-permute-start.17 = (bf16[32,3072]{1,0:T(8,128)(2,1)S(1)}, bf16[32,3072]{1,0:T(8,128)(2,1)S(1)}, u32[]{:S(2)}, u32[]{:S(2)}) collective-permute-start(bf16[32,3072]{1,0:T(8,128)(2,1)S(1)} %get-tuple-element.79), channel_id=1, source_target_pairs={{0,1},{1,0},{2,3},{3,2},{4,5},{5,4},{6,7},{7,6},{8,9},{9,8},{10,11... | collective-permute-start | bytes 589832 | tf_op jit(solution)/shard_map/ppermute | solution.py:123
  107.5 9.0 %collective-permute-start.18 = (bf16[32,3072]{1,0:T(8,128)(2,1)S(1)}, bf16[32,3072]{1,0:T(8,128)(2,1)S(1)}, u32[]{:S(2)}, u32[]{:S(2)}) collective-permute-start(bf16[32,3072]{1,0:T(8,128)(2,1)S(1)} %add_convert_fusion.7), channel_id=1, source_target_pairs={{0,3},{1,2},{2,1},{3,0},{4,7},{5,6},{6,5},{7,4},{8,11},{9,10},{10,... | collective-permute-start | bytes 589832 | tf_op jit(solution)/shard_map/ppermute | solution.py:123
  116.6 5.7 %collective-permute-start.20 = (bf16[32,3072]{1,0:T(8,128)(2,1)S(1)}, bf16[32,3072]{1,0:T(8,128)(2,1)S(1)}, u32[]{:S(2)}, u32[]{:S(2)}) collective-permute-start(bf16[32,3072]{1,0:T(8,128)(2,1)S(1)} %fusion.2.refs_0_), channel_id=1, source_target_pairs={{0,3},{1,2},{2,1},{3,0},{4,7},{5,6},{6,5},{7,4},{8,11},{9,10},{10,... | collective-permute-start | bytes 589832 | tf_op jit(solution)/shard_map/ppermute | solution.py:123
  117.0 9.6 %collective-permute-start.19 = (bf16[32,3072]{1,0:T(8,128)(2,1)S(1)}, bf16[32,3072]{1,0:T(8,128)(2,1)S(1)}, u32[]{:S(2)}, u32[]{:S(2)}) collective-permute-start(bf16[32,3072]{1,0:T(8,128)(2,1)S(1)} %fusion.2.refs_0_), channel_id=1, source_target_pairs={{0,1},{1,0},{2,3},{3,2},{4,5},{5,4},{6,7},{7,6},{8,9},{9,8},{10,11... | collective-permute-start | bytes 589832 | tf_op jit(solution)/shard_map/ppermute | solution.py:123
  122.4 9.1 %collective-permute-start.21 = (bf16[32,3072]{1,0:T(8,128)(2,1)S(1)}, bf16[32,3072]{1,0:T(8,128)(2,1)S(1)}, u32[]{:S(2)}, u32[]{:S(2)}) collective-permute-start(bf16[32,3072]{1,0:T(8,128)(2,1)S(1)} %collective-permute-done.20.refs_2_), channel_id=1, source_target_pairs={{0,1},{1,0},{2,3},{3,2},{4,5},{5,4},{6,7},{7,6},{8,9},{9,8},{10,11... | collective-permute-start | bytes 589832 | tf_op jit(solution)/shard_map/ppermute | solution.py:123
  143.9 11.8 %collective-permute-start.24 = (bf16[32,3072]{1,0:T(8,128)(2,1)S(1)}, bf16[32,3072]{1,0:T(8,128)(2,1)S(1)}, u32[]{:S(2)}, u32[]{:S(2)}) collective-permute-start(bf16[32,3072]{1,0:T(8,128)(2,1)S(1)} %add_convert_fusion.5), channel_id=1, source_target_pairs={{0,3},{1,2},{2,1},{3,0},{4,7},{5,6},{6,5},{7,4},{8,11},{9,10},{10,... | collective-permute-start | bytes 589832 | tf_op jit(solution)/shard_map/ppermute | solution.py:123
  155.9 8.0 %collective-permute-start.27 = (bf16[32,3072]{1,0:T(8,128)(2,1)S(1)}, bf16[32,3072]{1,0:T(8,128)(2,1)S(1)}, u32[]{:S(2)}, u32[]{:S(2)}) collective-permute-start(bf16[32,3072]{1,0:T(8,128)(2,1)S(1)} %fusion.3), channel_id=1, source_target_pairs={{0,7},{1,6},{2,5},{3,4},{4,11},{5,10},{6,9},{7,8},{8,15},{9,14},{1... | collective-permute-start | bytes 589832 | tf_op jit(solution)/shard_map/ppermute | solution.py:123
  156.0 8.7 %collective-permute-start.26 = (bf16[32,3072]{1,0:T(8,128)(2,1)S(1)}, bf16[32,3072]{1,0:T(8,128)(2,1)S(1)}, u32[]{:S(2)}, u32[]{:S(2)}) collective-permute-start(bf16[32,3072]{1,0:T(8,128)(2,1)S(1)} %fusion.3), channel_id=1, source_target_pairs={{0,5},{1,4},{2,7},{3,6},{4,9},{5,8},{6,11},{7,10},{8,13},{9,12},{1... | collective-permute-start | bytes 589832 | tf_op jit(solution)/shard_map/ppermute | solution.py:123
  156.0 9.4 %collective-permute-start.25 = (bf16[32,3072]{1,0:T(8,128)(2,1)S(1)}, bf16[32,3072]{1,0:T(8,128)(2,1)S(1)}, u32[]{:S(2)}, u32[]{:S(2)}) collective-permute-start(bf16[32,3072]{1,0:T(8,128)(2,1)S(1)} %fusion.3), channel_id=1, source_target_pairs={{0,4},{1,5},{2,6},{3,7},{4,8},{5,9},{6,10},{7,11},{8,12},{9,13},{1... | collective-permute-start | bytes 589832 | tf_op jit(solution)/shard_map/ppermute | solution.py:123
  174.7 7.8 %collective-permute-start.29 = (bf16[32,3072]{1,0:T(8,128)(2,1)S(1)}, bf16[32,3072]{1,0:T(8,128)(2,1)S(1)}, u32[]{:S(2)}, u32[]{:S(2)}) collective-permute-start(bf16[32,3072]{1,0:T(8,128)(2,1)S(1)} %get-tuple-element.94), channel_id=1, source_target_pairs={{0,1},{1,0},{2,3},{3,2},{4,5},{5,4},{6,7},{7,6},{8,9},{9,8},{10,11... | collective-permute-start | bytes 589832 | tf_op jit(solution)/shard_map/ppermute | solution.py:123
  182.6 5.8 %collective-permute-start.30 = (bf16[32,3072]{1,0:T(8,128)(2,1)S(1)}, bf16[32,3072]{1,0:T(8,128)(2,1)S(1)}, u32[]{:S(2)}, u32[]{:S(2)}) collective-permute-start(bf16[32,3072]{1,0:T(8,128)(2,1)S(1)} %get-tuple-element.95), channel_id=1, source_target_pairs={{0,1},{1,0},{2,3},{3,2},{4,5},{5,4},{6,7},{7,6},{8,9},{9,8},{10,11... | collective-permute-start | bytes 589832 | tf_op jit(solution)/shard_map/ppermute | solution.py:123
  182.6 6.3 %collective-permute-start.31 = (bf16[32,3072]{1,0:T(8,128)(2,1)S(1)}, bf16[32,3072]{1,0:T(8,128)(2,1)S(1)}, u32[]{:S(2)}, u32[]{:S(2)}) collective-permute-start(bf16[32,3072]{1,0:T(8,128)(2,1)S(1)} %add_convert_fusion.3), channel_id=1, source_target_pairs={{0,3},{1,2},{2,1},{3,0},{4,7},{5,6},{6,5},{7,4},{8,11},{9,10},{10,... | collective-permute-start | bytes 589832 | tf_op jit(solution)/shard_map/ppermute | solution.py:123
  189.1 7.6 %collective-permute-start.33 = (bf16[32,3072]{1,0:T(8,128)(2,1)S(1)}, bf16[32,3072]{1,0:T(8,128)(2,1)S(1)}, u32[]{:S(2)}, u32[]{:S(2)}) collective-permute-start(bf16[32,3072]{1,0:T(8,128)(2,1)S(1)} %fusion.4.refs_0_), channel_id=1, source_target_pairs={{0,3},{1,2},{2,1},{3,0},{4,7},{5,6},{6,5},{7,4},{8,11},{9,10},{10,... | collective-permute-start | bytes 589832 | tf_op jit(solution)/shard_map/ppermute | solution.py:123
  189.9 12.5 %collective-permute-start.32 = (bf16[32,3072]{1,0:T(8,128)(2,1)S(1)}, bf16[32,3072]{1,0:T(8,128)(2,1)S(1)}, u32[]{:S(2)}, u32[]{:S(2)}) collective-permute-start(bf16[32,3072]{1,0:T(8,128)(2,1)S(1)} %fusion.4.refs_0_), channel_id=1, source_target_pairs={{0,1},{1,0},{2,3},{3,2},{4,5},{5,4},{6,7},{7,6},{8,9},{9,8},{10,11... | collective-permute-start | bytes 589832 | tf_op jit(solution)/shard_map/ppermute | solution.py:123
  196.7 10.1 %collective-permute-start.34 = (bf16[32,3072]{1,0:T(8,128)(2,1)S(1)}, bf16[32,3072]{1,0:T(8,128)(2,1)S(1)}, u32[]{:S(2)}, u32[]{:S(2)}) collective-permute-start(bf16[32,3072]{1,0:T(8,128)(2,1)S(1)} %collective-permute-done.33.refs_2_), channel_id=1, source_target_pairs={{0,1},{1,0},{2,3},{3,2},{4,5},{5,4},{6,7},{7,6},{8,9},{9,8},{10,11... | collective-permute-start | bytes 589832 | tf_op jit(solution)/shard_map/ppermute | solution.py:123
  211.7 6.1 %collective-permute-start.35 = (bf16[32,3072]{1,0:T(8,128)(2,1)S(1)}, bf16[32,3072]{1,0:T(8,128)(2,1)S(1)}, u32[]{:S(2)}, u32[]{:S(2)}) collective-permute-start(bf16[32,3072]{1,0:T(8,128)(2,1)S(1)} %get-tuple-element.102), channel_id=1, source_target_pairs={{0,1},{1,0},{2,3},{3,2},{4,5},{5,4},{6,7},{7,6},{8,9},{9,8},{10,11... | collective-permute-start | bytes 589832 | tf_op jit(solution)/shard_map/ppermute | solution.py:123
  219.9 7.8 %collective-permute-start.37 = (bf16[32,3072]{1,0:T(8,128)(2,1)S(1)}, bf16[32,3072]{1,0:T(8,128)(2,1)S(1)}, u32[]{:S(2)}, u32[]{:S(2)}) collective-permute-start(bf16[32,3072]{1,0:T(8,128)(2,1)S(1)} %add_convert_fusion.1), channel_id=1, source_target_pairs={{0,3},{1,2},{2,1},{3,0},{4,7},{5,6},{6,5},{7,4},{8,11},{9,10},{10,... | collective-permute-start | bytes 589832 | tf_op jit(solution)/shard_map/ppermute | solution.py:123
  (9 other events, 75.0 us)

commit v6 on v5

--- a/solution.py
+++ b/solution.py
@@ -1,4 +1,5 @@
 import functools
+import math
 
 import jax
 import jax.numpy as jnp
@@ -11,6 +12,8 @@
 TICKS = 3
 PASSES = 2
 VMEM_LIMIT = 24 * 2**20
+SCALE = HD ** (-0.5) * math.log2(math.e)
+OUT_STEPS = 3
 
 
 def block_kernel(chunks, info, *refs):
@@ -31,37 +34,42 @@
             normed[pl.ds(c * rows, rows), :] = (
                 wide * lax.rsqrt(mean_square + 1e-06) * gain_row
             ).astype(jnp.bfloat16)
-        query, key, value = [
-            jnp.dot(normed[...], w[part], preferred_element_type=jnp.float32).astype(jnp.bfloat16)
-            for part in range(3)
-        ]
+        projected = jnp.dot(
+            normed[...], w[...], preferred_element_type=jnp.float32
+        ).astype(jnp.bfloat16)
+        width = heads * HD
         start = pl.multiple_of(info[0], total_rows)
-        kc[pl.ds(start, total_rows), :] = key
-        vc[pl.ds(start, total_rows), :] = value
+        kc[pl.ds(start, total_rows), :] = projected[:, width:2 * width]
+        vc[pl.ds(start, total_rows), :] = projected[:, 2 * width:]
         for h in range(heads):
             cols = pl.ds(h * HD, HD)
             scores = lax.dot_general(
-                query[:, h * HD:(h + 1) * HD],
+                projected[:, h * HD:(h + 1) * HD],
                 kc[:, cols],
                 (((1,), (1,)), ((), ())),
                 preferred_element_type=jnp.float32,
-            ) * HD ** (-0.5)
+            )
             top = jnp.max(scores, axis=-1, keepdims=True)
-            weights = jnp.exp(scores - top)
-            probs = (weights / jnp.sum(weights, axis=-1, keepdims=True)).astype(jnp.bfloat16)
-            attended[:, cols] = jnp.dot(
-                probs, vc[:, cols], preferred_element_type=jnp.float32
+            weights = jnp.exp2((scores - top) * SCALE)
+            share = 1.0 / jnp.sum(weights, axis=-1, keepdims=True)
+            mixed = jnp.dot(
+                weights.astype(jnp.bfloat16), vc[:, cols], preferred_element_type=jnp.float32
+            )
+            attended[:, cols] = (mixed * share).astype(jnp.bfloat16)
+        step = wo.shape[1] // OUT_STEPS
+        for i in range(OUT_STEPS):
+            cols = pl.ds(i * step, step)
+            product = jnp.dot(
+                attended[...], wo[:, cols], preferred_element_type=jnp.float32
             ).astype(jnp.bfloat16)
-        for c in range(chunks):
-            terms[c][...] = jnp.dot(
-                attended[pl.ds(c * rows, rows), :], wo[...], preferred_element_type=jnp.float32
-            ).astype(jnp.bfloat16)
-
-
-def load_kernel(*refs):
-    count = len(refs) // 2
-    sems = refs[-1]
-    pairs = list(zip(refs[:count], refs[count:2 * count]))
+            for c in range(chunks):
+                terms[c][:, cols] = product[c * rows:(c + 1) * rows]
+
+
+def load_kernel(w_hbm, wo_hbm, kc_hbm, vc_hbm, w, wo, kc, vc, sems):
+    parts, _, width = w_hbm.shape
+    pairs = [(w_hbm.at[i], w.at[:, pl.ds(i * width, width)]) for i in range(parts)]
+    pairs += [(wo_hbm, wo), (kc_hbm, kc), (vc_hbm, vc)]
     copies = [pltpu.make_async_copy(a, b, sems.at[i]) for i, (a, b) in enumerate(pairs)]
     for copy in copies:
         copy.start()
@@ -69,13 +77,16 @@
         copy.wait()
 
 
-def loaded(*arrays):
+def loaded(w, wo, kc, vc):
+    parts, depth, width = w.shape
+    arrays = (w, wo, kc, vc)
+    shapes = [(depth, parts * width), wo.shape, kc.shape, vc.shape]
     return pl.pallas_call(
         load_kernel,
-        out_shape=[pltpu.VMEM(a.shape, a.dtype) for a in arrays],
+        out_shape=[pltpu.VMEM(shape, w.dtype) for shape in shapes],
         in_specs=[pl.BlockSpec(memory_space=pl.ANY)] * len(arrays),
         out_specs=[pl.BlockSpec(memory_space=pltpu.VMEM)] * len(arrays),
-        scratch_shapes=[pltpu.SemaphoreType.DMA((len(arrays),))],
+        scratch_shapes=[pltpu.SemaphoreType.DMA((parts + 3,))],
         compiler_params=pltpu.CompilerParams(vmem_limit_bytes=VMEM_LIMIT),
         cost_estimate=pl.CostEstimate(
             flops=0, bytes_accessed=2 * sum(a.size for a in arrays), transcendentals=0
@@ -130,10 +141,11 @@
     return total
 
 
-def gathered(own, hop=0):
+def gathered(own, hop=0, between=lambda far: far):
     far = send(own, FAR, hop)
     near = send(own, NEAR, hop)
     first = send(own, STAY, hop) if hop else own
+    far = between(far)
     return [first, near, far, send(far, NEAR)]
 
 
@@ -149,14 +161,22 @@
 ):
     section_count = lax.axis_size("section")
     section_index = lax.axis_index("section")
-    w = jnp.transpose(qkv_weight[0], (1, 0, 2))
-    wo = out_weight[0]
-    w, wo, kc, vc = loaded(w, wo, stale_keys[0], stale_values[0])
     block_count = section_active[0]
     n = lax.axis_size("uly")
     patch_rows = state.shape[1] * n
     own = state[0]
-    blocks = gathered(own)
+    stored = (
+        jnp.transpose(qkv_weight[0], (1, 0, 2)), out_weight[0], stale_keys[0], stale_values[0]
+    )
+    held = []
+
+    def load(far):
+        far, *rest = lax.optimization_barrier((far, *loaded(*stored)))
+        held.extend(rest)
+        return far
+
+    blocks = gathered(own, between=load)
+    w, wo, kc, vc = held
     for tick in range(TICKS):
         slot = patch_slot[(section_index - tick) % section_count]
         for index in range(PASSES):

time: 233 us -> 226 us (0.970); the launches traced: 234 us -> 224 us
  Pallas kernels: 33.7 us -> 23.8 us
  starting transfers between devices: 59.2 us -> 53.5 us
  local copies, waits for them, and re-layouts: 2.11 us -> 7.19 us
    pallas_call x6, Pallas kernels: 29.8 us -> 19.9 us  [block_terms(): pl.pallas_call(functools.partial(block_kernel, chunks), out_shape=[jax.Sh...]
    unnamed x5 -> x11, local copies, waits for them, and re-layouts: 0.68 us -> 6.53 us
    ppermute x39, starting transfers between devices: 59.2 us -> 53.5 us  [send(): return lax.ppermute(block, ('section', 'uly'), route)]
  transfers between devices with their start and end apart: 39 -> 39, of which waited for: 31 -> 38; matrix products, arithmetic and copies ran while one was open for 1% -> 0% of each run, Pallas kernels for 2% -> 2%
where the time goes in v6:
time: 226 us; the launch traced here: 224 us
  waiting for transfers between devices  135 us (60%)
  starting transfers between devices  53.5 us (24%)
  Pallas kernels  23.8 us (11%)
  local copies, waits for them, and re-layouts  7.19 us (3%)
  between operations  2.85 us (1%)
    ppermute x39, waiting for transfers between devices, send(): return lax.ppermute(block, ('section', 'uly'), route)  135 us
    ppermute x39, starting transfers between devices, send(): return lax.ppermute(block, ('section', 'uly'), route)  53.5 us
    pallas_call x6, Pallas kernels, block_terms(): pl.pallas_call(functools.partial(block_kernel, chunks), out_shape=[jax.Sh...  19.9 us
    unnamed x11, local copies, waits for them, and re-layouts  6.53 us
  transfers between devices with their start and end apart: 39, of which 38 were waited for; matrix products, arithmetic and copies ran while one was open for 0% of the time, Pallas kernels for 2%

profile of v6, /device:TPU:14, one launch (start us, length us, event | category | flops | bytes accessed | tf_op | source)
XLA Modules:
  0.0 224.1 jit_solution(1806276486846677956)
XLA Ops:
  4.1 3.9 %shard_map.82 = (bf16[3072,1152]{1,0:T(8,128)(2,1)S(1)}, bf16[384,3072]{1,0:T(8,128)(2,1)S(1)}, bf16[512,384]{1,0:T(8,128)(2,1)S(1)}, bf16[512,384]{1,0:T(8,128)(2,1)S(1)}) custom-call(bf16[3,3072,384]{2,1,0:T(8,128)(2,1)} %bitcast.14, bf16[384,3072]{1,0:T(8,128)(2,1)} %bitcast.15, bf16[512,384]{1,0:T(8,128)(2,1)} %bitcast.16, bf16[512,384]{1,0:T(8,128)(2,1)} %bitcast.17), custom_call_target="tpu_custom_call" | custom-call | bytes 10223616 | tf_op jit(solution)/shard_map/pallas_call | solution.py:84
  13.5 4.1 %collective-permute-done.2.refs_3_ = bf16[32,3072]{1,0:T(8,128)(2,1)} collective-permute-done((bf16[32,3072]{1,0:T(8,128)(2,1)S(1)}, bf16[32,3072]{1,0:T(8,128)(2,1)}, u32[]{:S(2)}, u32[]{:S(2)}) %collective-permute-start.2) | collective-permute-done | bytes 196640 | tf_op jit(solution)/shard_map/ppermute | solution.py:134
  20.5 3.7 %shard_map.83 = (bf16[32,3072]{1,0:T(8,128)(2,1)S(1)}, bf16[32,3072]{1,0:T(8,128)(2,1)S(1)}, bf16[32,3072]{1,0:T(8,128)(2,1)S(1)}, bf16[32,3072]{1,0:T(8,128)(2,...) custom-call(s32[2]{0:T(128)S(1)} %pad_add_fusion.1.info, ...), custom_call_target="tpu_custom_call", output_to_operand_aliasing={{4}: (8, {}), {5}: (9, {})} | custom-call | flops 1308622848 | bytes 9437184 | tf_op jit(solution)/shard_map/pallas_call | solution.py:105
  24.7 5.3 %collective-permute-done.3 = bf16[32,3072]{1,0:T(8,128)(2,1)S(1)} collective-permute-done((bf16[32,3072]{1,0:T(8,128)(2,1)S(1)}, bf16[32,3072]{1,0:T(8,128)(2,1)S(1)}, u32[]{:S(2)}, u32[]{:S(2)}) %collective-permute-start.3) | collective-permute-done | bytes 196640 | tf_op jit(solution)/shard_map/ppermute | solution.py:134
  31.8 4.6 %collective-permute-done.4 = bf16[32,3072]{1,0:T(8,128)(2,1)S(1)} collective-permute-done((bf16[32,3072]{1,0:T(8,128)(2,1)S(1)}, bf16[32,3072]{1,0:T(8,128)(2,1)S(1)}, u32[]{:S(2)}, u32[]{:S(2)}) %collective-permute-start.4) | collective-permute-done | bytes 196640 | tf_op jit(solution)/shard_map/ppermute | solution.py:134
  36.4 6.5 %collective-permute-done.5 = bf16[32,3072]{1,0:T(8,128)(2,1)S(1)} collective-permute-done((bf16[32,3072]{1,0:T(8,128)(2,1)S(1)}, bf16[32,3072]{1,0:T(8,128)(2,1)S(1)}, u32[]{:S(2)}, u32[]{:S(2)}) %collective-permute-start.5) | collective-permute-done | bytes 196640 | tf_op jit(solution)/shard_map/ppermute | solution.py:134
  44.2 4.9 %collective-permute-done.7.refs_2_ = bf16[32,3072]{1,0:T(8,128)(2,1)S(1)} collective-permute-done((bf16[32,3072]{1,0:T(8,128)(2,1)S(1)}, bf16[32,3072]{1,0:T(8,128)(2,1)S(1)}, u32[]{:S(2)}, u32[]{:S(2)}) %collective-permute-start.7) | collective-permute-done | bytes 196640 | tf_op jit(solution)/shard_map/ppermute | solution.py:134
  50.5 4.3 %collective-permute-done.8.refs_3_ = bf16[32,3072]{1,0:T(8,128)(2,1)S(1)} collective-permute-done((bf16[32,3072]{1,0:T(8,128)(2,1)S(1)}, bf16[32,3072]{1,0:T(8,128)(2,1)S(1)}, u32[]{:S(2)}, u32[]{:S(2)}) %collective-permute-start.8) | collective-permute-done | bytes 196640 | tf_op jit(solution)/shard_map/ppermute | solution.py:134
  54.7 3.2 %shard_map.84 = (bf16[32,3072]{1,0:T(8,128)(2,1)S(1)}, bf16[32,3072]{1,0:T(8,128)(2,1)S(1)}, bf16[32,3072]{1,0:T(8,128)(2,1)S(1)}, bf16[32,3072]{1,0:T(8,128)(2,...) custom-call(s32[2]{0:T(128)S(1)} %pad_add_fusion.info, ...), custom_call_target="tpu_custom_call", output_to_operand_aliasing={{4}: (8, {}), {5}: (9, {})} | custom-call | flops 1308622848 | bytes 9437184 | tf_op jit(solution)/shard_map/pallas_call | solution.py:105
  58.0 7.7 %collective-permute-done.9 = bf16[32,3072]{1,0:T(8,128)(2,1)S(1)} collective-permute-done((bf16[32,3072]{1,0:T(8,128)(2,1)S(1)}, bf16[32,3072]{1,0:T(8,128)(2,1)S(1)}, u32[]{:S(2)}, u32[]{:S(2)}) %collective-permute-start.9) | collective-permute-done | bytes 196640 | tf_op jit(solution)/shard_map/ppermute | solution.py:134
  67.0 4.5 %collective-permute-done.10 = bf16[32,3072]{1,0:T(8,128)(2,1)S(1)} collective-permute-done((bf16[32,3072]{1,0:T(8,128)(2,1)S(1)}, bf16[32,3072]{1,0:T(8,128)(2,1)S(1)}, u32[]{:S(2)}, u32[]{:S(2)}) %collective-permute-start.10) | collective-permute-done | bytes 196640 | tf_op jit(solution)/shard_map/ppermute | solution.py:134
  71.8 5.5 %collective-permute-start.13 = (bf16[32,3072]{1,0:T(8,128)(2,1)S(1)}, bf16[32,3072]{1,0:T(8,128)(2,1)S(1)}, u32[]{:S(2)}, u32[]{:S(2)}) collective-permute-start(bf16[32,3072]{1,0:T(8,128)(2,1)S(1)} %fusion.1), channel_id=1, source_target_pairs={{0,5},{1,4},{2,7},{3,6},{4,9},{5,8},{6,11},{7,10},{8,13},{9,12},{1... | collective-permute-start | bytes 589832 | tf_op jit(solution)/shard_map/ppermute | solution.py:134
  79.9 4.3 %collective-permute-start.15 = (bf16[32,3072]{1,0:T(8,128)(2,1)S(1)}, bf16[32,3072]{1,0:T(8,128)(2,1)S(1)}, u32[]{:S(2)}, u32[]{:S(2)}) collective-permute-start(bf16[32,3072]{1,0:T(8,128)(2,1)S(1)} %collective-permute-done.14.refs_2_), channel_id=1, source_target_pairs={{0,1},{1,0},{2,3},{3,2},{4,5},{5,4},{6,7},{7,6},{8,9},{9,8},{10,11... | collective-permute-start | bytes 589832 | tf_op jit(solution)/shard_map/ppermute | solution.py:134
  85.3 4.7 %collective-permute-done.15.refs_3_ = bf16[32,3072]{1,0:T(8,128)(2,1)S(1)} collective-permute-done((bf16[32,3072]{1,0:T(8,128)(2,1)S(1)}, bf16[32,3072]{1,0:T(8,128)(2,1)S(1)}, u32[]{:S(2)}, u32[]{:S(2)}) %collective-permute-start.15) | collective-permute-done | bytes 196640 | tf_op jit(solution)/shard_map/ppermute | solution.py:134
  90.0 3.2 %shard_map.85 = (bf16[32,3072]{1,0:T(8,128)(2,1)S(1)}, bf16[32,3072]{1,0:T(8,128)(2,1)S(1)}, bf16[32,3072]{1,0:T(8,128)(2,1)S(1)}, bf16[32,3072]{1,0:T(8,128)(2,...) custom-call(s32[2]{0:T(128)S(1)} %pad_add_fusion.3.info, ...), custom_call_target="tpu_custom_call", output_to_operand_aliasing={{4}: (8, {}), {5}: (9, {})} | custom-call | flops 1308622848 | bytes 9437184 | tf_op jit(solution)/shard_map/pallas_call | solution.py:105
  94.8 5.3 %collective-permute-done.16 = bf16[32,3072]{1,0:T(8,128)(2,1)S(1)} collective-permute-done((bf16[32,3072]{1,0:T(8,128)(2,1)S(1)}, bf16[32,3072]{1,0:T(8,128)(2,1)S(1)}, u32[]{:S(2)}, u32[]{:S(2)}) %collective-permute-start.16) | collective-permute-done | bytes 196640 | tf_op jit(solution)/shard_map/ppermute | solution.py:134
  102.4 5.7 %collective-permute-done.17 = bf16[32,3072]{1,0:T(8,128)(2,1)S(1)} collective-permute-done((bf16[32,3072]{1,0:T(8,128)(2,1)S(1)}, bf16[32,3072]{1,0:T(8,128)(2,1)S(1)}, u32[]{:S(2)}, u32[]{:S(2)}) %collective-permute-start.17) | collective-permute-done | bytes 196640 | tf_op jit(solution)/shard_map/ppermute | solution.py:134
  108.1 3.9 %collective-permute-done.18 = bf16[32,3072]{1,0:T(8,128)(2,1)S(1)} collective-permute-done((bf16[32,3072]{1,0:T(8,128)(2,1)S(1)}, bf16[32,3072]{1,0:T(8,128)(2,1)S(1)}, u32[]{:S(2)}, u32[]{:S(2)}) %collective-permute-start.18) | collective-permute-done | bytes 196640 | tf_op jit(solution)/shard_map/ppermute | solution.py:134
  114.7 5.0 %collective-permute-done.20.refs_2_ = bf16[32,3072]{1,0:T(8,128)(2,1)S(1)} collective-permute-done((bf16[32,3072]{1,0:T(8,128)(2,1)S(1)}, bf16[32,3072]{1,0:T(8,128)(2,1)S(1)}, u32[]{:S(2)}, u32[]{:S(2)}) %collective-permute-start.20) | collective-permute-done | bytes 196640 | tf_op jit(solution)/shard_map/ppermute | solution.py:134
  131.4 4.4 %collective-permute-done.22 = bf16[32,3072]{1,0:T(8,128)(2,1)S(1)} collective-permute-done((bf16[32,3072]{1,0:T(8,128)(2,1)S(1)}, bf16[32,3072]{1,0:T(8,128)(2,1)S(1)}, u32[]{:S(2)}, u32[]{:S(2)}) %collective-permute-start.22) | collective-permute-done | bytes 196640 | tf_op jit(solution)/shard_map/ppermute | solution.py:134
  141.7 4.1 %collective-permute-done.24 = bf16[32,3072]{1,0:T(8,128)(2,1)S(1)} collective-permute-done((bf16[32,3072]{1,0:T(8,128)(2,1)S(1)}, bf16[32,3072]{1,0:T(8,128)(2,1)S(1)}, u32[]{:S(2)}, u32[]{:S(2)}) %collective-permute-start.24) | collective-permute-done | bytes 196640 | tf_op jit(solution)/shard_map/ppermute | solution.py:134
  148.8 6.1 %collective-permute-done.27.refs_2_ = bf16[32,3072]{1,0:T(8,128)(2,1)S(1)} collective-permute-done((bf16[32,3072]{1,0:T(8,128)(2,1)S(1)}, bf16[32,3072]{1,0:T(8,128)(2,1)S(1)}, u32[]{:S(2)}, u32[]{:S(2)}) %collective-permute-start.27) | collective-permute-done | bytes 196640 | tf_op jit(solution)/shard_map/ppermute | solution.py:134
  157.7 4.4 %collective-permute-done.28.refs_3_ = bf16[32,3072]{1,0:T(8,128)(2,1)S(1)} collective-permute-done((bf16[32,3072]{1,0:T(8,128)(2,1)S(1)}, bf16[32,3072]{1,0:T(8,128)(2,1)S(1)}, u32[]{:S(2)}, u32[]{:S(2)}) %collective-permute-start.28) | collective-permute-done | bytes 196640 | tf_op jit(solution)/shard_map/ppermute | solution.py:134
  162.0 3.4 %shard_map.87 = (bf16[32,3072]{1,0:T(8,128)(2,1)S(1)}, bf16[32,3072]{1,0:T(8,128)(2,1)S(1)}, bf16[32,3072]{1,0:T(8,128)(2,1)S(1)}, bf16[32,3072]{1,0:T(8,128)(2,...) custom-call(s32[2]{0:T(128)S(1)} %pad_add_fusion.5.info, ...), custom_call_target="tpu_custom_call", output_to_operand_aliasing={{4}: (8, {}), {5}: (9, {})} | custom-call | flops 1308622848 | bytes 9437184 | tf_op jit(solution)/shard_map/pallas_call | solution.py:105
  165.5 7.2 %collective-permute-done.29 = bf16[32,3072]{1,0:T(8,128)(2,1)S(1)} collective-permute-done((bf16[32,3072]{1,0:T(8,128)(2,1)S(1)}, bf16[32,3072]{1,0:T(8,128)(2,1)S(1)}, u32[]{:S(2)}, u32[]{:S(2)}) %collective-permute-start.29) | collective-permute-done | bytes 196640 | tf_op jit(solution)/shard_map/ppermute | solution.py:134
  174.2 6.5 %collective-permute-done.30 = bf16[32,3072]{1,0:T(8,128)(2,1)S(1)} collective-permute-done((bf16[32,3072]{1,0:T(8,128)(2,1)S(1)}, bf16[32,3072]{1,0:T(8,128)(2,1)S(1)}, u32[]{:S(2)}, u32[]{:S(2)}) %collective-permute-start.30) | collective-permute-done | bytes 196640 | tf_op jit(solution)/shard_map/ppermute | solution.py:134
  181.9 5.7 %collective-permute-start.32 = (bf16[32,3072]{1,0:T(8,128)(2,1)S(1)}, bf16[32,3072]{1,0:T(8,128)(2,1)S(1)}, u32[]{:S(2)}, u32[]{:S(2)}) collective-permute-start(bf16[32,3072]{1,0:T(8,128)(2,1)S(1)} %fusion.4.refs_0_), channel_id=1, source_target_pairs={{0,1},{1,0},{2,3},{3,2},{4,5},{5,4},{6,7},{7,6},{8,9},{9,8},{10,11... | collective-permute-start | bytes 589832 | tf_op jit(solution)/shard_map/ppermute | solution.py:134
  190.6 4.7 %collective-permute-start.34 = (bf16[32,3072]{1,0:T(8,128)(2,1)S(1)}, bf16[32,3072]{1,0:T(8,128)(2,1)S(1)}, u32[]{:S(2)}, u32[]{:S(2)}) collective-permute-start(bf16[32,3072]{1,0:T(8,128)(2,1)S(1)} %collective-permute-done.33.refs_2_), channel_id=1, source_target_pairs={{0,1},{1,0},{2,3},{3,2},{4,5},{5,4},{6,7},{7,6},{8,9},{9,8},{10,11... | collective-permute-start | bytes 589832 | tf_op jit(solution)/shard_map/ppermute | solution.py:134
  199.6 3.2 %shard_map.88 = (bf16[32,3072]{1,0:T(8,128)(2,1)S(1)}, bf16[32,3072]{1,0:T(8,128)(2,1)S(1)}, bf16[32,3072]{1,0:T(8,128)(2,1)S(1)}, bf16[32,3072]{1,0:T(8,128)(2,...) custom-call(s32[2]{0:T(128)S(1)} %pad_add_fusion.4.info, ...), custom_call_target="tpu_custom_call", output_to_operand_aliasing={{4}: (8, {}), {5}: (9, {})} | custom-call | flops 1308622848 | bytes 9437184 | tf_op jit(solution)/shard_map/pallas_call | solution.py:105
  204.5 4.1 %collective-permute-done.35 = bf16[32,3072]{1,0:T(8,128)(2,1)S(1)} collective-permute-done((bf16[32,3072]{1,0:T(8,128)(2,1)S(1)}, bf16[32,3072]{1,0:T(8,128)(2,1)S(1)}, u32[]{:S(2)}, u32[]{:S(2)}) %collective-permute-start.35) | collective-permute-done | bytes 196640 | tf_op jit(solution)/shard_map/ppermute | solution.py:134
  214.8 3.4 %collective-permute-done.37 = bf16[32,3072]{1,0:T(8,128)(2,1)S(1)} collective-permute-done((bf16[32,3072]{1,0:T(8,128)(2,1)S(1)}, bf16[32,3072]{1,0:T(8,128)(2,1)S(1)}, u32[]{:S(2)}, u32[]{:S(2)}) %collective-permute-start.37) | collective-permute-done | bytes 196640 | tf_op jit(solution)/shard_map/ppermute | solution.py:134
  218.4 5.1 %collective-permute-done.38 = bf16[32,3072]{1,0:T(8,128)(2,1)S(1)} collective-permute-done((bf16[32,3072]{1,0:T(8,128)(2,1)S(1)}, bf16[32,3072]{1,0:T(8,128)(2,1)S(1)}, u32[]{:S(2)}, u32[]{:S(2)}) %collective-permute-start.38) | collective-permute-done | bytes 196640 | tf_op jit(solution)/shard_map/ppermute | solution.py:134
  (83 shorter events, 68.7 us)
Async XLA Ops:
  0.0 11.1 %collective-permute-start.1 = (bf16[32,3072]{1,0:T(8,128)(2,1)}, bf16[32,3072]{1,0:T(8,128)(2,1)S(1)}, u32[]{:S(2)}, u32[]{:S(2)}) collective-permute-start(bf16[32,3072]{1,0:T(8,128)(2,1)} %bitcast.11), channel_id=1, source_target_pairs={{0,3},{1,2},{2,1},{3,0},{4,7},{5,6},{6,5},{7,4},{8,11},{9,10},{10,... | collective-permute-start | bytes 589832 | tf_op jit(solution)/shard_map/ppermute | solution.py:134
  1.7 11.8 %collective-permute-start = (bf16[32,3072]{1,0:T(8,128)(2,1)}, bf16[32,3072]{1,0:T(8,128)(2,1)}, u32[]{:S(2)}, u32[]{:S(2)}) collective-permute-start(bf16[32,3072]{1,0:T(8,128)(2,1)} %bitcast.12), channel_id=1, source_target_pairs={{0,1},{1,0},{2,3},{3,2},{4,5},{5,4},{6,7},{7,6},{8,9},{9,8},{10,11... | collective-permute-start | bytes 589832 | tf_op jit(solution)/shard_map/ppermute | solution.py:134
  11.1 6.4 %collective-permute-start.2 = (bf16[32,3072]{1,0:T(8,128)(2,1)S(1)}, bf16[32,3072]{1,0:T(8,128)(2,1)}, u32[]{:S(2)}, u32[]{:S(2)}) collective-permute-start(bf16[32,3072]{1,0:T(8,128)(2,1)S(1)} %collective-permute-done.1.refs_2_), channel_id=1, source_target_pairs={{0,1},{1,0},{2,3},{3,2},{4,5},{5,4},{6,7},{7,6},{8,9},{9,8},{10,11... | collective-permute-start | bytes 589832 | tf_op jit(solution)/shard_map/ppermute | solution.py:134
  30.0 6.4 %collective-permute-start.4 = (bf16[32,3072]{1,0:T(8,128)(2,1)S(1)}, bf16[32,3072]{1,0:T(8,128)(2,1)S(1)}, u32[]{:S(2)}, u32[]{:S(2)}) collective-permute-start(bf16[32,3072]{1,0:T(8,128)(2,1)S(1)} %get-tuple-element.73), channel_id=1, source_target_pairs={{0,1},{1,0},{2,3},{3,2},{4,5},{5,4},{6,7},{7,6},{8,9},{9,8},{10,11... | collective-permute-start | bytes 589832 | tf_op jit(solution)/shard_map/ppermute | solution.py:134
  30.5 12.4 %collective-permute-start.5 = (bf16[32,3072]{1,0:T(8,128)(2,1)S(1)}, bf16[32,3072]{1,0:T(8,128)(2,1)S(1)}, u32[]{:S(2)}, u32[]{:S(2)}) collective-permute-start(bf16[32,3072]{1,0:T(8,128)(2,1)S(1)} %add_convert_fusion.11), channel_id=1, source_target_pairs={{0,3},{1,2},{2,1},{3,0},{4,7},{5,6},{6,5},{7,4},{8,11},{9,10},{10,... | collective-permute-start | bytes 589832 | tf_op jit(solution)/shard_map/ppermute | solution.py:134
  43.0 6.1 %collective-permute-start.7 = (bf16[32,3072]{1,0:T(8,128)(2,1)S(1)}, bf16[32,3072]{1,0:T(8,128)(2,1)S(1)}, u32[]{:S(2)}, u32[]{:S(2)}) collective-permute-start(bf16[32,3072]{1,0:T(8,128)(2,1)S(1)} %fusion.refs_0_), channel_id=1, source_target_pairs={{0,3},{1,2},{2,1},{3,0},{4,7},{5,6},{6,5},{7,4},{8,11},{9,10},{10,... | collective-permute-start | bytes 589832 | tf_op jit(solution)/shard_map/ppermute | solution.py:134
  44.2 6.3 %collective-permute-start.6 = (bf16[32,3072]{1,0:T(8,128)(2,1)S(1)}, bf16[32,3072]{1,0:T(8,128)(2,1)S(1)}, u32[]{:S(2)}, u32[]{:S(2)}) collective-permute-start(bf16[32,3072]{1,0:T(8,128)(2,1)S(1)} %fusion.refs_0_), channel_id=1, source_target_pairs={{0,1},{1,0},{2,3},{3,2},{4,5},{5,4},{6,7},{7,6},{8,9},{9,8},{10,11... | collective-permute-start | bytes 589832 | tf_op jit(solution)/shard_map/ppermute | solution.py:134
  58.0 7.8 %collective-permute-start.9 = (bf16[32,3072]{1,0:T(8,128)(2,1)S(1)}, bf16[32,3072]{1,0:T(8,128)(2,1)S(1)}, u32[]{:S(2)}, u32[]{:S(2)}) collective-permute-start(bf16[32,3072]{1,0:T(8,128)(2,1)S(1)} %get-tuple-element.80), channel_id=1, source_target_pairs={{0,1},{1,0},{2,3},{3,2},{4,5},{5,4},{6,7},{7,6},{8,9},{9,8},{10,11... | collective-permute-start | bytes 589832 | tf_op jit(solution)/shard_map/ppermute | solution.py:134
  71.7 8.2 %collective-permute-start.14 = (bf16[32,3072]{1,0:T(8,128)(2,1)S(1)}, bf16[32,3072]{1,0:T(8,128)(2,1)S(1)}, u32[]{:S(2)}, u32[]{:S(2)}) collective-permute-start(bf16[32,3072]{1,0:T(8,128)(2,1)S(1)} %fusion.1), channel_id=1, source_target_pairs={{0,7},{1,6},{2,5},{3,4},{4,11},{5,10},{6,9},{7,8},{8,15},{9,14},{1... | collective-permute-start | bytes 589832 | tf_op jit(solution)/shard_map/ppermute | solution.py:134
  71.8 13.5 %collective-permute-start.13 = (bf16[32,3072]{1,0:T(8,128)(2,1)S(1)}, bf16[32,3072]{1,0:T(8,128)(2,1)S(1)}, u32[]{:S(2)}, u32[]{:S(2)}) collective-permute-start(bf16[32,3072]{1,0:T(8,128)(2,1)S(1)} %fusion.1), channel_id=1, source_target_pairs={{0,5},{1,4},{2,7},{3,6},{4,9},{5,8},{6,11},{7,10},{8,13},{9,12},{1... | collective-permute-start | bytes 589832 | tf_op jit(solution)/shard_map/ppermute | solution.py:134
  77.3 8.0 %collective-permute-start.12 = (bf16[32,3072]{1,0:T(8,128)(2,1)S(1)}, bf16[32,3072]{1,0:T(8,128)(2,1)S(1)}, u32[]{:S(2)}, u32[]{:S(2)}) collective-permute-start(bf16[32,3072]{1,0:T(8,128)(2,1)S(1)} %fusion.1), channel_id=1, source_target_pairs={{0,4},{1,5},{2,6},{3,7},{4,8},{5,9},{6,10},{7,11},{8,12},{9,13},{1... | collective-permute-start | bytes 589832 | tf_op jit(solution)/shard_map/ppermute | solution.py:134
  79.9 10.1 %collective-permute-start.15 = (bf16[32,3072]{1,0:T(8,128)(2,1)S(1)}, bf16[32,3072]{1,0:T(8,128)(2,1)S(1)}, u32[]{:S(2)}, u32[]{:S(2)}) collective-permute-start(bf16[32,3072]{1,0:T(8,128)(2,1)S(1)} %collective-permute-done.14.refs_2_), channel_id=1, source_target_pairs={{0,1},{1,0},{2,3},{3,2},{4,5},{5,4},{6,7},{7,6},{8,9},{9,8},{10,11... | collective-permute-start | bytes 589832 | tf_op jit(solution)/shard_map/ppermute | solution.py:134
  93.2 7.0 %collective-permute-start.16 = (bf16[32,3072]{1,0:T(8,128)(2,1)S(1)}, bf16[32,3072]{1,0:T(8,128)(2,1)S(1)}, u32[]{:S(2)}, u32[]{:S(2)}) collective-permute-start(bf16[32,3072]{1,0:T(8,128)(2,1)S(1)} %get-tuple-element.88), channel_id=1, source_target_pairs={{0,1},{1,0},{2,3},{3,2},{4,5},{5,4},{6,7},{7,6},{8,9},{9,8},{10,11... | collective-permute-start | bytes 589832 | tf_op jit(solution)/shard_map/ppermute | solution.py:134
  100.2 7.9 %collective-permute-start.17 = (bf16[32,3072]{1,0:T(8,128)(2,1)S(1)}, bf16[32,3072]{1,0:T(8,128)(2,1)S(1)}, u32[]{:S(2)}, u32[]{:S(2)}) collective-permute-start(bf16[32,3072]{1,0:T(8,128)(2,1)S(1)} %get-tuple-element.89), channel_id=1, source_target_pairs={{0,1},{1,0},{2,3},{3,2},{4,5},{5,4},{6,7},{7,6},{8,9},{9,8},{10,11... | collective-permute-start | bytes 589832 | tf_op jit(solution)/shard_map/ppermute | solution.py:134
  101.4 10.6 %collective-permute-start.18 = (bf16[32,3072]{1,0:T(8,128)(2,1)S(1)}, bf16[32,3072]{1,0:T(8,128)(2,1)S(1)}, u32[]{:S(2)}, u32[]{:S(2)}) collective-permute-start(bf16[32,3072]{1,0:T(8,128)(2,1)S(1)} %add_convert_fusion.7), channel_id=1, source_target_pairs={{0,3},{1,2},{2,1},{3,0},{4,7},{5,6},{6,5},{7,4},{8,11},{9,10},{10,... | collective-permute-start | bytes 589832 | tf_op jit(solution)/shard_map/ppermute | solution.py:134
  112.2 7.5 %collective-permute-start.20 = (bf16[32,3072]{1,0:T(8,128)(2,1)S(1)}, bf16[32,3072]{1,0:T(8,128)(2,1)S(1)}, u32[]{:S(2)}, u32[]{:S(2)}) collective-permute-start(bf16[32,3072]{1,0:T(8,128)(2,1)S(1)} %fusion.2.refs_0_), channel_id=1, source_target_pairs={{0,3},{1,2},{2,1},{3,0},{4,7},{5,6},{6,5},{7,4},{8,11},{9,10},{10,... | collective-permute-start | bytes 589832 | tf_op jit(solution)/shard_map/ppermute | solution.py:134
  113.2 10.8 %collective-permute-start.19 = (bf16[32,3072]{1,0:T(8,128)(2,1)S(1)}, bf16[32,3072]{1,0:T(8,128)(2,1)S(1)}, u32[]{:S(2)}, u32[]{:S(2)}) collective-permute-start(bf16[32,3072]{1,0:T(8,128)(2,1)S(1)} %fusion.2.refs_0_), channel_id=1, source_target_pairs={{0,1},{1,0},{2,3},{3,2},{4,5},{5,4},{6,7},{7,6},{8,9},{9,8},{10,11... | collective-permute-start | bytes 589832 | tf_op jit(solution)/shard_map/ppermute | solution.py:134
  119.7 6.4 %collective-permute-start.21 = (bf16[32,3072]{1,0:T(8,128)(2,1)S(1)}, bf16[32,3072]{1,0:T(8,128)(2,1)S(1)}, u32[]{:S(2)}, u32[]{:S(2)}) collective-permute-start(bf16[32,3072]{1,0:T(8,128)(2,1)S(1)} %collective-permute-done.20.refs_2_), channel_id=1, source_target_pairs={{0,1},{1,0},{2,3},{3,2},{4,5},{5,4},{6,7},{7,6},{8,9},{9,8},{10,11... | collective-permute-start | bytes 589832 | tf_op jit(solution)/shard_map/ppermute | solution.py:134
  129.4 6.4 %collective-permute-start.22 = (bf16[32,3072]{1,0:T(8,128)(2,1)S(1)}, bf16[32,3072]{1,0:T(8,128)(2,1)S(1)}, u32[]{:S(2)}, u32[]{:S(2)}) collective-permute-start(bf16[32,3072]{1,0:T(8,128)(2,1)S(1)} %get-tuple-element.96), channel_id=1, source_target_pairs={{0,1},{1,0},{2,3},{3,2},{4,5},{5,4},{6,7},{7,6},{8,9},{9,8},{10,11... | collective-permute-start | bytes 589832 | tf_op jit(solution)/shard_map/ppermute | solution.py:134
  138.1 7.8 %collective-permute-start.24 = (bf16[32,3072]{1,0:T(8,128)(2,1)S(1)}, bf16[32,3072]{1,0:T(8,128)(2,1)S(1)}, u32[]{:S(2)}, u32[]{:S(2)}) collective-permute-start(bf16[32,3072]{1,0:T(8,128)(2,1)S(1)} %add_convert_fusion.5), channel_id=1, source_target_pairs={{0,3},{1,2},{2,1},{3,0},{4,7},{5,6},{6,5},{7,4},{8,11},{9,10},{10,... | collective-permute-start | bytes 589832 | tf_op jit(solution)/shard_map/ppermute | solution.py:134
  145.9 8.9 %collective-permute-start.27 = (bf16[32,3072]{1,0:T(8,128)(2,1)S(1)}, bf16[32,3072]{1,0:T(8,128)(2,1)S(1)}, u32[]{:S(2)}, u32[]{:S(2)}) collective-permute-start(bf16[32,3072]{1,0:T(8,128)(2,1)S(1)} %fusion.3), channel_id=1, source_target_pairs={{0,7},{1,6},{2,5},{3,4},{4,11},{5,10},{6,9},{7,8},{8,15},{9,14},{1... | collective-permute-start | bytes 589832 | tf_op jit(solution)/shard_map/ppermute | solution.py:134
  146.0 10.2 %collective-permute-start.26 = (bf16[32,3072]{1,0:T(8,128)(2,1)S(1)}, bf16[32,3072]{1,0:T(8,128)(2,1)S(1)}, u32[]{:S(2)}, u32[]{:S(2)}) collective-permute-start(bf16[32,3072]{1,0:T(8,128)(2,1)S(1)} %fusion.3), channel_id=1, source_target_pairs={{0,5},{1,4},{2,7},{3,6},{4,9},{5,8},{6,11},{7,10},{8,13},{9,12},{1... | collective-permute-start | bytes 589832 | tf_op jit(solution)/shard_map/ppermute | solution.py:134
  148.8 8.9 %collective-permute-start.25 = (bf16[32,3072]{1,0:T(8,128)(2,1)S(1)}, bf16[32,3072]{1,0:T(8,128)(2,1)S(1)}, u32[]{:S(2)}, u32[]{:S(2)}) collective-permute-start(bf16[32,3072]{1,0:T(8,128)(2,1)S(1)} %fusion.3), channel_id=1, source_target_pairs={{0,4},{1,5},{2,6},{3,7},{4,8},{5,9},{6,10},{7,11},{8,12},{9,13},{1... | collective-permute-start | bytes 589832 | tf_op jit(solution)/shard_map/ppermute | solution.py:134
  154.9 7.2 %collective-permute-start.28 = (bf16[32,3072]{1,0:T(8,128)(2,1)S(1)}, bf16[32,3072]{1,0:T(8,128)(2,1)S(1)}, u32[]{:S(2)}, u32[]{:S(2)}) collective-permute-start(bf16[32,3072]{1,0:T(8,128)(2,1)S(1)} %collective-permute-done.27.refs_2_), channel_id=1, source_target_pairs={{0,1},{1,0},{2,3},{3,2},{4,5},{5,4},{6,7},{7,6},{8,9},{9,8},{10,11... | collective-permute-start | bytes 589832 | tf_op jit(solution)/shard_map/ppermute | solution.py:134
  165.4 7.3 %collective-permute-start.29 = (bf16[32,3072]{1,0:T(8,128)(2,1)S(1)}, bf16[32,3072]{1,0:T(8,128)(2,1)S(1)}, u32[]{:S(2)}, u32[]{:S(2)}) collective-permute-start(bf16[32,3072]{1,0:T(8,128)(2,1)S(1)} %get-tuple-element.104), channel_id=1, source_target_pairs={{0,1},{1,0},{2,3},{3,2},{4,5},{5,4},{6,7},{7,6},{8,9},{9,8},{10,11... | collective-permute-start | bytes 589832 | tf_op jit(solution)/shard_map/ppermute | solution.py:134
  172.8 7.9 %collective-permute-start.30 = (bf16[32,3072]{1,0:T(8,128)(2,1)S(1)}, bf16[32,3072]{1,0:T(8,128)(2,1)S(1)}, u32[]{:S(2)}, u32[]{:S(2)}) collective-permute-start(bf16[32,3072]{1,0:T(8,128)(2,1)S(1)} %get-tuple-element.105), channel_id=1, source_target_pairs={{0,1},{1,0},{2,3},{3,2},{4,5},{5,4},{6,7},{7,6},{8,9},{9,8},{10,11... | collective-permute-start | bytes 589832 | tf_op jit(solution)/shard_map/ppermute | solution.py:134
  173.1 7.7 %collective-permute-start.31 = (bf16[32,3072]{1,0:T(8,128)(2,1)S(1)}, bf16[32,3072]{1,0:T(8,128)(2,1)S(1)}, u32[]{:S(2)}, u32[]{:S(2)}) collective-permute-start(bf16[32,3072]{1,0:T(8,128)(2,1)S(1)} %add_convert_fusion.3), channel_id=1, source_target_pairs={{0,3},{1,2},{2,1},{3,0},{4,7},{5,6},{6,5},{7,4},{8,11},{9,10},{10,... | collective-permute-start | bytes 589832 | tf_op jit(solution)/shard_map/ppermute | solution.py:134
  181.0 9.6 %collective-permute-start.33 = (bf16[32,3072]{1,0:T(8,128)(2,1)S(1)}, bf16[32,3072]{1,0:T(8,128)(2,1)S(1)}, u32[]{:S(2)}, u32[]{:S(2)}) collective-permute-start(bf16[32,3072]{1,0:T(8,128)(2,1)S(1)} %fusion.4.refs_0_), channel_id=1, source_target_pairs={{0,3},{1,2},{2,1},{3,0},{4,7},{5,6},{6,5},{7,4},{8,11},{9,10},{10,... | collective-permute-start | bytes 589832 | tf_op jit(solution)/shard_map/ppermute | solution.py:134
  181.9 15.5 %collective-permute-start.32 = (bf16[32,3072]{1,0:T(8,128)(2,1)S(1)}, bf16[32,3072]{1,0:T(8,128)(2,1)S(1)}, u32[]{:S(2)}, u32[]{:S(2)}) collective-permute-start(bf16[32,3072]{1,0:T(8,128)(2,1)S(1)} %fusion.4.refs_0_), channel_id=1, source_target_pairs={{0,1},{1,0},{2,3},{3,2},{4,5},{5,4},{6,7},{7,6},{8,9},{9,8},{10,11... | collective-permute-start | bytes 589832 | tf_op jit(solution)/shard_map/ppermute | solution.py:134
  190.6 9.0 %collective-permute-start.34 = (bf16[32,3072]{1,0:T(8,128)(2,1)S(1)}, bf16[32,3072]{1,0:T(8,128)(2,1)S(1)}, u32[]{:S(2)}, u32[]{:S(2)}) collective-permute-start(bf16[32,3072]{1,0:T(8,128)(2,1)S(1)} %collective-permute-done.33.refs_2_), channel_id=1, source_target_pairs={{0,1},{1,0},{2,3},{3,2},{4,5},{5,4},{6,7},{7,6},{8,9},{9,8},{10,11... | collective-permute-start | bytes 589832 | tf_op jit(solution)/shard_map/ppermute | solution.py:134
  208.7 6.1 %collective-permute-start.36 = (bf16[32,3072]{1,0:T(8,128)(2,1)S(1)}, bf16[32,3072]{1,0:T(8,128)(2,1)S(1)}, u32[]{:S(2)}, u32[]{:S(2)}) collective-permute-start(bf16[32,3072]{1,0:T(8,128)(2,1)S(1)} %get-tuple-element.113), channel_id=1, source_target_pairs={{0,1},{1,0},{2,3},{3,2},{4,5},{5,4},{6,7},{7,6},{8,9},{9,8},{10,11... | collective-permute-start | bytes 589832 | tf_op jit(solution)/shard_map/ppermute | solution.py:134
  210.4 7.8 %collective-permute-start.37 = (bf16[32,3072]{1,0:T(8,128)(2,1)S(1)}, bf16[32,3072]{1,0:T(8,128)(2,1)S(1)}, u32[]{:S(2)}, u32[]{:S(2)}) collective-permute-start(bf16[32,3072]{1,0:T(8,128)(2,1)S(1)} %add_convert_fusion.1), channel_id=1, source_target_pairs={{0,3},{1,2},{2,1},{3,0},{4,7},{5,6},{6,5},{7,4},{8,11},{9,10},{10,... | collective-permute-start | bytes 589832 | tf_op jit(solution)/shard_map/ppermute | solution.py:134
  (12 other events, 92.5 us)

commit v7 on v6

--- a/solution.py
+++ b/solution.py
@@ -66,10 +66,10 @@
                 terms[c][:, cols] = product[c * rows:(c + 1) * rows]
 
 
-def load_kernel(w_hbm, wo_hbm, kc_hbm, vc_hbm, w, wo, kc, vc, sems):
+def load_kernel(w_hbm, wo_hbm, kc_hbm, vc_hbm, gain_hbm, w, wo, kc, vc, gain, sems):
     parts, _, width = w_hbm.shape
     pairs = [(w_hbm.at[i], w.at[:, pl.ds(i * width, width)]) for i in range(parts)]
-    pairs += [(wo_hbm, wo), (kc_hbm, kc), (vc_hbm, vc)]
+    pairs += [(wo_hbm, wo), (kc_hbm, kc), (vc_hbm, vc), (gain_hbm, gain)]
     copies = [pltpu.make_async_copy(a, b, sems.at[i]) for i, (a, b) in enumerate(pairs)]
     for copy in copies:
         copy.start()
@@ -77,16 +77,16 @@
         copy.wait()
 
 
-def loaded(w, wo, kc, vc):
+def loaded(w, wo, kc, vc, gain):
     parts, depth, width = w.shape
-    arrays = (w, wo, kc, vc)
-    shapes = [(depth, parts * width), wo.shape, kc.shape, vc.shape]
+    arrays = (w, wo, kc, vc, gain)
+    shapes = [(depth, parts * width)] + [a.shape for a in arrays[1:]]
     return pl.pallas_call(
         load_kernel,
         out_shape=[pltpu.VMEM(shape, w.dtype) for shape in shapes],
         in_specs=[pl.BlockSpec(memory_space=pl.ANY)] * len(arrays),
         out_specs=[pl.BlockSpec(memory_space=pltpu.VMEM)] * len(arrays),
-        scratch_shapes=[pltpu.SemaphoreType.DMA((parts + 3,))],
+        scratch_shapes=[pltpu.SemaphoreType.DMA((parts + 4,))],
         compiler_params=pltpu.CompilerParams(vmem_limit_bytes=VMEM_LIMIT),
         cost_estimate=pl.CostEstimate(
             flops=0, bytes_accessed=2 * sum(a.size for a in arrays), transcendentals=0
@@ -100,7 +100,7 @@
     vmem = pl.BlockSpec(memory_space=pltpu.VMEM)
     row_count = rows * chunks
     flops = 2 * row_count * (w.size + wo.size + 2 * kc.size)
-    held = [pltpu.with_memory_space_constraint(x, pltpu.VMEM) for x in (w, wo, kc, vc)]
+    held = [pltpu.with_memory_space_constraint(x, pltpu.VMEM) for x in (gain, w, wo, kc, vc)]
     cache = pltpu.VMEM(kc.shape, kc.dtype)
     out = pl.pallas_call(
         functools.partial(block_kernel, chunks),
@@ -116,13 +116,13 @@
         cost_estimate=pl.CostEstimate(
             flops=flops, bytes_accessed=2 * (w.size + wo.size), transcendentals=0
         ),
-    )(info, *blocks, gain, *held)
+    )(info, *blocks, *held)
     return out[:chunks], out[chunks], out[chunks + 1]
 
 
 STAY = ((0, 0), (1, 1), (2, 2), (3, 3))
 NEAR = ((0, 1), (1, 0), (2, 3), (3, 2))
-FAR = ((0, 3), (1, 2), (2, 1), (3, 0))
+FAR = ((0, 2), (1, 3), (2, 0), (3, 1))
 
 
 def send(block, pairs, hop=0):
@@ -153,7 +153,9 @@
     own, near, far, last = terms
     pair = summed(far, send(last, NEAR)).astype(jnp.bfloat16)
     near, pair = lax.optimization_barrier((near, pair))
-    return summed(own, send(near, NEAR), send(pair, FAR))
+    far = send(pair, FAR)
+    near = send(near, NEAR)
+    return lax.optimization_barrier(summed(own, far)) + near.astype(jnp.float32)
 
 
 def shards(
@@ -166,7 +168,11 @@
     patch_rows = state.shape[1] * n
     own = state[0]
     stored = (
-        jnp.transpose(qkv_weight[0], (1, 0, 2)), out_weight[0], stale_keys[0], stale_values[0]
+        jnp.transpose(qkv_weight[0], (1, 0, 2)),
+        out_weight[0],
+        stale_keys[0],
+        stale_values[0],
+        norm_gain,
     )
     held = []
 
@@ -176,13 +182,13 @@
         return far
 
     blocks = gathered(own, between=load)
-    w, wo, kc, vc = held
+    w, wo, kc, vc, gain = held
     for tick in range(TICKS):
         slot = patch_slot[(section_index - tick) % section_count]
         for index in range(PASSES):
             applies = block_count > index
             info = jnp.stack([slot * patch_rows, applies.astype(jnp.int32)])
-            terms, kc, vc = block_terms(info, blocks, norm_gain, w, wo, kc, vc)
+            terms, kc, vc = block_terms(info, blocks, gain, w, wo, kc, vc)
             updated = own.astype(jnp.float32) + scattered(terms)
             updated = jnp.where(applies, updated.astype(jnp.bfloat16), own)
             last = index == PASSES - 1

time: 226 us -> 242 us (1.071)
  waiting for transfers between devices: 135 us -> 159 us
  Pallas kernels: 23.8 us -> 15.9 us
    ppermute x39, waiting for transfers between devices: 135 us -> 159 us  [send(): return lax.ppermute(block, ('section', 'uly'), route)]
    pallas_call x6, Pallas kernels: 19.9 us -> 11.9 us  [block_terms(): pl.pallas_call(functools.partial(block_kernel, chunks), out_shape=[jax.Sh...]
    unnamed x11 -> x9, local copies, waits for them, and re-layouts: 6.53 us -> 6.53 us
  transfers between devices with their start and end apart: 39 -> 39, of which waited for: 38 -> 33; matrix products, arithmetic and copies ran while one was open for 0% -> 1% of each run, Pallas kernels for 2% -> 2%
where the time goes in v7:
time: 242 us; the launch traced here: 240 us
  waiting for transfers between devices  159 us (66%)
  starting transfers between devices  53.4 us (22%)
  Pallas kernels  15.9 us (7%)
  local copies, waits for them, and re-layouts  7.14 us (3%)
  between operations  2.72 us (1%)
    ppermute x39, waiting for transfers between devices, send(): return lax.ppermute(block, ('section', 'uly'), route)  159 us
    ppermute x39, starting transfers between devices, send(): return lax.ppermute(block, ('section', 'uly'), route)  53.4 us
    pallas_call x6, Pallas kernels, block_terms(): pl.pallas_call(functools.partial(block_kernel, chunks), out_shape=[jax.Sh...  11.9 us
    unnamed x9, local copies, waits for them, and re-layouts  6.53 us
  transfers between devices with their start and end apart: 39, of which 33 were waited for; matrix products, arithmetic and copies ran while one was open for 1% of the time, Pallas kernels for 2%

profile of v7, /device:TPU:14, one launch (start us, length us, event | category | flops | bytes accessed | tf_op | source)
XLA Modules:
  0.0 239.5 jit_solution(16000317465656036309)
XLA Ops:
  3.0 3.9 %shard_map.82 = (bf16[3072,1152]{1,0:T(8,128)(2,1)S(1)}, bf16[384,3072]{1,0:T(8,128)(2,1)S(1)}, bf16[512,384]{1,0:T(8,128)(2,1)S(1)}, bf16[512,384]{1,0:T(8,128)(2,1)S(1)}, bf16[1,3072]{1,0:T(2,128)(2,1)S(1)}) custom-call(bf16[3,3072,384]{2,1,0:T(8,128)(2,1)} %bitcast.14, bf16[384,3072]{1,0:T(8,128)(2,1)} %bitcast.15, bf16[512,384]{1,0:T(8,128)(2,1)} %bitcast.16, ...), custom_call_target="tpu_custom_call" | custom-call | bytes 10229760 | tf_op jit(solution)/shard_map/pallas_call | solution.py:84
  14.6 3.5 %collective-permute-done.2.refs_3_ = bf16[32,3072]{1,0:T(8,128)(2,1)} collective-permute-done((bf16[32,3072]{1,0:T(8,128)(2,1)S(1)}, bf16[32,3072]{1,0:T(8,128)(2,1)}, u32[]{:S(2)}, u32[]{:S(2)}) %collective-permute-start.2) | collective-permute-done | bytes 196640 | tf_op jit(solution)/shard_map/ppermute | solution.py:134
  18.1 3.0 %copy-done.1 = bf16[3072,1152]{1,0:T(8,128)(2,1)S(1)} copy-done((bf16[3072,1152]{1,0:T(8,128)(2,1)S(1)}, bf16[3072,1152]{1,0:T(8,128)(2,1)}, u32[]{:S(2)}) %copy-start.1) | copy-done | bytes 7077912
  21.1 3.7 %shard_map.83 = (bf16[32,3072]{1,0:T(8,128)(2,1)S(1)}, bf16[32,3072]{1,0:T(8,128)(2,1)S(1)}, bf16[32,3072]{1,0:T(8,128)(2,1)S(1)}, bf16[32,3072]{1,0:T(8,128)(2,...) custom-call(s32[2]{0:T(128)S(1)} %pad_add_fusion.1.info, ...), custom_call_target="tpu_custom_call", output_to_operand_aliasing={{4}: (8, {}), {5}: (9, {})} | custom-call | flops 1308622848 | bytes 9437184 | tf_op jit(solution)/shard_map/pallas_call | solution.py:105
  25.2 5.7 %collective-permute-done.3 = bf16[32,3072]{1,0:T(8,128)(2,1)S(1)} collective-permute-done((bf16[32,3072]{1,0:T(8,128)(2,1)S(1)}, bf16[32,3072]{1,0:T(8,128)(2,1)S(1)}, u32[]{:S(2)}, u32[]{:S(2)}) %collective-permute-start.3) | collective-permute-done | bytes 196640 | tf_op jit(solution)/shard_map/ppermute | solution.py:134
  30.9 3.3 %collective-permute-start.4 = (bf16[32,3072]{1,0:T(8,128)(2,1)S(1)}, bf16[32,3072]{1,0:T(8,128)(2,1)S(1)}, u32[]{:S(2)}, u32[]{:S(2)}) collective-permute-start(bf16[32,3072]{1,0:T(8,128)(2,1)S(1)} %add_convert_fusion.11), channel_id=1, source_target_pairs={{0,2},{1,3},{2,0},{3,1},{4,6},{5,7},{6,4},{7,5},{8,10},{9,11},{10,... | collective-permute-start | bytes 589832 | tf_op jit(solution)/shard_map/ppermute | solution.py:134
  34.8 6.2 %collective-permute-done.4 = bf16[32,3072]{1,0:T(8,128)(2,1)S(1)} collective-permute-done((bf16[32,3072]{1,0:T(8,128)(2,1)S(1)}, bf16[32,3072]{1,0:T(8,128)(2,1)S(1)}, u32[]{:S(2)}, u32[]{:S(2)}) %collective-permute-start.4) | collective-permute-done | bytes 196640 | tf_op jit(solution)/shard_map/ppermute | solution.py:134
  44.6 6.7 %collective-permute-done.7.refs_2_ = bf16[32,3072]{1,0:T(8,128)(2,1)S(1)} collective-permute-done((bf16[32,3072]{1,0:T(8,128)(2,1)S(1)}, bf16[32,3072]{1,0:T(8,128)(2,1)S(1)}, u32[]{:S(2)}, u32[]{:S(2)}) %collective-permute-start.7) | collective-permute-done | bytes 196640 | tf_op jit(solution)/shard_map/ppermute | solution.py:134
  51.3 3.0 %collective-permute-start.8 = (bf16[32,3072]{1,0:T(8,128)(2,1)S(1)}, bf16[32,3072]{1,0:T(8,128)(2,1)S(1)}, u32[]{:S(2)}, u32[]{:S(2)}) collective-permute-start(bf16[32,3072]{1,0:T(8,128)(2,1)S(1)} %collective-permute-done.7.refs_2_), channel_id=1, source_target_pairs={{0,1},{1,0},{2,3},{3,2},{4,5},{5,4},{6,7},{7,6},{8,9},{9,8},{10,11... | collective-permute-start | bytes 589832 | tf_op jit(solution)/shard_map/ppermute | solution.py:134
  54.4 4.2 %collective-permute-done.8.refs_3_ = bf16[32,3072]{1,0:T(8,128)(2,1)S(1)} collective-permute-done((bf16[32,3072]{1,0:T(8,128)(2,1)S(1)}, bf16[32,3072]{1,0:T(8,128)(2,1)S(1)}, u32[]{:S(2)}, u32[]{:S(2)}) %collective-permute-start.8) | collective-permute-done | bytes 196640 | tf_op jit(solution)/shard_map/ppermute | solution.py:134
  61.0 5.7 %collective-permute-done.9 = bf16[32,3072]{1,0:T(8,128)(2,1)S(1)} collective-permute-done((bf16[32,3072]{1,0:T(8,128)(2,1)S(1)}, bf16[32,3072]{1,0:T(8,128)(2,1)S(1)}, u32[]{:S(2)}, u32[]{:S(2)}) %collective-permute-start.9) | collective-permute-done | bytes 196640 | tf_op jit(solution)/shard_map/ppermute | solution.py:134
  68.9 8.3 %collective-permute-done.10 = bf16[32,3072]{1,0:T(8,128)(2,1)S(1)} collective-permute-done((bf16[32,3072]{1,0:T(8,128)(2,1)S(1)}, bf16[32,3072]{1,0:T(8,128)(2,1)S(1)}, u32[]{:S(2)}, u32[]{:S(2)}) %collective-permute-start.10) | collective-permute-done | bytes 196640 | tf_op jit(solution)/shard_map/ppermute | solution.py:134
  84.6 4.9 %collective-permute-done.14.refs_2_ = bf16[32,3072]{1,0:T(8,128)(2,1)S(1)} collective-permute-done((bf16[32,3072]{1,0:T(8,128)(2,1)S(1)}, bf16[32,3072]{1,0:T(8,128)(2,1)S(1)}, u32[]{:S(2)}, u32[]{:S(2)}) %collective-permute-start.14) | collective-permute-done | bytes 196640 | tf_op jit(solution)/shard_map/ppermute | solution.py:134
  91.3 5.9 %collective-permute-done.15.refs_3_ = bf16[32,3072]{1,0:T(8,128)(2,1)S(1)} collective-permute-done((bf16[32,3072]{1,0:T(8,128)(2,1)S(1)}, bf16[32,3072]{1,0:T(8,128)(2,1)S(1)}, u32[]{:S(2)}, u32[]{:S(2)}) %collective-permute-start.15) | collective-permute-done | bytes 196640 | tf_op jit(solution)/shard_map/ppermute | solution.py:134
  97.2 3.2 %shard_map.85 = (bf16[32,3072]{1,0:T(8,128)(2,1)S(1)}, bf16[32,3072]{1,0:T(8,128)(2,1)S(1)}, bf16[32,3072]{1,0:T(8,128)(2,1)S(1)}, bf16[32,3072]{1,0:T(8,128)(2,...) custom-call(s32[2]{0:T(128)S(1)} %pad_add_fusion.3.info, ...), custom_call_target="tpu_custom_call", output_to_operand_aliasing={{4}: (8, {}), {5}: (9, {})} | custom-call | flops 1308622848 | bytes 9437184 | tf_op jit(solution)/shard_map/pallas_call | solution.py:105
  101.2 6.2 %collective-permute-done.16 = bf16[32,3072]{1,0:T(8,128)(2,1)S(1)} collective-permute-done((bf16[32,3072]{1,0:T(8,128)(2,1)S(1)}, bf16[32,3072]{1,0:T(8,128)(2,1)S(1)}, u32[]{:S(2)}, u32[]{:S(2)}) %collective-permute-start.16) | collective-permute-done | bytes 196640 | tf_op jit(solution)/shard_map/ppermute | solution.py:134
  109.7 7.6 %collective-permute-done.17 = bf16[32,3072]{1,0:T(8,128)(2,1)S(1)} collective-permute-done((bf16[32,3072]{1,0:T(8,128)(2,1)S(1)}, bf16[32,3072]{1,0:T(8,128)(2,1)S(1)}, u32[]{:S(2)}, u32[]{:S(2)}) %collective-permute-start.17) | collective-permute-done | bytes 196640 | tf_op jit(solution)/shard_map/ppermute | solution.py:134
  121.0 7.7 %collective-permute-done.20.refs_2_ = bf16[32,3072]{1,0:T(8,128)(2,1)S(1)} collective-permute-done((bf16[32,3072]{1,0:T(8,128)(2,1)S(1)}, bf16[32,3072]{1,0:T(8,128)(2,1)S(1)}, u32[]{:S(2)}, u32[]{:S(2)}) %collective-permute-start.20) | collective-permute-done | bytes 196640 | tf_op jit(solution)/shard_map/ppermute | solution.py:134
  128.7 3.0 %collective-permute-start.21 = (bf16[32,3072]{1,0:T(8,128)(2,1)S(1)}, bf16[32,3072]{1,0:T(8,128)(2,1)S(1)}, u32[]{:S(2)}, u32[]{:S(2)}) collective-permute-start(bf16[32,3072]{1,0:T(8,128)(2,1)S(1)} %collective-permute-done.20.refs_2_), channel_id=1, source_target_pairs={{0,1},{1,0},{2,3},{3,2},{4,5},{5,4},{6,7},{7,6},{8,9},{9,8},{10,11... | collective-permute-start | bytes 589832 | tf_op jit(solution)/shard_map/ppermute | solution.py:134
  131.8 4.9 %collective-permute-done.21.refs_3_ = bf16[32,3072]{1,0:T(8,128)(2,1)S(1)} collective-permute-done((bf16[32,3072]{1,0:T(8,128)(2,1)S(1)}, bf16[32,3072]{1,0:T(8,128)(2,1)S(1)}, u32[]{:S(2)}, u32[]{:S(2)}) %collective-permute-start.21) | collective-permute-done | bytes 196640 | tf_op jit(solution)/shard_map/ppermute | solution.py:134
  139.1 4.9 %collective-permute-done.22 = bf16[32,3072]{1,0:T(8,128)(2,1)S(1)} collective-permute-done((bf16[32,3072]{1,0:T(8,128)(2,1)S(1)}, bf16[32,3072]{1,0:T(8,128)(2,1)S(1)}, u32[]{:S(2)}, u32[]{:S(2)}) %collective-permute-start.22) | collective-permute-done | bytes 196640 | tf_op jit(solution)/shard_map/ppermute | solution.py:134
  146.7 8.9 %collective-permute-done.23 = bf16[32,3072]{1,0:T(8,128)(2,1)S(1)} collective-permute-done((bf16[32,3072]{1,0:T(8,128)(2,1)S(1)}, bf16[32,3072]{1,0:T(8,128)(2,1)S(1)}, u32[]{:S(2)}, u32[]{:S(2)}) %collective-permute-start.23) | collective-permute-done | bytes 196640 | tf_op jit(solution)/shard_map/ppermute | solution.py:134
  160.3 7.5 %collective-permute-done.27.refs_2_ = bf16[32,3072]{1,0:T(8,128)(2,1)S(1)} collective-permute-done((bf16[32,3072]{1,0:T(8,128)(2,1)S(1)}, bf16[32,3072]{1,0:T(8,128)(2,1)S(1)}, u32[]{:S(2)}, u32[]{:S(2)}) %collective-permute-start.27) | collective-permute-done | bytes 196640 | tf_op jit(solution)/shard_map/ppermute | solution.py:134
  169.1 6.5 %collective-permute-done.28.refs_3_ = bf16[32,3072]{1,0:T(8,128)(2,1)S(1)} collective-permute-done((bf16[32,3072]{1,0:T(8,128)(2,1)S(1)}, bf16[32,3072]{1,0:T(8,128)(2,1)S(1)}, u32[]{:S(2)}, u32[]{:S(2)}) %collective-permute-start.28) | collective-permute-done | bytes 196640 | tf_op jit(solution)/shard_map/ppermute | solution.py:134
  175.6 3.4 %shard_map.87 = (bf16[32,3072]{1,0:T(8,128)(2,1)S(1)}, bf16[32,3072]{1,0:T(8,128)(2,1)S(1)}, bf16[32,3072]{1,0:T(8,128)(2,1)S(1)}, bf16[32,3072]{1,0:T(8,128)(2,...) custom-call(s32[2]{0:T(128)S(1)} %pad_add_fusion.5.info, ...), custom_call_target="tpu_custom_call", output_to_operand_aliasing={{4}: (8, {}), {5}: (9, {})} | custom-call | flops 1308622848 | bytes 9437184 | tf_op jit(solution)/shard_map/pallas_call | solution.py:105
  179.0 6.9 %collective-permute-done.29 = bf16[32,3072]{1,0:T(8,128)(2,1)S(1)} collective-permute-done((bf16[32,3072]{1,0:T(8,128)(2,1)S(1)}, bf16[32,3072]{1,0:T(8,128)(2,1)S(1)}, u32[]{:S(2)}, u32[]{:S(2)}) %collective-permute-start.29) | collective-permute-done | bytes 196640 | tf_op jit(solution)/shard_map/ppermute | solution.py:134
  188.4 6.4 %collective-permute-done.30 = bf16[32,3072]{1,0:T(8,128)(2,1)S(1)} collective-permute-done((bf16[32,3072]{1,0:T(8,128)(2,1)S(1)}, bf16[32,3072]{1,0:T(8,128)(2,1)S(1)}, u32[]{:S(2)}, u32[]{:S(2)}) %collective-permute-start.30) | collective-permute-done | bytes 196640 | tf_op jit(solution)/shard_map/ppermute | solution.py:134
  199.5 6.4 %collective-permute-done.33.refs_2_ = bf16[32,3072]{1,0:T(8,128)(2,1)S(1)} collective-permute-done((bf16[32,3072]{1,0:T(8,128)(2,1)S(1)}, bf16[32,3072]{1,0:T(8,128)(2,1)S(1)}, u32[]{:S(2)}, u32[]{:S(2)}) %collective-permute-start.33) | collective-permute-done | bytes 196640 | tf_op jit(solution)/shard_map/ppermute | solution.py:134
  208.8 4.8 %collective-permute-done.34.refs_3_ = bf16[32,3072]{1,0:T(8,128)(2,1)S(1)} collective-permute-done((bf16[32,3072]{1,0:T(8,128)(2,1)S(1)}, bf16[32,3072]{1,0:T(8,128)(2,1)S(1)}, u32[]{:S(2)}, u32[]{:S(2)}) %collective-permute-start.34) | collective-permute-done | bytes 196640 | tf_op jit(solution)/shard_map/ppermute | solution.py:134
  216.0 5.1 %collective-permute-done.35 = bf16[32,3072]{1,0:T(8,128)(2,1)S(1)} collective-permute-done((bf16[32,3072]{1,0:T(8,128)(2,1)S(1)}, bf16[32,3072]{1,0:T(8,128)(2,1)S(1)}, u32[]{:S(2)}, u32[]{:S(2)}) %collective-permute-start.35) | collective-permute-done | bytes 196640 | tf_op jit(solution)/shard_map/ppermute | solution.py:134
  223.8 8.9 %collective-permute-done.36 = bf16[32,3072]{1,0:T(8,128)(2,1)S(1)} collective-permute-done((bf16[32,3072]{1,0:T(8,128)(2,1)S(1)}, bf16[32,3072]{1,0:T(8,128)(2,1)S(1)}, u32[]{:S(2)}, u32[]{:S(2)}) %collective-permute-start.36) | collective-permute-done | bytes 196640 | tf_op jit(solution)/shard_map/ppermute | solution.py:134
  233.9 5.0 %collective-permute-done.38 = bf16[32,3072]{1,0:T(8,128)(2,1)S(1)} collective-permute-done((bf16[32,3072]{1,0:T(8,128)(2,1)S(1)}, bf16[32,3072]{1,0:T(8,128)(2,1)S(1)}, u32[]{:S(2)}, u32[]{:S(2)}) %collective-permute-start.38) | collective-permute-done | bytes 196640 | tf_op jit(solution)/shard_map/ppermute | solution.py:134
  (87 shorter events, 61.5 us)
Async XLA Ops:
  0.0 11.2 %collective-permute-start.1 = (bf16[32,3072]{1,0:T(8,128)(2,1)}, bf16[32,3072]{1,0:T(8,128)(2,1)S(1)}, u32[]{:S(2)}, u32[]{:S(2)}) collective-permute-start(bf16[32,3072]{1,0:T(8,128)(2,1)} %bitcast.11), channel_id=1, source_target_pairs={{0,2},{1,3},{2,0},{3,1},{4,6},{5,7},{6,4},{7,5},{8,10},{9,11},{10,... | collective-permute-start | bytes 589832 | tf_op jit(solution)/shard_map/ppermute | solution.py:134
  2.6 12.0 %collective-permute-start = (bf16[32,3072]{1,0:T(8,128)(2,1)}, bf16[32,3072]{1,0:T(8,128)(2,1)}, u32[]{:S(2)}, u32[]{:S(2)}) collective-permute-start(bf16[32,3072]{1,0:T(8,128)(2,1)} %bitcast.12), channel_id=1, source_target_pairs={{0,1},{1,0},{2,3},{3,2},{4,5},{5,4},{6,7},{7,6},{8,9},{9,8},{10,11... | collective-permute-start | bytes 589832 | tf_op jit(solution)/shard_map/ppermute | solution.py:134
  30.9 10.1 %collective-permute-start.4 = (bf16[32,3072]{1,0:T(8,128)(2,1)S(1)}, bf16[32,3072]{1,0:T(8,128)(2,1)S(1)}, u32[]{:S(2)}, u32[]{:S(2)}) collective-permute-start(bf16[32,3072]{1,0:T(8,128)(2,1)S(1)} %add_convert_fusion.11), channel_id=1, source_target_pairs={{0,2},{1,3},{2,0},{3,1},{4,6},{5,7},{6,4},{7,5},{8,10},{9,11},{10,... | collective-permute-start | bytes 589832 | tf_op jit(solution)/shard_map/ppermute | solution.py:134
  34.2 8.2 %collective-permute-start.5 = (bf16[32,3072]{1,0:T(8,128)(2,1)S(1)}, bf16[32,3072]{1,0:T(8,128)(2,1)S(1)}, u32[]{:S(2)}, u32[]{:S(2)}) collective-permute-start(bf16[32,3072]{1,0:T(8,128)(2,1)S(1)} %get-tuple-element.78), channel_id=1, source_target_pairs={{0,1},{1,0},{2,3},{3,2},{4,5},{5,4},{6,7},{7,6},{8,9},{9,8},{10,11... | collective-permute-start | bytes 589832 | tf_op jit(solution)/shard_map/ppermute | solution.py:134
  42.5 8.8 %collective-permute-start.7 = (bf16[32,3072]{1,0:T(8,128)(2,1)S(1)}, bf16[32,3072]{1,0:T(8,128)(2,1)S(1)}, u32[]{:S(2)}, u32[]{:S(2)}) collective-permute-start(bf16[32,3072]{1,0:T(8,128)(2,1)S(1)} %fusion.refs_0_), channel_id=1, source_target_pairs={{0,2},{1,3},{2,0},{3,1},{4,6},{5,7},{6,4},{7,5},{8,10},{9,11},{10,... | collective-permute-start | bytes 589832 | tf_op jit(solution)/shard_map/ppermute | solution.py:134
  44.6 9.8 %collective-permute-start.6 = (bf16[32,3072]{1,0:T(8,128)(2,1)S(1)}, bf16[32,3072]{1,0:T(8,128)(2,1)S(1)}, u32[]{:S(2)}, u32[]{:S(2)}) collective-permute-start(bf16[32,3072]{1,0:T(8,128)(2,1)S(1)} %fusion.refs_0_), channel_id=1, source_target_pairs={{0,1},{1,0},{2,3},{3,2},{4,5},{5,4},{6,7},{7,6},{8,9},{9,8},{10,11... | collective-permute-start | bytes 589832 | tf_op jit(solution)/shard_map/ppermute | solution.py:134
  51.3 7.3 %collective-permute-start.8 = (bf16[32,3072]{1,0:T(8,128)(2,1)S(1)}, bf16[32,3072]{1,0:T(8,128)(2,1)S(1)}, u32[]{:S(2)}, u32[]{:S(2)}) collective-permute-start(bf16[32,3072]{1,0:T(8,128)(2,1)S(1)} %collective-permute-done.7.refs_2_), channel_id=1, source_target_pairs={{0,1},{1,0},{2,3},{3,2},{4,5},{5,4},{6,7},{7,6},{8,9},{9,8},{10,11... | collective-permute-start | bytes 589832 | tf_op jit(solution)/shard_map/ppermute | solution.py:134
  59.2 7.6 %collective-permute-start.9 = (bf16[32,3072]{1,0:T(8,128)(2,1)S(1)}, bf16[32,3072]{1,0:T(8,128)(2,1)S(1)}, u32[]{:S(2)}, u32[]{:S(2)}) collective-permute-start(bf16[32,3072]{1,0:T(8,128)(2,1)S(1)} %get-tuple-element.84), channel_id=1, source_target_pairs={{0,1},{1,0},{2,3},{3,2},{4,5},{5,4},{6,7},{7,6},{8,9},{9,8},{10,11... | collective-permute-start | bytes 589832 | tf_op jit(solution)/shard_map/ppermute | solution.py:134
  66.8 10.5 %collective-permute-start.10 = (bf16[32,3072]{1,0:T(8,128)(2,1)S(1)}, bf16[32,3072]{1,0:T(8,128)(2,1)S(1)}, u32[]{:S(2)}, u32[]{:S(2)}) collective-permute-start(bf16[32,3072]{1,0:T(8,128)(2,1)S(1)} %add_convert_fusion.9), channel_id=1, source_target_pairs={{0,2},{1,3},{2,0},{3,1},{4,6},{5,7},{6,4},{7,5},{8,10},{9,11},{10,... | collective-permute-start | bytes 589832 | tf_op jit(solution)/shard_map/ppermute | solution.py:134
  68.5 9.8 %collective-permute-start.11 = (bf16[32,3072]{1,0:T(8,128)(2,1)S(1)}, bf16[32,3072]{1,0:T(8,128)(2,1)S(1)}, u32[]{:S(2)}, u32[]{:S(2)}) collective-permute-start(bf16[32,3072]{1,0:T(8,128)(2,1)S(1)} %get-tuple-element.86), channel_id=1, source_target_pairs={{0,1},{1,0},{2,3},{3,2},{4,5},{5,4},{6,7},{7,6},{8,9},{9,8},{10,11... | collective-permute-start | bytes 589832 | tf_op jit(solution)/shard_map/ppermute | solution.py:134
  78.4 11.0 %collective-permute-start.14 = (bf16[32,3072]{1,0:T(8,128)(2,1)S(1)}, bf16[32,3072]{1,0:T(8,128)(2,1)S(1)}, u32[]{:S(2)}, u32[]{:S(2)}) collective-permute-start(bf16[32,3072]{1,0:T(8,128)(2,1)S(1)} %fusion.1), channel_id=1, source_target_pairs={{0,6},{1,7},{2,4},{3,5},{4,10},{5,11},{6,8},{7,9},{8,14},{9,15},{1... | collective-permute-start | bytes 589832 | tf_op jit(solution)/shard_map/ppermute | solution.py:134
  80.4 10.9 %collective-permute-start.13 = (bf16[32,3072]{1,0:T(8,128)(2,1)S(1)}, bf16[32,3072]{1,0:T(8,128)(2,1)S(1)}, u32[]{:S(2)}, u32[]{:S(2)}) collective-permute-start(bf16[32,3072]{1,0:T(8,128)(2,1)S(1)} %fusion.1), channel_id=1, source_target_pairs={{0,5},{1,4},{2,7},{3,6},{4,9},{5,8},{6,11},{7,10},{8,13},{9,12},{1... | collective-permute-start | bytes 589832 | tf_op jit(solution)/shard_map/ppermute | solution.py:134
  82.9 8.4 %collective-permute-start.12 = (bf16[32,3072]{1,0:T(8,128)(2,1)S(1)}, bf16[32,3072]{1,0:T(8,128)(2,1)S(1)}, u32[]{:S(2)}, u32[]{:S(2)}) collective-permute-start(bf16[32,3072]{1,0:T(8,128)(2,1)S(1)} %fusion.1), channel_id=1, source_target_pairs={{0,4},{1,5},{2,6},{3,7},{4,8},{5,9},{6,10},{7,11},{8,12},{9,13},{1... | collective-permute-start | bytes 589832 | tf_op jit(solution)/shard_map/ppermute | solution.py:134
  89.4 7.8 %collective-permute-start.15 = (bf16[32,3072]{1,0:T(8,128)(2,1)S(1)}, bf16[32,3072]{1,0:T(8,128)(2,1)S(1)}, u32[]{:S(2)}, u32[]{:S(2)}) collective-permute-start(bf16[32,3072]{1,0:T(8,128)(2,1)S(1)} %collective-permute-done.14.refs_2_), channel_id=1, source_target_pairs={{0,1},{1,0},{2,3},{3,2},{4,5},{5,4},{6,7},{7,6},{8,9},{9,8},{10,11... | collective-permute-start | bytes 589832 | tf_op jit(solution)/shard_map/ppermute | solution.py:134
  107.4 9.8 %collective-permute-start.17 = (bf16[32,3072]{1,0:T(8,128)(2,1)S(1)}, bf16[32,3072]{1,0:T(8,128)(2,1)S(1)}, u32[]{:S(2)}, u32[]{:S(2)}) collective-permute-start(bf16[32,3072]{1,0:T(8,128)(2,1)S(1)} %add_convert_fusion.7), channel_id=1, source_target_pairs={{0,2},{1,3},{2,0},{3,1},{4,6},{5,7},{6,4},{7,5},{8,10},{9,11},{10,... | collective-permute-start | bytes 589832 | tf_op jit(solution)/shard_map/ppermute | solution.py:134
  108.8 9.5 %collective-permute-start.18 = (bf16[32,3072]{1,0:T(8,128)(2,1)S(1)}, bf16[32,3072]{1,0:T(8,128)(2,1)S(1)}, u32[]{:S(2)}, u32[]{:S(2)}) collective-permute-start(bf16[32,3072]{1,0:T(8,128)(2,1)S(1)} %get-tuple-element.94), channel_id=1, source_target_pairs={{0,1},{1,0},{2,3},{3,2},{4,5},{5,4},{6,7},{7,6},{8,9},{9,8},{10,11... | collective-permute-start | bytes 589832 | tf_op jit(solution)/shard_map/ppermute | solution.py:134
  118.4 10.3 %collective-permute-start.20 = (bf16[32,3072]{1,0:T(8,128)(2,1)S(1)}, bf16[32,3072]{1,0:T(8,128)(2,1)S(1)}, u32[]{:S(2)}, u32[]{:S(2)}) collective-permute-start(bf16[32,3072]{1,0:T(8,128)(2,1)S(1)} %fusion.2.refs_0_), channel_id=1, source_target_pairs={{0,2},{1,3},{2,0},{3,1},{4,6},{5,7},{6,4},{7,5},{8,10},{9,11},{10,... | collective-permute-start | bytes 589832 | tf_op jit(solution)/shard_map/ppermute | solution.py:134
  121.0 10.8 %collective-permute-start.19 = (bf16[32,3072]{1,0:T(8,128)(2,1)S(1)}, bf16[32,3072]{1,0:T(8,128)(2,1)S(1)}, u32[]{:S(2)}, u32[]{:S(2)}) collective-permute-start(bf16[32,3072]{1,0:T(8,128)(2,1)S(1)} %fusion.2.refs_0_), channel_id=1, source_target_pairs={{0,1},{1,0},{2,3},{3,2},{4,5},{5,4},{6,7},{7,6},{8,9},{9,8},{10,11... | collective-permute-start | bytes 589832 | tf_op jit(solution)/shard_map/ppermute | solution.py:134
  128.7 8.1 %collective-permute-start.21 = (bf16[32,3072]{1,0:T(8,128)(2,1)S(1)}, bf16[32,3072]{1,0:T(8,128)(2,1)S(1)}, u32[]{:S(2)}, u32[]{:S(2)}) collective-permute-start(bf16[32,3072]{1,0:T(8,128)(2,1)S(1)} %collective-permute-done.20.refs_2_), channel_id=1, source_target_pairs={{0,1},{1,0},{2,3},{3,2},{4,5},{5,4},{6,7},{7,6},{8,9},{9,8},{10,11... | collective-permute-start | bytes 589832 | tf_op jit(solution)/shard_map/ppermute | solution.py:134
  144.1 11.5 %collective-permute-start.23 = (bf16[32,3072]{1,0:T(8,128)(2,1)S(1)}, bf16[32,3072]{1,0:T(8,128)(2,1)S(1)}, u32[]{:S(2)}, u32[]{:S(2)}) collective-permute-start(bf16[32,3072]{1,0:T(8,128)(2,1)S(1)} %add_convert_fusion.5), channel_id=1, source_target_pairs={{0,2},{1,3},{2,0},{3,1},{4,6},{5,7},{6,4},{7,5},{8,10},{9,11},{10,... | collective-permute-start | bytes 589832 | tf_op jit(solution)/shard_map/ppermute | solution.py:134
  146.7 9.9 %collective-permute-start.24 = (bf16[32,3072]{1,0:T(8,128)(2,1)S(1)}, bf16[32,3072]{1,0:T(8,128)(2,1)S(1)}, u32[]{:S(2)}, u32[]{:S(2)}) collective-permute-start(bf16[32,3072]{1,0:T(8,128)(2,1)S(1)} %get-tuple-element.102), channel_id=1, source_target_pairs={{0,1},{1,0},{2,3},{3,2},{4,5},{5,4},{6,7},{7,6},{8,9},{9,8},{10,11... | collective-permute-start | bytes 589832 | tf_op jit(solution)/shard_map/ppermute | solution.py:134
  156.6 11.2 %collective-permute-start.27 = (bf16[32,3072]{1,0:T(8,128)(2,1)S(1)}, bf16[32,3072]{1,0:T(8,128)(2,1)S(1)}, u32[]{:S(2)}, u32[]{:S(2)}) collective-permute-start(bf16[32,3072]{1,0:T(8,128)(2,1)S(1)} %fusion.3), channel_id=1, source_target_pairs={{0,6},{1,7},{2,4},{3,5},{4,10},{5,11},{6,8},{7,9},{8,14},{9,15},{1... | collective-permute-start | bytes 589832 | tf_op jit(solution)/shard_map/ppermute | solution.py:134
  158.8 10.3 %collective-permute-start.26 = (bf16[32,3072]{1,0:T(8,128)(2,1)S(1)}, bf16[32,3072]{1,0:T(8,128)(2,1)S(1)}, u32[]{:S(2)}, u32[]{:S(2)}) collective-permute-start(bf16[32,3072]{1,0:T(8,128)(2,1)S(1)} %fusion.3), channel_id=1, source_target_pairs={{0,5},{1,4},{2,7},{3,6},{4,9},{5,8},{6,11},{7,10},{8,13},{9,12},{1... | collective-permute-start | bytes 589832 | tf_op jit(solution)/shard_map/ppermute | solution.py:134
  159.6 9.5 %collective-permute-start.25 = (bf16[32,3072]{1,0:T(8,128)(2,1)S(1)}, bf16[32,3072]{1,0:T(8,128)(2,1)S(1)}, u32[]{:S(2)}, u32[]{:S(2)}) collective-permute-start(bf16[32,3072]{1,0:T(8,128)(2,1)S(1)} %fusion.3), channel_id=1, source_target_pairs={{0,4},{1,5},{2,6},{3,7},{4,8},{5,9},{6,10},{7,11},{8,12},{9,13},{1... | collective-permute-start | bytes 589832 | tf_op jit(solution)/shard_map/ppermute | solution.py:134
  167.8 7.7 %collective-permute-start.28 = (bf16[32,3072]{1,0:T(8,128)(2,1)S(1)}, bf16[32,3072]{1,0:T(8,128)(2,1)S(1)}, u32[]{:S(2)}, u32[]{:S(2)}) collective-permute-start(bf16[32,3072]{1,0:T(8,128)(2,1)S(1)} %collective-permute-done.27.refs_2_), channel_id=1, source_target_pairs={{0,1},{1,0},{2,3},{3,2},{4,5},{5,4},{6,7},{7,6},{8,9},{9,8},{10,11... | collective-permute-start | bytes 589832 | tf_op jit(solution)/shard_map/ppermute | solution.py:134
  186.0 8.8 %collective-permute-start.30 = (bf16[32,3072]{1,0:T(8,128)(2,1)S(1)}, bf16[32,3072]{1,0:T(8,128)(2,1)S(1)}, u32[]{:S(2)}, u32[]{:S(2)}) collective-permute-start(bf16[32,3072]{1,0:T(8,128)(2,1)S(1)} %add_convert_fusion.3), channel_id=1, source_target_pairs={{0,2},{1,3},{2,0},{3,1},{4,6},{5,7},{6,4},{7,5},{8,10},{9,11},{10,... | collective-permute-start | bytes 589832 | tf_op jit(solution)/shard_map/ppermute | solution.py:134
  186.6 10.1 %collective-permute-start.31 = (bf16[32,3072]{1,0:T(8,128)(2,1)S(1)}, bf16[32,3072]{1,0:T(8,128)(2,1)S(1)}, u32[]{:S(2)}, u32[]{:S(2)}) collective-permute-start(bf16[32,3072]{1,0:T(8,128)(2,1)S(1)} %get-tuple-element.110), channel_id=1, source_target_pairs={{0,1},{1,0},{2,3},{3,2},{4,5},{5,4},{6,7},{7,6},{8,9},{9,8},{10,11... | collective-permute-start | bytes 589832 | tf_op jit(solution)/shard_map/ppermute | solution.py:134
  196.8 9.1 %collective-permute-start.33 = (bf16[32,3072]{1,0:T(8,128)(2,1)S(1)}, bf16[32,3072]{1,0:T(8,128)(2,1)S(1)}, u32[]{:S(2)}, u32[]{:S(2)}) collective-permute-start(bf16[32,3072]{1,0:T(8,128)(2,1)S(1)} %fusion.4.refs_0_), channel_id=1, source_target_pairs={{0,2},{1,3},{2,0},{3,1},{4,6},{5,7},{6,4},{7,5},{8,10},{9,11},{10,... | collective-permute-start | bytes 589832 | tf_op jit(solution)/shard_map/ppermute | solution.py:134
  198.4 10.4 %collective-permute-start.32 = (bf16[32,3072]{1,0:T(8,128)(2,1)S(1)}, bf16[32,3072]{1,0:T(8,128)(2,1)S(1)}, u32[]{:S(2)}, u32[]{:S(2)}) collective-permute-start(bf16[32,3072]{1,0:T(8,128)(2,1)S(1)} %fusion.4.refs_0_), channel_id=1, source_target_pairs={{0,1},{1,0},{2,3},{3,2},{4,5},{5,4},{6,7},{7,6},{8,9},{9,8},{10,11... | collective-permute-start | bytes 589832 | tf_op jit(solution)/shard_map/ppermute | solution.py:134
  205.9 7.7 %collective-permute-start.34 = (bf16[32,3072]{1,0:T(8,128)(2,1)S(1)}, bf16[32,3072]{1,0:T(8,128)(2,1)S(1)}, u32[]{:S(2)}, u32[]{:S(2)}) collective-permute-start(bf16[32,3072]{1,0:T(8,128)(2,1)S(1)} %collective-permute-done.33.refs_2_), channel_id=1, source_target_pairs={{0,1},{1,0},{2,3},{3,2},{4,5},{5,4},{6,7},{7,6},{8,9},{9,8},{10,11... | collective-permute-start | bytes 589832 | tf_op jit(solution)/shard_map/ppermute | solution.py:134
  221.1 11.5 %collective-permute-start.36 = (bf16[32,3072]{1,0:T(8,128)(2,1)S(1)}, bf16[32,3072]{1,0:T(8,128)(2,1)S(1)}, u32[]{:S(2)}, u32[]{:S(2)}) collective-permute-start(bf16[32,3072]{1,0:T(8,128)(2,1)S(1)} %add_convert_fusion.1), channel_id=1, source_target_pairs={{0,2},{1,3},{2,0},{3,1},{4,6},{5,7},{6,4},{7,5},{8,10},{9,11},{10,... | collective-permute-start | bytes 589832 | tf_op jit(solution)/shard_map/ppermute | solution.py:134
  223.7 9.9 %collective-permute-start.37 = (bf16[32,3072]{1,0:T(8,128)(2,1)S(1)}, bf16[32,3072]{1,0:T(8,128)(2,1)S(1)}, u32[]{:S(2)}, u32[]{:S(2)}) collective-permute-start(bf16[32,3072]{1,0:T(8,128)(2,1)S(1)} %get-tuple-element.118), channel_id=1, source_target_pairs={{0,1},{1,0},{2,3},{3,2},{4,5},{5,4},{6,7},{7,6},{8,9},{9,8},{10,11... | collective-permute-start | bytes 589832 | tf_op jit(solution)/shard_map/ppermute | solution.py:134
  (11 other events, 82.9 us)

commit v8 on v7

--- a/solution.py
+++ b/solution.py
@@ -11,7 +11,7 @@
 HD = 128
 TICKS = 3
 PASSES = 2
-VMEM_LIMIT = 24 * 2**20
+VMEM_LIMIT = 12 * 2**20
 SCALE = HD ** (-0.5) * math.log2(math.e)
 OUT_STEPS = 3
 
@@ -122,7 +122,7 @@
 
 STAY = ((0, 0), (1, 1), (2, 2), (3, 3))
 NEAR = ((0, 1), (1, 0), (2, 3), (3, 2))
-FAR = ((0, 2), (1, 3), (2, 0), (3, 1))
+FAR = ((0, 3), (1, 2), (2, 1), (3, 0))
 
 
 def send(block, pairs, hop=0):
@@ -141,11 +141,10 @@
     return total
 
 
-def gathered(own, hop=0, between=lambda far: far):
+def gathered(own, hop=0):
     far = send(own, FAR, hop)
     near = send(own, NEAR, hop)
     first = send(own, STAY, hop) if hop else own
-    far = between(far)
     return [first, near, far, send(far, NEAR)]
 
 
@@ -174,15 +173,8 @@
         stale_values[0],
         norm_gain,
     )
-    held = []
-
-    def load(far):
-        far, *rest = lax.optimization_barrier((far, *loaded(*stored)))
-        held.extend(rest)
-        return far
-
-    blocks = gathered(own, between=load)
-    w, wo, kc, vc, gain = held
+    w, wo, kc, vc, gain = loaded(*stored)
+    blocks = gathered(own)
     for tick in range(TICKS):
         slot = patch_slot[(section_index - tick) % section_count]
         for index in range(PASSES):

time: 242 us -> 234 us (0.967)
  the two profiles are of different devices: /device:TPU:14 before, /device:TPU:0 now
where the time goes in v8:
time: 234 us; the launch traced here: 232 us
  waiting for transfers between devices  152 us (65%)
  starting transfers between devices  58.4 us (25%)
  Pallas kernels  15.4 us (7%)
  between operations  2.72 us (1%)
    ppermute x39, waiting for transfers between devices, send(): return lax.ppermute(block, ('section', 'uly'), route)  152 us
    ppermute x39, starting transfers between devices, send(): return lax.ppermute(block, ('section', 'uly'), route)  58.4 us
    pallas_call x6, Pallas kernels, block_terms(): pl.pallas_call(functools.partial(block_kernel, chunks), out_shape=[jax.Sh...  11.5 us
  transfers between devices with their start and end apart: 39, of which 33 were waited for; matrix products, arithmetic and copies ran while one was open for 1% of the time, Pallas kernels for 2%

profile of v8, /device:TPU:0, one launch (start us, length us, event | category | flops | bytes accessed | tf_op | source)
XLA Modules:
  0.0 231.8 jit_solution(1405308763701529403)
XLA Ops:
  0.0 5.0 %collective-permute-start.1 = (bf16[32,3072]{1,0:T(8,128)(2,1)}, bf16[32,3072]{1,0:T(8,128)(2,1)S(1)}, u32[]{:S(2)}, u32[]{:S(2)}) collective-permute-start(bf16[32,3072]{1,0:T(8,128)(2,1)} %bitcast.11), channel_id=1, source_target_pairs={{0,3},{1,2},{2,1},{3,0},{4,7},{5,6},{6,5},{7,4},{8,11},{9,10},{10,... | collective-permute-start | bytes 589832 | tf_op jit(solution)/shard_map/ppermute | solution.py:134
  5.1 6.1 %collective-permute-done.1.refs_2_ = bf16[32,3072]{1,0:T(8,128)(2,1)S(1)} collective-permute-done((bf16[32,3072]{1,0:T(8,128)(2,1)}, bf16[32,3072]{1,0:T(8,128)(2,1)S(1)}, u32[]{:S(2)}, u32[]{:S(2)}) %collective-permute-start.1) | collective-permute-done | bytes 196640 | tf_op jit(solution)/shard_map/ppermute | solution.py:134
  16.8 3.9 %shard_map.82 = (bf16[3072,1152]{1,0:T(8,128)(2,1)S(1)}, bf16[384,3072]{1,0:T(8,128)(2,1)S(1)}, bf16[512,384]{1,0:T(8,128)(2,1)S(1)}, bf16[512,384]{1,0:T(8,128)(2,1)S(1)}, bf16[1,3072]{1,0:T(2,128)(2,1)S(1)}) custom-call(bf16[3,3072,384]{2,1,0:T(8,128)(2,1)} %bitcast.14, bf16[384,3072]{1,0:T(8,128)(2,1)} %bitcast.15, bf16[512,384]{1,0:T(8,128)(2,1)} %bitcast.16, ...), custom_call_target="tpu_custom_call" | custom-call | bytes 10229760 | tf_op jit(solution)/shard_map/pallas_call | solution.py:84
  20.8 3.2 %shard_map.83 = (bf16[32,3072]{1,0:T(8,128)(2,1)S(1)}, bf16[32,3072]{1,0:T(8,128)(2,1)S(1)}, bf16[32,3072]{1,0:T(8,128)(2,1)S(1)}, bf16[32,3072]{1,0:T(8,128)(2,...) custom-call(s32[2]{0:T(128)S(1)} %pad_add_fusion.1.info, ...), custom_call_target="tpu_custom_call", output_to_operand_aliasing={{4}: (8, {}), {5}: (9, {})} | custom-call | flops 1308622848 | bytes 9437184 | tf_op jit(solution)/shard_map/pallas_call | solution.py:105
  24.1 5.7 %collective-permute-done.3 = bf16[32,3072]{1,0:T(8,128)(2,1)S(1)} collective-permute-done((bf16[32,3072]{1,0:T(8,128)(2,1)S(1)}, bf16[32,3072]{1,0:T(8,128)(2,1)S(1)}, u32[]{:S(2)}, u32[]{:S(2)}) %collective-permute-start.3) | collective-permute-done | bytes 196640 | tf_op jit(solution)/shard_map/ppermute | solution.py:134
  32.4 6.1 %collective-permute-done.4 = bf16[32,3072]{1,0:T(8,128)(2,1)S(1)} collective-permute-done((bf16[32,3072]{1,0:T(8,128)(2,1)S(1)}, bf16[32,3072]{1,0:T(8,128)(2,1)S(1)}, u32[]{:S(2)}, u32[]{:S(2)}) %collective-permute-start.4) | collective-permute-done | bytes 196640 | tf_op jit(solution)/shard_map/ppermute | solution.py:134
  42.3 8.0 %collective-permute-done.7.refs_2_ = bf16[32,3072]{1,0:T(8,128)(2,1)S(1)} collective-permute-done((bf16[32,3072]{1,0:T(8,128)(2,1)S(1)}, bf16[32,3072]{1,0:T(8,128)(2,1)S(1)}, u32[]{:S(2)}, u32[]{:S(2)}) %collective-permute-start.7) | collective-permute-done | bytes 196640 | tf_op jit(solution)/shard_map/ppermute | solution.py:134
  51.2 5.1 %collective-permute-done.8.refs_3_ = bf16[32,3072]{1,0:T(8,128)(2,1)S(1)} collective-permute-done((bf16[32,3072]{1,0:T(8,128)(2,1)S(1)}, bf16[32,3072]{1,0:T(8,128)(2,1)S(1)}, u32[]{:S(2)}, u32[]{:S(2)}) %collective-permute-start.8) | collective-permute-done | bytes 196640 | tf_op jit(solution)/shard_map/ppermute | solution.py:134
  57.0 8.0 %collective-permute-done.9 = bf16[32,3072]{1,0:T(8,128)(2,1)S(1)} collective-permute-done((bf16[32,3072]{1,0:T(8,128)(2,1)S(1)}, bf16[32,3072]{1,0:T(8,128)(2,1)S(1)}, u32[]{:S(2)}, u32[]{:S(2)}) %collective-permute-start.9) | collective-permute-done | bytes 196640 | tf_op jit(solution)/shard_map/ppermute | solution.py:134
  65.2 7.5 %collective-permute-done.10 = bf16[32,3072]{1,0:T(8,128)(2,1)S(1)} collective-permute-done((bf16[32,3072]{1,0:T(8,128)(2,1)S(1)}, bf16[32,3072]{1,0:T(8,128)(2,1)S(1)}, u32[]{:S(2)}, u32[]{:S(2)}) %collective-permute-start.10) | collective-permute-done | bytes 196640 | tf_op jit(solution)/shard_map/ppermute | solution.py:134
  73.2 7.1 %collective-permute-start.13 = (bf16[32,3072]{1,0:T(8,128)(2,1)S(1)}, bf16[32,3072]{1,0:T(8,128)(2,1)S(1)}, u32[]{:S(2)}, u32[]{:S(2)}) collective-permute-start(bf16[32,3072]{1,0:T(8,128)(2,1)S(1)} %fusion.1), channel_id=1, source_target_pairs={{0,5},{1,4},{2,7},{3,6},{4,9},{5,8},{6,11},{7,10},{8,13},{9,12},{1... | collective-permute-start | bytes 589832 | tf_op jit(solution)/shard_map/ppermute | solution.py:134
  82.9 3.2 %collective-permute-done.13.refs_1_ = bf16[32,3072]{1,0:T(8,128)(2,1)S(1)} collective-permute-done((bf16[32,3072]{1,0:T(8,128)(2,1)S(1)}, bf16[32,3072]{1,0:T(8,128)(2,1)S(1)}, u32[]{:S(2)}, u32[]{:S(2)}) %collective-permute-start.13) | collective-permute-done | bytes 196640 | tf_op jit(solution)/shard_map/ppermute | solution.py:134
  86.8 5.3 %collective-permute-done.15.refs_3_ = bf16[32,3072]{1,0:T(8,128)(2,1)S(1)} collective-permute-done((bf16[32,3072]{1,0:T(8,128)(2,1)S(1)}, bf16[32,3072]{1,0:T(8,128)(2,1)S(1)}, u32[]{:S(2)}, u32[]{:S(2)}) %collective-permute-start.15) | collective-permute-done | bytes 196640 | tf_op jit(solution)/shard_map/ppermute | solution.py:134
  92.1 3.2 %shard_map.85 = (bf16[32,3072]{1,0:T(8,128)(2,1)S(1)}, bf16[32,3072]{1,0:T(8,128)(2,1)S(1)}, bf16[32,3072]{1,0:T(8,128)(2,1)S(1)}, bf16[32,3072]{1,0:T(8,128)(2,...) custom-call(s32[2]{0:T(128)S(1)} %pad_add_fusion.3.info, ...), custom_call_target="tpu_custom_call", output_to_operand_aliasing={{4}: (8, {}), {5}: (9, {})} | custom-call | flops 1308622848 | bytes 9437184 | tf_op jit(solution)/shard_map/pallas_call | solution.py:105
  95.6 6.0 %collective-permute-done.16 = bf16[32,3072]{1,0:T(8,128)(2,1)S(1)} collective-permute-done((bf16[32,3072]{1,0:T(8,128)(2,1)S(1)}, bf16[32,3072]{1,0:T(8,128)(2,1)S(1)}, u32[]{:S(2)}, u32[]{:S(2)}) %collective-permute-start.16) | collective-permute-done | bytes 196640 | tf_op jit(solution)/shard_map/ppermute | solution.py:134
  103.5 7.8 %collective-permute-done.17 = bf16[32,3072]{1,0:T(8,128)(2,1)S(1)} collective-permute-done((bf16[32,3072]{1,0:T(8,128)(2,1)S(1)}, bf16[32,3072]{1,0:T(8,128)(2,1)S(1)}, u32[]{:S(2)}, u32[]{:S(2)}) %collective-permute-start.17) | collective-permute-done | bytes 196640 | tf_op jit(solution)/shard_map/ppermute | solution.py:134
  115.2 7.5 %collective-permute-done.20.refs_2_ = bf16[32,3072]{1,0:T(8,128)(2,1)S(1)} collective-permute-done((bf16[32,3072]{1,0:T(8,128)(2,1)S(1)}, bf16[32,3072]{1,0:T(8,128)(2,1)S(1)}, u32[]{:S(2)}, u32[]{:S(2)}) %collective-permute-start.20) | collective-permute-done | bytes 196640 | tf_op jit(solution)/shard_map/ppermute | solution.py:134
  125.5 5.0 %collective-permute-done.21.refs_3_ = bf16[32,3072]{1,0:T(8,128)(2,1)S(1)} collective-permute-done((bf16[32,3072]{1,0:T(8,128)(2,1)S(1)}, bf16[32,3072]{1,0:T(8,128)(2,1)S(1)}, u32[]{:S(2)}, u32[]{:S(2)}) %collective-permute-start.21) | collective-permute-done | bytes 196640 | tf_op jit(solution)/shard_map/ppermute | solution.py:134
  132.9 4.6 %collective-permute-done.22 = bf16[32,3072]{1,0:T(8,128)(2,1)S(1)} collective-permute-done((bf16[32,3072]{1,0:T(8,128)(2,1)S(1)}, bf16[32,3072]{1,0:T(8,128)(2,1)S(1)}, u32[]{:S(2)}, u32[]{:S(2)}) %collective-permute-start.22) | collective-permute-done | bytes 196640 | tf_op jit(solution)/shard_map/ppermute | solution.py:134
  139.1 7.9 %collective-permute-done.23 = bf16[32,3072]{1,0:T(8,128)(2,1)S(1)} collective-permute-done((bf16[32,3072]{1,0:T(8,128)(2,1)S(1)}, bf16[32,3072]{1,0:T(8,128)(2,1)S(1)}, u32[]{:S(2)}, u32[]{:S(2)}) %collective-permute-start.23) | collective-permute-done | bytes 196640 | tf_op jit(solution)/shard_map/ppermute | solution.py:134
  147.8 8.6 %collective-permute-start.26 = (bf16[32,3072]{1,0:T(8,128)(2,1)S(1)}, bf16[32,3072]{1,0:T(8,128)(2,1)S(1)}, u32[]{:S(2)}, u32[]{:S(2)}) collective-permute-start(bf16[32,3072]{1,0:T(8,128)(2,1)S(1)} %fusion.3), channel_id=1, source_target_pairs={{0,5},{1,4},{2,7},{3,6},{4,9},{5,8},{6,11},{7,10},{8,13},{9,12},{1... | collective-permute-start | bytes 589832 | tf_op jit(solution)/shard_map/ppermute | solution.py:134
  158.2 3.4 %collective-permute-start.28 = (bf16[32,3072]{1,0:T(8,128)(2,1)S(1)}, bf16[32,3072]{1,0:T(8,128)(2,1)S(1)}, u32[]{:S(2)}, u32[]{:S(2)}) collective-permute-start(bf16[32,3072]{1,0:T(8,128)(2,1)S(1)} %collective-permute-done.27.refs_2_), channel_id=1, source_target_pairs={{0,1},{1,0},{2,3},{3,2},{4,5},{5,4},{6,7},{7,6},{8,9},{9,8},{10,11... | collective-permute-start | bytes 589832 | tf_op jit(solution)/shard_map/ppermute | solution.py:134
  162.5 7.8 %collective-permute-done.28.refs_3_ = bf16[32,3072]{1,0:T(8,128)(2,1)S(1)} collective-permute-done((bf16[32,3072]{1,0:T(8,128)(2,1)S(1)}, bf16[32,3072]{1,0:T(8,128)(2,1)S(1)}, u32[]{:S(2)}, u32[]{:S(2)}) %collective-permute-start.28) | collective-permute-done | bytes 196640 | tf_op jit(solution)/shard_map/ppermute | solution.py:134
  170.2 3.4 %shard_map.87 = (bf16[32,3072]{1,0:T(8,128)(2,1)S(1)}, bf16[32,3072]{1,0:T(8,128)(2,1)S(1)}, bf16[32,3072]{1,0:T(8,128)(2,1)S(1)}, bf16[32,3072]{1,0:T(8,128)(2,...) custom-call(s32[2]{0:T(128)S(1)} %pad_add_fusion.5.info, ...), custom_call_target="tpu_custom_call", output_to_operand_aliasing={{4}: (8, {}), {5}: (9, {})} | custom-call | flops 1308622848 | bytes 9437184 | tf_op jit(solution)/shard_map/pallas_call | solution.py:105
  173.7 5.7 %collective-permute-done.29 = bf16[32,3072]{1,0:T(8,128)(2,1)S(1)} collective-permute-done((bf16[32,3072]{1,0:T(8,128)(2,1)S(1)}, bf16[32,3072]{1,0:T(8,128)(2,1)S(1)}, u32[]{:S(2)}, u32[]{:S(2)}) %collective-permute-start.29) | collective-permute-done | bytes 196640 | tf_op jit(solution)/shard_map/ppermute | solution.py:134
  182.2 6.3 %collective-permute-done.30 = bf16[32,3072]{1,0:T(8,128)(2,1)S(1)} collective-permute-done((bf16[32,3072]{1,0:T(8,128)(2,1)S(1)}, bf16[32,3072]{1,0:T(8,128)(2,1)S(1)}, u32[]{:S(2)}, u32[]{:S(2)}) %collective-permute-start.30) | collective-permute-done | bytes 196640 | tf_op jit(solution)/shard_map/ppermute | solution.py:134
  193.3 7.0 %collective-permute-done.33.refs_2_ = bf16[32,3072]{1,0:T(8,128)(2,1)S(1)} collective-permute-done((bf16[32,3072]{1,0:T(8,128)(2,1)S(1)}, bf16[32,3072]{1,0:T(8,128)(2,1)S(1)}, u32[]{:S(2)}, u32[]{:S(2)}) %collective-permute-start.33) | collective-permute-done | bytes 196640 | tf_op jit(solution)/shard_map/ppermute | solution.py:134
  202.7 4.4 %collective-permute-done.34.refs_3_ = bf16[32,3072]{1,0:T(8,128)(2,1)S(1)} collective-permute-done((bf16[32,3072]{1,0:T(8,128)(2,1)S(1)}, bf16[32,3072]{1,0:T(8,128)(2,1)S(1)}, u32[]{:S(2)}, u32[]{:S(2)}) %collective-permute-start.34) | collective-permute-done | bytes 196640 | tf_op jit(solution)/shard_map/ppermute | solution.py:134
  209.5 3.9 %collective-permute-done.35 = bf16[32,3072]{1,0:T(8,128)(2,1)S(1)} collective-permute-done((bf16[32,3072]{1,0:T(8,128)(2,1)S(1)}, bf16[32,3072]{1,0:T(8,128)(2,1)S(1)}, u32[]{:S(2)}, u32[]{:S(2)}) %collective-permute-start.35) | collective-permute-done | bytes 196640 | tf_op jit(solution)/shard_map/ppermute | solution.py:134
  213.5 3.6 %collective-permute-start.36 = (bf16[32,3072]{1,0:T(8,128)(2,1)S(1)}, bf16[32,3072]{1,0:T(8,128)(2,1)S(1)}, u32[]{:S(2)}, u32[]{:S(2)}) collective-permute-start(bf16[32,3072]{1,0:T(8,128)(2,1)S(1)} %add_convert_fusion.1), channel_id=1, source_target_pairs={{0,3},{1,2},{2,1},{3,0},{4,7},{5,6},{6,5},{7,4},{8,11},{9,10},{10,... | collective-permute-start | bytes 589832 | tf_op jit(solution)/shard_map/ppermute | solution.py:134
  217.6 5.3 %collective-permute-done.36 = bf16[32,3072]{1,0:T(8,128)(2,1)S(1)} collective-permute-done((bf16[32,3072]{1,0:T(8,128)(2,1)S(1)}, bf16[32,3072]{1,0:T(8,128)(2,1)S(1)}, u32[]{:S(2)}, u32[]{:S(2)}) %collective-permute-start.36) | collective-permute-done | bytes 196640 | tf_op jit(solution)/shard_map/ppermute | solution.py:134
  225.2 6.0 %collective-permute-done.38 = bf16[32,3072]{1,0:T(8,128)(2,1)S(1)} collective-permute-done((bf16[32,3072]{1,0:T(8,128)(2,1)S(1)}, bf16[32,3072]{1,0:T(8,128)(2,1)S(1)}, u32[]{:S(2)}, u32[]{:S(2)}) %collective-permute-start.38) | collective-permute-done | bytes 196640 | tf_op jit(solution)/shard_map/ppermute | solution.py:134
  (81 shorter events, 47.6 us)
Async XLA Ops:
  0.0 11.1 %collective-permute-start.1 = (bf16[32,3072]{1,0:T(8,128)(2,1)}, bf16[32,3072]{1,0:T(8,128)(2,1)S(1)}, u32[]{:S(2)}, u32[]{:S(2)}) collective-permute-start(bf16[32,3072]{1,0:T(8,128)(2,1)} %bitcast.11), channel_id=1, source_target_pairs={{0,3},{1,2},{2,1},{3,0},{4,7},{5,6},{6,5},{7,4},{8,11},{9,10},{10,... | collective-permute-start | bytes 589832 | tf_op jit(solution)/shard_map/ppermute | solution.py:134
  5.1 15.8 %collective-permute-start = (bf16[32,3072]{1,0:T(8,128)(2,1)}, bf16[32,3072]{1,0:T(8,128)(2,1)S(1)}, u32[]{:S(2)}, u32[]{:S(2)}) collective-permute-start(bf16[32,3072]{1,0:T(8,128)(2,1)} %bitcast.12), channel_id=1, source_target_pairs={{0,1},{1,0},{2,3},{3,2},{4,5},{5,4},{6,7},{7,6},{8,9},{9,8},{10,11... | collective-permute-start | bytes 589832 | tf_op jit(solution)/shard_map/ppermute | solution.py:134
  11.1 9.7 %collective-permute-start.2 = (bf16[32,3072]{1,0:T(8,128)(2,1)S(1)}, bf16[32,3072]{1,0:T(8,128)(2,1)S(1)}, u32[]{:S(2)}, u32[]{:S(2)}) collective-permute-start(bf16[32,3072]{1,0:T(8,128)(2,1)S(1)} %collective-permute-done.1.refs_2_), channel_id=1, source_target_pairs={{0,1},{1,0},{2,3},{3,2},{4,5},{5,4},{6,7},{7,6},{8,9},{9,8},{10,11... | collective-permute-start | bytes 589832 | tf_op jit(solution)/shard_map/ppermute | solution.py:134
  29.8 8.6 %collective-permute-start.4 = (bf16[32,3072]{1,0:T(8,128)(2,1)S(1)}, bf16[32,3072]{1,0:T(8,128)(2,1)S(1)}, u32[]{:S(2)}, u32[]{:S(2)}) collective-permute-start(bf16[32,3072]{1,0:T(8,128)(2,1)S(1)} %add_convert_fusion.11), channel_id=1, source_target_pairs={{0,3},{1,2},{2,1},{3,0},{4,7},{5,6},{6,5},{7,4},{8,11},{9,10},{10,... | collective-permute-start | bytes 589832 | tf_op jit(solution)/shard_map/ppermute | solution.py:134
  32.4 8.1 %collective-permute-start.5 = (bf16[32,3072]{1,0:T(8,128)(2,1)S(1)}, bf16[32,3072]{1,0:T(8,128)(2,1)S(1)}, u32[]{:S(2)}, u32[]{:S(2)}) collective-permute-start(bf16[32,3072]{1,0:T(8,128)(2,1)S(1)} %get-tuple-element.66), channel_id=1, source_target_pairs={{0,1},{1,0},{2,3},{3,2},{4,5},{5,4},{6,7},{7,6},{8,9},{9,8},{10,11... | collective-permute-start | bytes 589832 | tf_op jit(solution)/shard_map/ppermute | solution.py:134
  40.6 9.7 %collective-permute-start.7 = (bf16[32,3072]{1,0:T(8,128)(2,1)S(1)}, bf16[32,3072]{1,0:T(8,128)(2,1)S(1)}, u32[]{:S(2)}, u32[]{:S(2)}) collective-permute-start(bf16[32,3072]{1,0:T(8,128)(2,1)S(1)} %fusion.refs_0_), channel_id=1, source_target_pairs={{0,3},{1,2},{2,1},{3,0},{4,7},{5,6},{6,5},{7,4},{8,11},{9,10},{10,... | collective-permute-start | bytes 589832 | tf_op jit(solution)/shard_map/ppermute | solution.py:134
  42.3 9.0 %collective-permute-start.6 = (bf16[32,3072]{1,0:T(8,128)(2,1)S(1)}, bf16[32,3072]{1,0:T(8,128)(2,1)S(1)}, u32[]{:S(2)}, u32[]{:S(2)}) collective-permute-start(bf16[32,3072]{1,0:T(8,128)(2,1)S(1)} %fusion.refs_0_), channel_id=1, source_target_pairs={{0,1},{1,0},{2,3},{3,2},{4,5},{5,4},{6,7},{7,6},{8,9},{9,8},{10,11... | collective-permute-start | bytes 589832 | tf_op jit(solution)/shard_map/ppermute | solution.py:134
  56.9 8.1 %collective-permute-start.9 = (bf16[32,3072]{1,0:T(8,128)(2,1)S(1)}, bf16[32,3072]{1,0:T(8,128)(2,1)S(1)}, u32[]{:S(2)}, u32[]{:S(2)}) collective-permute-start(bf16[32,3072]{1,0:T(8,128)(2,1)S(1)} %get-tuple-element.72), channel_id=1, source_target_pairs={{0,1},{1,0},{2,3},{3,2},{4,5},{5,4},{6,7},{7,6},{8,9},{9,8},{10,11... | collective-permute-start | bytes 589832 | tf_op jit(solution)/shard_map/ppermute | solution.py:134
  65.1 7.6 %collective-permute-start.10 = (bf16[32,3072]{1,0:T(8,128)(2,1)S(1)}, bf16[32,3072]{1,0:T(8,128)(2,1)S(1)}, u32[]{:S(2)}, u32[]{:S(2)}) collective-permute-start(bf16[32,3072]{1,0:T(8,128)(2,1)S(1)} %add_convert_fusion.9), channel_id=1, source_target_pairs={{0,3},{1,2},{2,1},{3,0},{4,7},{5,6},{6,5},{7,4},{8,11},{9,10},{10,... | collective-permute-start | bytes 589832 | tf_op jit(solution)/shard_map/ppermute | solution.py:134
  65.2 7.8 %collective-permute-start.11 = (bf16[32,3072]{1,0:T(8,128)(2,1)S(1)}, bf16[32,3072]{1,0:T(8,128)(2,1)S(1)}, u32[]{:S(2)}, u32[]{:S(2)}) collective-permute-start(bf16[32,3072]{1,0:T(8,128)(2,1)S(1)} %get-tuple-element.74), channel_id=1, source_target_pairs={{0,1},{1,0},{2,3},{3,2},{4,5},{5,4},{6,7},{7,6},{8,9},{9,8},{10,11... | collective-permute-start | bytes 589832 | tf_op jit(solution)/shard_map/ppermute | solution.py:134
  73.1 9.2 %collective-permute-start.14 = (bf16[32,3072]{1,0:T(8,128)(2,1)S(1)}, bf16[32,3072]{1,0:T(8,128)(2,1)S(1)}, u32[]{:S(2)}, u32[]{:S(2)}) collective-permute-start(bf16[32,3072]{1,0:T(8,128)(2,1)S(1)} %fusion.1), channel_id=1, source_target_pairs={{0,7},{1,6},{2,5},{3,4},{4,11},{5,10},{6,9},{7,8},{8,15},{9,14},{1... | collective-permute-start | bytes 589832 | tf_op jit(solution)/shard_map/ppermute | solution.py:134
  73.2 12.9 %collective-permute-start.13 = (bf16[32,3072]{1,0:T(8,128)(2,1)S(1)}, bf16[32,3072]{1,0:T(8,128)(2,1)S(1)}, u32[]{:S(2)}, u32[]{:S(2)}) collective-permute-start(bf16[32,3072]{1,0:T(8,128)(2,1)S(1)} %fusion.1), channel_id=1, source_target_pairs={{0,5},{1,4},{2,7},{3,6},{4,9},{5,8},{6,11},{7,10},{8,13},{9,12},{1... | collective-permute-start | bytes 589832 | tf_op jit(solution)/shard_map/ppermute | solution.py:134
  80.3 6.6 %collective-permute-start.12 = (bf16[32,3072]{1,0:T(8,128)(2,1)S(1)}, bf16[32,3072]{1,0:T(8,128)(2,1)S(1)}, u32[]{:S(2)}, u32[]{:S(2)}) collective-permute-start(bf16[32,3072]{1,0:T(8,128)(2,1)S(1)} %fusion.1), channel_id=1, source_target_pairs={{0,4},{1,5},{2,6},{3,7},{4,8},{5,9},{6,10},{7,11},{8,12},{9,13},{1... | collective-permute-start | bytes 589832 | tf_op jit(solution)/shard_map/ppermute | solution.py:134
  82.3 9.8 %collective-permute-start.15 = (bf16[32,3072]{1,0:T(8,128)(2,1)S(1)}, bf16[32,3072]{1,0:T(8,128)(2,1)S(1)}, u32[]{:S(2)}, u32[]{:S(2)}) collective-permute-start(bf16[32,3072]{1,0:T(8,128)(2,1)S(1)} %collective-permute-done.14.refs_2_), channel_id=1, source_target_pairs={{0,1},{1,0},{2,3},{3,2},{4,5},{5,4},{6,7},{7,6},{8,9},{9,8},{10,11... | collective-permute-start | bytes 589832 | tf_op jit(solution)/shard_map/ppermute | solution.py:134
  101.6 9.7 %collective-permute-start.17 = (bf16[32,3072]{1,0:T(8,128)(2,1)S(1)}, bf16[32,3072]{1,0:T(8,128)(2,1)S(1)}, u32[]{:S(2)}, u32[]{:S(2)}) collective-permute-start(bf16[32,3072]{1,0:T(8,128)(2,1)S(1)} %add_convert_fusion.7), channel_id=1, source_target_pairs={{0,3},{1,2},{2,1},{3,0},{4,7},{5,6},{6,5},{7,4},{8,11},{9,10},{10,... | collective-permute-start | bytes 589832 | tf_op jit(solution)/shard_map/ppermute | solution.py:134
  102.5 10.3 %collective-permute-start.18 = (bf16[32,3072]{1,0:T(8,128)(2,1)S(1)}, bf16[32,3072]{1,0:T(8,128)(2,1)S(1)}, u32[]{:S(2)}, u32[]{:S(2)}) collective-permute-start(bf16[32,3072]{1,0:T(8,128)(2,1)S(1)} %get-tuple-element.82), channel_id=1, source_target_pairs={{0,1},{1,0},{2,3},{3,2},{4,5},{5,4},{6,7},{7,6},{8,9},{9,8},{10,11... | collective-permute-start | bytes 589832 | tf_op jit(solution)/shard_map/ppermute | solution.py:134
  113.0 9.7 %collective-permute-start.20 = (bf16[32,3072]{1,0:T(8,128)(2,1)S(1)}, bf16[32,3072]{1,0:T(8,128)(2,1)S(1)}, u32[]{:S(2)}, u32[]{:S(2)}) collective-permute-start(bf16[32,3072]{1,0:T(8,128)(2,1)S(1)} %fusion.2.refs_0_), channel_id=1, source_target_pairs={{0,3},{1,2},{2,1},{3,0},{4,7},{5,6},{6,5},{7,4},{8,11},{9,10},{10,... | collective-permute-start | bytes 589832 | tf_op jit(solution)/shard_map/ppermute | solution.py:134
  114.4 11.1 %collective-permute-start.19 = (bf16[32,3072]{1,0:T(8,128)(2,1)S(1)}, bf16[32,3072]{1,0:T(8,128)(2,1)S(1)}, u32[]{:S(2)}, u32[]{:S(2)}) collective-permute-start(bf16[32,3072]{1,0:T(8,128)(2,1)S(1)} %fusion.2.refs_0_), channel_id=1, source_target_pairs={{0,1},{1,0},{2,3},{3,2},{4,5},{5,4},{6,7},{7,6},{8,9},{9,8},{10,11... | collective-permute-start | bytes 589832 | tf_op jit(solution)/shard_map/ppermute | solution.py:134
  122.7 7.8 %collective-permute-start.21 = (bf16[32,3072]{1,0:T(8,128)(2,1)S(1)}, bf16[32,3072]{1,0:T(8,128)(2,1)S(1)}, u32[]{:S(2)}, u32[]{:S(2)}) collective-permute-start(bf16[32,3072]{1,0:T(8,128)(2,1)S(1)} %collective-permute-done.20.refs_2_), channel_id=1, source_target_pairs={{0,1},{1,0},{2,3},{3,2},{4,5},{5,4},{6,7},{7,6},{8,9},{9,8},{10,11... | collective-permute-start | bytes 589832 | tf_op jit(solution)/shard_map/ppermute | solution.py:134
  131.1 6.4 %collective-permute-start.22 = (bf16[32,3072]{1,0:T(8,128)(2,1)S(1)}, bf16[32,3072]{1,0:T(8,128)(2,1)S(1)}, u32[]{:S(2)}, u32[]{:S(2)}) collective-permute-start(bf16[32,3072]{1,0:T(8,128)(2,1)S(1)} %get-tuple-element.88), channel_id=1, source_target_pairs={{0,1},{1,0},{2,3},{3,2},{4,5},{5,4},{6,7},{7,6},{8,9},{9,8},{10,11... | collective-permute-start | bytes 589832 | tf_op jit(solution)/shard_map/ppermute | solution.py:134
  137.5 9.4 %collective-permute-start.23 = (bf16[32,3072]{1,0:T(8,128)(2,1)S(1)}, bf16[32,3072]{1,0:T(8,128)(2,1)S(1)}, u32[]{:S(2)}, u32[]{:S(2)}) collective-permute-start(bf16[32,3072]{1,0:T(8,128)(2,1)S(1)} %add_convert_fusion.5), channel_id=1, source_target_pairs={{0,3},{1,2},{2,1},{3,0},{4,7},{5,6},{6,5},{7,4},{8,11},{9,10},{10,... | collective-permute-start | bytes 589832 | tf_op jit(solution)/shard_map/ppermute | solution.py:134
  138.2 9.0 %collective-permute-start.24 = (bf16[32,3072]{1,0:T(8,128)(2,1)S(1)}, bf16[32,3072]{1,0:T(8,128)(2,1)S(1)}, u32[]{:S(2)}, u32[]{:S(2)}) collective-permute-start(bf16[32,3072]{1,0:T(8,128)(2,1)S(1)} %get-tuple-element.90), channel_id=1, source_target_pairs={{0,1},{1,0},{2,3},{3,2},{4,5},{5,4},{6,7},{7,6},{8,9},{9,8},{10,11... | collective-permute-start | bytes 589832 | tf_op jit(solution)/shard_map/ppermute | solution.py:134
  147.3 10.9 %collective-permute-start.27 = (bf16[32,3072]{1,0:T(8,128)(2,1)S(1)}, bf16[32,3072]{1,0:T(8,128)(2,1)S(1)}, u32[]{:S(2)}, u32[]{:S(2)}) collective-permute-start(bf16[32,3072]{1,0:T(8,128)(2,1)S(1)} %fusion.3), channel_id=1, source_target_pairs={{0,7},{1,6},{2,5},{3,4},{4,11},{5,10},{6,9},{7,8},{8,15},{9,14},{1... | collective-permute-start | bytes 589832 | tf_op jit(solution)/shard_map/ppermute | solution.py:134
  147.8 14.5 %collective-permute-start.26 = (bf16[32,3072]{1,0:T(8,128)(2,1)S(1)}, bf16[32,3072]{1,0:T(8,128)(2,1)S(1)}, u32[]{:S(2)}, u32[]{:S(2)}) collective-permute-start(bf16[32,3072]{1,0:T(8,128)(2,1)S(1)} %fusion.3), channel_id=1, source_target_pairs={{0,5},{1,4},{2,7},{3,6},{4,9},{5,8},{6,11},{7,10},{8,13},{9,12},{1... | collective-permute-start | bytes 589832 | tf_op jit(solution)/shard_map/ppermute | solution.py:134
  158.2 12.0 %collective-permute-start.28 = (bf16[32,3072]{1,0:T(8,128)(2,1)S(1)}, bf16[32,3072]{1,0:T(8,128)(2,1)S(1)}, u32[]{:S(2)}, u32[]{:S(2)}) collective-permute-start(bf16[32,3072]{1,0:T(8,128)(2,1)S(1)} %collective-permute-done.27.refs_2_), channel_id=1, source_target_pairs={{0,1},{1,0},{2,3},{3,2},{4,5},{5,4},{6,7},{7,6},{8,9},{9,8},{10,11... | collective-permute-start | bytes 589832 | tf_op jit(solution)/shard_map/ppermute | solution.py:134
  179.4 9.1 %collective-permute-start.30 = (bf16[32,3072]{1,0:T(8,128)(2,1)S(1)}, bf16[32,3072]{1,0:T(8,128)(2,1)S(1)}, u32[]{:S(2)}, u32[]{:S(2)}) collective-permute-start(bf16[32,3072]{1,0:T(8,128)(2,1)S(1)} %add_convert_fusion.3), channel_id=1, source_target_pairs={{0,3},{1,2},{2,1},{3,0},{4,7},{5,6},{6,5},{7,4},{8,11},{9,10},{10,... | collective-permute-start | bytes 589832 | tf_op jit(solution)/shard_map/ppermute | solution.py:134
  181.6 8.9 %collective-permute-start.31 = (bf16[32,3072]{1,0:T(8,128)(2,1)S(1)}, bf16[32,3072]{1,0:T(8,128)(2,1)S(1)}, u32[]{:S(2)}, u32[]{:S(2)}) collective-permute-start(bf16[32,3072]{1,0:T(8,128)(2,1)S(1)} %get-tuple-element.98), channel_id=1, source_target_pairs={{0,1},{1,0},{2,3},{3,2},{4,5},{5,4},{6,7},{7,6},{8,9},{9,8},{10,11... | collective-permute-start | bytes 589832 | tf_op jit(solution)/shard_map/ppermute | solution.py:134
  190.6 9.7 %collective-permute-start.33 = (bf16[32,3072]{1,0:T(8,128)(2,1)S(1)}, bf16[32,3072]{1,0:T(8,128)(2,1)S(1)}, u32[]{:S(2)}, u32[]{:S(2)}) collective-permute-start(bf16[32,3072]{1,0:T(8,128)(2,1)S(1)} %fusion.4.refs_0_), channel_id=1, source_target_pairs={{0,3},{1,2},{2,1},{3,0},{4,7},{5,6},{6,5},{7,4},{8,11},{9,10},{10,... | collective-permute-start | bytes 589832 | tf_op jit(solution)/shard_map/ppermute | solution.py:134
  192.6 10.1 %collective-permute-start.32 = (bf16[32,3072]{1,0:T(8,128)(2,1)S(1)}, bf16[32,3072]{1,0:T(8,128)(2,1)S(1)}, u32[]{:S(2)}, u32[]{:S(2)}) collective-permute-start(bf16[32,3072]{1,0:T(8,128)(2,1)S(1)} %fusion.4.refs_0_), channel_id=1, source_target_pairs={{0,1},{1,0},{2,3},{3,2},{4,5},{5,4},{6,7},{7,6},{8,9},{9,8},{10,11... | collective-permute-start | bytes 589832 | tf_op jit(solution)/shard_map/ppermute | solution.py:134
  200.3 6.8 %collective-permute-start.34 = (bf16[32,3072]{1,0:T(8,128)(2,1)S(1)}, bf16[32,3072]{1,0:T(8,128)(2,1)S(1)}, u32[]{:S(2)}, u32[]{:S(2)}) collective-permute-start(bf16[32,3072]{1,0:T(8,128)(2,1)S(1)} %collective-permute-done.33.refs_2_), channel_id=1, source_target_pairs={{0,1},{1,0},{2,3},{3,2},{4,5},{5,4},{6,7},{7,6},{8,9},{9,8},{10,11... | collective-permute-start | bytes 589832 | tf_op jit(solution)/shard_map/ppermute | solution.py:134
  213.5 9.4 %collective-permute-start.36 = (bf16[32,3072]{1,0:T(8,128)(2,1)S(1)}, bf16[32,3072]{1,0:T(8,128)(2,1)S(1)}, u32[]{:S(2)}, u32[]{:S(2)}) collective-permute-start(bf16[32,3072]{1,0:T(8,128)(2,1)S(1)} %add_convert_fusion.1), channel_id=1, source_target_pairs={{0,3},{1,2},{2,1},{3,0},{4,7},{5,6},{6,5},{7,4},{8,11},{9,10},{10,... | collective-permute-start | bytes 589832 | tf_op jit(solution)/shard_map/ppermute | solution.py:134
  217.1 8.0 %collective-permute-start.37 = (bf16[32,3072]{1,0:T(8,128)(2,1)S(1)}, bf16[32,3072]{1,0:T(8,128)(2,1)S(1)}, u32[]{:S(2)}, u32[]{:S(2)}) collective-permute-start(bf16[32,3072]{1,0:T(8,128)(2,1)S(1)} %get-tuple-element.106), channel_id=1, source_target_pairs={{0,1},{1,0},{2,3},{3,2},{4,5},{5,4},{6,7},{7,6},{8,9},{9,8},{10,11... | collective-permute-start | bytes 589832 | tf_op jit(solution)/shard_map/ppermute | solution.py:134
  (8 other events, 62.4 us)
